TPU v7x, 32 devices: a whole 2x2x4 slice. The times are simulated.
32 devices in a mesh: dp: 8 (over z, y), mp: 4 (over x, core).
Axes of the slice: x: 2, y: 2, z: 4, core: 2. Of those that a mesh axis runs over, the one named last changes fastest.
Arguments:
- tokens: bfloat16 [8192, 768], P('dp'), may hold values from -12 to 12
- w_qkv: bfloat16 [3, 768, 768], P(None, 'dp', 'mp'), may hold values from -0.21875 to 0.21875
- w_out: bfloat16 [768, 768], P('mp', 'dp'), may hold values from -1.5 to 1.5
- w_up: bfloat16 [768, 3072], P('dp', 'mp'), may hold values from -0.21875 to 0.21875
- w_down: bfloat16 [3072, 768], P('mp', 'dp'), may hold values from -0.109375 to 0.109375
- b_qv: bfloat16 [2, 12, 64], P(None, 'mp', 'dp'), may hold values from -3 to 3
- b_up: bfloat16 [12, 256], P('mp', 'dp'), may hold values from -3 to 3
- vectors: bfloat16 [6, 768], P(None, 'dp'), may hold values from -1.2 to 1.4, as said below
- ema_ranges: float32 [4], replicated, may hold values from 1 to 4
- key_mask: int32 [8192], P('dp'), may hold values from 0 to 1, as said below
- long_rows: int32 [16], P('dp'), may hold values 0 or 1
- grad_out: bfloat16 [8192, 768], P(('dp', 'mp')), may hold values from -6 to 6
Outputs:
- layer_out: bfloat16 [8192, 768], P(('dp', 'mp'))
- grad_tokens: float32 [8192, 768], P('dp')
- grad_qkv: float32 [3, 768, 768], P(None, 'dp', 'mp')
- grad_wout: float32 [768, 768], P('mp', 'dp')
- grad_wup: float32 [768, 3072], P('dp', 'mp')
- grad_wdown: float32 [3072, 768], P('mp', 'dp')
- grad_bqv: float32 [2, 12, 64], P(None, 'mp', 'dp')
- grad_bup: float32 [12, 256], P('mp', 'dp')
- grad_vectors: float32 [6, 768], P(None, 'dp')
- new_ranges: float32 [4], replicated
Inputs may be any that keep to these rules, and one draw needn't show every extreme that they name: `key_mask`: the first of every 128 positions is 1. `vectors`: rows 2 and 4 lie near 1.
All inputs are finite; a program needn't handle non-finite values. No bound on the sum of `long_rows` on one device may be relied on, other than what follows from the above.
Results may differ from a plain program's by a relative error of at most 0.014.
Values may be sent and summed in bfloat16 or wider, within the bound.
A program may use at most 128 MiB of HBM per device.

v0:
```python
import jax
import jax.numpy as jnp
from jax import lax
from jax.sharding import PartitionSpec as P

HD = 64
BLOCK = 512
SEG = 128


eps_norm = 1e-12
root_half = 0.7071067811865476
inv_root_tau = 0.3989422804014327


def squash(values, limit):
    return limit * jnp.tanh(values / limit)


def slope(values, limit):
    bent = jnp.tanh(values / limit)
    return 1.0 - bent * bent


def peak_of(values):
    return jnp.max(jnp.abs(values.astype(jnp.float32)))


def product(left, right):
    return jnp.dot(left, right, preferred_element_type=jnp.float32)


def contract_rows(left, right):
    return lax.dot_general(
        left, right, (((0,), (0,)), ((), ())), preferred_element_type=jnp.float32
    )


def contract_cols(left, right):
    return lax.dot_general(
        left, right, (((1,), (1,)), ((), ())), preferred_element_type=jnp.float32
    )


def normalize(values):
    center = values - jnp.mean(values, axis=-1, keepdims=True)
    factor = lax.rsqrt(jnp.mean(center * center, axis=-1, keepdims=True) + eps_norm)
    return (center * factor, factor)


def norm_back(grad_normed, normed, factor):
    first_mean = jnp.mean(grad_normed, axis=-1, keepdims=True)
    cross_mean = jnp.mean(grad_normed * normed, axis=-1, keepdims=True)
    return factor * (grad_normed - first_mean - normed * cross_mean)


def allowed_keys(live, long_flag):
    places = jnp.arange(BLOCK) // SEG
    return (live[None, :] > 0) & ((long_flag > 0) | (places[:, None] == places[None, :]))


def block_scores(queries, keys_in, live, long_flag):
    scores = jnp.einsum("qhd,khd->hqk", queries, keys_in, preferred_element_type=jnp.float32)
    return jnp.where(allowed_keys(live, long_flag)[None], scores, -1e30)


def attend_block(pieces):
    queries, keys_in, values, live, long_flag = pieces
    scores = block_scores(queries, keys_in, live, long_flag)
    top_score = jnp.max(scores, axis=-1, keepdims=True)
    weights = jnp.exp(scores - top_score)
    totals = jnp.sum(weights, axis=-1, keepdims=True)
    attn_probs = (weights / totals).astype(jnp.bfloat16)
    context = jnp.einsum("hqk,khd->qhd", attn_probs, values, preferred_element_type=jnp.float32)
    return (context, top_score + jnp.log(totals))


def attend_back(pieces):
    queries, keys_in, values, live, long_flag, log_total, grad_ctx = pieces
    attn_probs = jnp.exp(block_scores(queries, keys_in, live, long_flag) - log_total)
    grad_probs = jnp.einsum("qhd,khd->hqk", grad_ctx, values, preferred_element_type=jnp.float32)
    grad_values = jnp.einsum(
        "hqk,qhd->khd",
        attn_probs.astype(jnp.bfloat16),
        grad_ctx,
        preferred_element_type=jnp.float32,
    )
    inner = jnp.sum(grad_probs * attn_probs, axis=-1, keepdims=True)
    grad_scores = (attn_probs * (grad_probs - inner)).astype(jnp.bfloat16)
    grad_queries = jnp.einsum(
        "hqk,khd->qhd", grad_scores, keys_in, preferred_element_type=jnp.float32
    )
    grad_keys = jnp.einsum("hqk,qhd->khd", grad_scores, queries, preferred_element_type=jnp.float32)
    return (
        grad_queries.astype(jnp.bfloat16),
        grad_keys.astype(jnp.bfloat16),
        grad_values.astype(jnp.bfloat16),
    )


def prepare(gathered, w_peaks):
    return tuple(
        (
            squash(gathered[index].astype(jnp.float32), w_peaks[index]).astype(jnp.bfloat16)
            for index in range(4)
        )
    )


def peak_all(values):
    return lax.pmax(peak_of(values), ("dp", "mp"))


def per_device(
    tokens,
    w_qkv,
    w_out,
    w_up,
    w_down,
    b_qv,
    b_up,
    vectors,
    ema_ranges,
    key_mask,
    long_rows,
    grad_out,
):
    row_count = tokens.shape[0]
    quarter = row_count // lax.axis_size("mp")
    row_start = lax.axis_index("mp") * quarter
    blocks = row_count // BLOCK
    w_peaks = lax.pmax(
        (peak_of(w_qkv), peak_of(w_out), peak_of(w_up), peak_of(w_down)), ("dp", "mp")
    )
    gathered = (
        lax.all_gather(w_qkv, "dp", axis=1, tiled=True),
        lax.all_gather(w_out, "dp", axis=1, tiled=True),
        lax.all_gather(w_up, "dp", axis=0, tiled=True),
        lax.all_gather(w_down, "dp", axis=1, tiled=True),
        lax.all_gather(b_qv, "dp", axis=2, tiled=True),
        lax.all_gather(b_up, "dp", axis=1, tiled=True),
        lax.all_gather(vectors, "dp", axis=1, tiled=True),
    )
    qkv_q, out_q, up_q, down_q = prepare(gathered, w_peaks)
    bias_qv = gathered[4].astype(jnp.float32).reshape(2, -1)
    bias_up = gathered[5].astype(jnp.float32).reshape(-1)
    vec = gathered[6].astype(jnp.float32)
    head_width = bias_qv.shape[1]
    heads_here = head_width // HD
    scale_q = HD ** (-0.5)
    tok_float = tokens.astype(jnp.float32)
    peak_tok = peak_all(tok_float)
    tok_quant = squash(tok_float, ema_ranges[0]).astype(jnp.bfloat16)
    projected = jnp.einsum("td,jde->jte", tok_quant, qkv_q, preferred_element_type=jnp.float32)
    queries = ((projected[0] + bias_qv[0]) * scale_q).astype(jnp.bfloat16)
    keys_all = projected[1].astype(jnp.bfloat16)
    values = (projected[2] + bias_qv[1]).astype(jnp.bfloat16)
    shape_four = (blocks, BLOCK, heads_here, HD)
    mask_blocks = key_mask.reshape(blocks, BLOCK)
    block_inputs = (
        queries.reshape(shape_four),
        keys_all.reshape(shape_four),
        values.reshape(shape_four),
        mask_blocks,
        long_rows,
    )
    context, log_total = lax.map(attend_block, block_inputs)
    context = context.reshape(row_count, head_width)
    peak_ctx = peak_all(context)
    ctx_quant = squash(context, ema_ranges[1]).astype(jnp.bfloat16)
    partial_attn = product(ctx_quant, out_q)
    attn = lax.psum_scatter(partial_attn, "mp", scatter_dimension=0, tiled=True) + vec[0]
    first_own = lax.dynamic_slice_in_dim(tok_float, row_start, quarter, 0) + attn
    normed, factor_one = normalize(first_own)
    hidden_in = normed * vec[2] + vec[3]
    hid_quant = lax.all_gather(
        squash(hidden_in, ema_ranges[2]).astype(jnp.bfloat16), "mp", axis=0, tiled=True
    )
    peak_hid = peak_all(hidden_in)
    pre_act = product(hid_quant, up_q) + bias_up
    active = pre_act * 0.5 * (1.0 + lax.erf(pre_act * root_half))
    peak_act = peak_all(active)
    act_quant = squash(active, ema_ranges[3]).astype(jnp.bfloat16)
    branch = (
        lax.psum_scatter(product(act_quant, down_q), "mp", scatter_dimension=0, tiled=True) + vec[1]
    )
    second = first_own + branch
    normed_two, factor_two = normalize(second)
    layer_out = (normed_two * vec[4] + vec[5]).astype(jnp.bfloat16)
    new_ranges = 0.9 * ema_ranges + 0.1 * jnp.stack([peak_tok, peak_ctx, peak_hid, peak_act])
    gathered = (
        lax.all_gather(w_qkv, "dp", axis=1, tiled=True),
        lax.all_gather(w_out, "dp", axis=1, tiled=True),
        lax.all_gather(w_up, "dp", axis=0, tiled=True),
        lax.all_gather(w_down, "dp", axis=1, tiled=True),
        lax.all_gather(b_qv, "dp", axis=2, tiled=True),
        lax.all_gather(b_up, "dp", axis=1, tiled=True),
        lax.all_gather(vectors, "dp", axis=1, tiled=True),
    )
    qkv_q, out_q, up_q, down_q = prepare(gathered, w_peaks)
    grad_y = grad_out.astype(jnp.float32)
    grad_gain_two = jnp.sum(grad_y * normed_two, axis=0)
    grad_shift_two = jnp.sum(grad_y, axis=0)
    grad_second = norm_back(grad_y * vec[4], normed_two, factor_two)
    grad_resid = lax.all_gather(grad_second.astype(jnp.bfloat16), "mp", axis=0, tiled=True).astype(
        grad_second.dtype
    )
    grad_branch = grad_resid.astype(jnp.bfloat16)
    grad_bias_down = jnp.sum(grad_branch.astype(jnp.float32), axis=0)
    grad_down_w = contract_rows(act_quant, grad_branch)
    grad_active = contract_cols(grad_branch, down_q) * slope(active, ema_ranges[3])
    normal_cdf = 0.5 * (1.0 + lax.erf(pre_act * root_half))
    normal_pdf = inv_root_tau * jnp.exp(-0.5 * pre_act * pre_act)
    grad_pre = (grad_active * (normal_cdf + pre_act * normal_pdf)).astype(jnp.bfloat16)
    grad_bias_up = jnp.sum(grad_pre.astype(jnp.float32), axis=0)
    grad_up_w = contract_rows(hid_quant, grad_pre)
    partial_hid = contract_cols(grad_pre, up_q)
    grad_hid_q = lax.psum_scatter(partial_hid, "mp", scatter_dimension=0, tiled=True)
    grad_hidden = grad_hid_q * slope(hidden_in, ema_ranges[2])
    grad_gain_one = jnp.sum(grad_hidden * normed, axis=0)
    grad_shift_one = jnp.sum(grad_hidden, axis=0)
    grad_first = norm_back(grad_hidden * vec[2], normed, factor_one) + grad_second
    grad_attn = lax.all_gather(grad_first.astype(jnp.bfloat16), "mp", axis=0, tiled=True)
    grad_bias_out = jnp.sum(grad_attn.astype(jnp.float32), axis=0)
    grad_out_w = contract_rows(ctx_quant, grad_attn)
    grad_ctx = (contract_cols(grad_attn, out_q) * slope(context, ema_ranges[1])).astype(
        jnp.bfloat16
    )
    back_inputs = block_inputs + (log_total, grad_ctx.reshape(shape_four))
    grad_q, grad_k, grad_v = lax.map(attend_back, back_inputs)
    stacked = jnp.stack(
        [
            grad_q.reshape(row_count, head_width) * jnp.bfloat16(scale_q),
            grad_k.reshape(row_count, head_width),
            grad_v.reshape(row_count, head_width),
        ]
    )
    grad_qkv_w = jnp.einsum("td,jte->jde", tok_quant, stacked, preferred_element_type=jnp.float32)
    stacked_float = stacked.astype(jnp.float32)
    grad_bias_qv = jnp.stack([jnp.sum(stacked_float[0], axis=0), jnp.sum(stacked_float[2], axis=0)])
    part_input = jnp.einsum("jte,jde->td", stacked, qkv_q, preferred_element_type=jnp.float32)
    own_term = part_input * slope(tok_float, ema_ranges[0])
    own_rows = lax.dynamic_slice_in_dim(own_term, row_start, quarter, 0) + grad_first
    own_term = lax.dynamic_update_slice_in_dim(own_term, own_rows, row_start, 0)
    grad_tokens, norm_tail = (
        lax.psum(own_term.astype(jnp.bfloat16), "mp").astype(jnp.float32),
        lax.psum(
            jnp.stack([grad_gain_one, grad_shift_one, grad_gain_two, grad_shift_two]).astype(
                jnp.bfloat16
            ),
            "mp",
        ).astype(jnp.float32),
    )
    grad_vec = jnp.stack(
        [grad_bias_out, grad_bias_down, norm_tail[0], norm_tail[1], norm_tail[2], norm_tail[3]]
    )
    summed = (
        lax.psum_scatter(
            grad_qkv_w * slope(gathered[0].astype(jnp.float32), w_peaks[0]),
            "dp",
            scatter_dimension=1,
            tiled=True,
        ),
        lax.psum_scatter(
            grad_out_w * slope(gathered[1].astype(jnp.float32), w_peaks[1]),
            "dp",
            scatter_dimension=1,
            tiled=True,
        ),
        lax.psum_scatter(
            grad_up_w * slope(gathered[2].astype(jnp.float32), w_peaks[2]),
            "dp",
            scatter_dimension=0,
            tiled=True,
        ),
        lax.psum_scatter(
            grad_down_w * slope(gathered[3].astype(jnp.float32), w_peaks[3]),
            "dp",
            scatter_dimension=1,
            tiled=True,
        ),
        lax.psum_scatter(
            grad_bias_qv.reshape(gathered[4].shape), "dp", scatter_dimension=2, tiled=True
        ),
        lax.psum_scatter(
            grad_bias_up.reshape(gathered[5].shape), "dp", scatter_dimension=1, tiled=True
        ),
        lax.psum_scatter(grad_vec, "dp", scatter_dimension=1, tiled=True),
    )
    return (
        layer_out,
        grad_tokens,
        summed[0],
        summed[1],
        summed[2],
        summed[3],
        summed[4],
        summed[5],
        summed[6],
        new_ranges,
    )


def solution(mesh):
    placed = (
        P("dp", None),
        P(None, "dp", "mp"),
        P("mp", "dp"),
        P("dp", "mp"),
        P("mp", "dp"),
        P(None, "mp", "dp"),
        P("mp", "dp"),
        P(None, "dp"),
        P(),
        P("dp"),
        P("dp"),
        P(("dp", "mp"), None),
    )
    return jax.shard_map(
        per_device,
        mesh=mesh,
        in_specs=placed,
        out_specs=(
            P(("dp", "mp"), None),
            P("dp", None),
            P(None, "dp", "mp"),
            P("mp", "dp"),
            P("dp", "mp"),
            P("mp", "dp"),
            P(None, "mp", "dp"),
            P("mp", "dp"),
            P(None, "dp"),
            P(),
        ),
        check_vma=False,
    )
```

profile of v0, /device:TPU:0, one launch (start us, length us, event | category | flops | bytes accessed | tf_op | source)
XLA Modules:
  0.0 840.6 jit_solution(4800025141592634390)
XLA Ops:
  17.7 38.6 %all_gather.34 = bf16[3,768,192]{2,0,1:T(4,128)(2,1)S(1)} all-gather(bf16[3,96,192]{2,0,1:T(4,128)(2,1)S(1)} %copy.94), channel_id=1, replica_groups=mesh['dp'=8,'mp'=4] {'dp'}, dimensions={1}, use_global_device_ids=true | all-gather | bytes 995328 | tf_op jit(solution)/shard_map/all_gather | solution.py:136
  58.3 38.5 %all-reduce.2 = (f32[]{:T(128)}, f32[]{:T(128)}, f32[]{:T(128)}, f32[]{:T(128)}) all-reduce(f32[]{:T(128)} %abs_reduce_fusion.6, f32[]{:T(128)} %abs_reduce_fusion.7, f32[]{:T(128)} %abs_reduce_fusion.5, f32[]{:T(128)} %abs_reduce_fusion.4), channel_id=1, replica_groups=mesh['dp'=8,'mp'=4] {'dp','mp'}, use_global_device_ids=true, to_apply=%region_1.0 | all-reduce | flops 4 | bytes 32 | tf_op jit(solution)/shard_map/pmax | solution.py:132
  101.6 30.4 %all_gather.35 = bf16[2,3,64]{1,0,2:T(2,128)(2,1)S(1)} all-gather(bf16[2,3,8]{1,0,2:T(2,128)(2,1)S(1)} %copy.96), channel_id=1, replica_groups=mesh['dp'=8,'mp'=4] {'dp'}, dimensions={2}, use_global_device_ids=true | all-gather | bytes 864 | tf_op jit(solution)/shard_map/all_gather | solution.py:140
  132.2 31.0 %all_gather.36 = bf16[192,768]{0,1:T(8,128)(2,1)S(1)} all-gather(bf16[192,96]{0,1:T(8,128)(2,1)S(1)} %copy.103), channel_id=1, replica_groups=mesh['dp'=8,'mp'=4] {'dp'}, dimensions={1}, use_global_device_ids=true | all-gather | bytes 331776 | tf_op jit(solution)/shard_map/all_gather | solution.py:137
  170.4 10.6 %while.30 = (s32[]{:T(128)}, f32[2,512,3,64]{1,3,2,0:T(8,128)}, f32[2,3,512,1]{2,1,3,0:T(4,128)}, bf16[2,512,3,64]{1,3,2,0:T(8,128)(2,1)S(1)}, s32[2,512]{1,0:T(...) while((s32[]{:T(128)}, f32[2,512,3,64]{1,3,2,0:T(8,128)}, ...), condition=%wide.region_5.0_spmd, body=%wide.region_2.5_spmd.sunk | while | flops 209193984 | bytes 17824964 | solution.py:167
  191.0 26.1 %all-gather = bf16[8,96,6]{1,2,0:T(8,128)(2,1)S(1)} all-gather(bf16[1,96,6]{1,2,0:T(8,128)(2,1)S(1)} %bitcast.209), channel_id=1, replica_groups=mesh['dp'=8,'mp'=4] {'dp'}, dimensions={0}, use_global_device_ids=true | all-gather | bytes 10368 | tf_op jit(solution)/shard_map/all_gather | solution.py:142
  217.2 8.7 %reduce-scatter.21.cloned.1.call-done = f32[256,768]{1,0:T(8,128)} async-done(((f32[1024,768]{1,0:T(8,128)}), f32[256,768]{1,0:T(8,128)}) %reduce-scatter.21.cloned.1.call-update) | async-done | bytes 786448 | tf_op jit(solution)/shard_map/reduce_scatter | solution.py:172
  229.5 20.7 %all-gather.1 = bf16[8,32,3]{1,2,0:T(4,128)(2,1)S(1)} all-gather(bf16[1,32,3]{1,2,0:T(4,128)(2,1)S(1)} %bitcast.210), channel_id=1, replica_groups=mesh['dp'=8,'mp'=4] {'dp'}, dimensions={0}, use_global_device_ids=true | all-gather | bytes 1728 | tf_op jit(solution)/shard_map/all_gather | solution.py:141
  251.8 22.2 %all-gather.10.cloned.1.call-done = bf16[768,768]{1,0:T(8,128)(2,1)} async-done(((bf16[96,768]{1,0:T(8,128)(2,1)}), bf16[768,768]{1,0:T(8,128)(2,1)}) %all-gather.10.cloned.1.call-update) | async-done | bytes 1179664 | tf_op jit(solution)/shard_map/all_gather | solution.py:138
  274.0 20.1 %all-gather.8.cloned.1.call-done = bf16[1024,768]{1,0:T(8,128)(2,1)} async-done(((bf16[256,768]{1,0:T(8,128)(2,1)}), bf16[1024,768]{1,0:T(8,128)(2,1)}) %all-gather.8.cloned.1.call-update) | async-done | bytes 1572880 | tf_op jit(solution)/shard_map/all_gather | solution.py:176
  294.1 7.0 abs_reduce_fusion
  306.3 38.0 %reduce-scatter.23.cloned.1.call-done = f32[256,768]{1,0:T(8,128)} async-done(((f32[1024,768]{1,0:T(8,128)}), f32[256,768]{1,0:T(8,128)}) %reduce-scatter.23.cloned.1.call-update) | async-done | bytes 786448 | tf_op jit(solution)/shard_map/reduce_scatter | solution.py:185
  347.4 19.6 %all-gather.14.cloned.1.call-done = bf16[1024,768]{1,0:T(8,128)(2,1)} async-done(((bf16[256,768]{1,0:T(8,128)(2,1)}), bf16[1024,768]{1,0:T(8,128)(2,1)}) %all-gather.14.cloned.1.call-update) | async-done | bytes 1572880 | tf_op jit(solution)/shard_map/all_gather | solution.py:205
  367.0 7.6 convert_reduce_fusion.2
  379.6 37.9 %reduce-scatter.25.cloned.1.call-done = f32[256,768]{1,0:T(8,128)} async-done(((f32[1024,768]{1,0:T(8,128)}), f32[256,768]{1,0:T(8,128)}) %reduce-scatter.25.cloned.1.call-update) | async-done | bytes 786448 | tf_op jit(solution)/shard_map/reduce_scatter | solution.py:218
  427.6 6.1 psum.15
  433.7 8.5 %all-gather.16.cloned.1.call-done = bf16[1024,768]{1,0:T(8,128)(2,1)} async-done(((bf16[256,768]{1,0:T(8,128)(2,1)}), bf16[1024,768]{1,0:T(8,128)(2,1)}) %all-gather.16.cloned.1.call-update) | async-done | bytes 1572880 | tf_op jit(solution)/shard_map/all_gather | solution.py:223
  447.5 14.8 %while.31 = (s32[]{:T(128)}, bf16[2,512,3,64]{1,3,2,0:T(8,128)(2,1)}, bf16[2,512,3,64]{1,3,2,0:T(8,128)(2,1)}, bf16[2,512,3,64]{1,3,2,0:T(8,128)(2,1)S(1)}, bf16...) while((s32[]{:T(128)}, ...), condition=%wide.region_25.26_spmd, body=%wide.region_23.25_spmd.sunk | while | flops 513838080 | bytes 32958740 | solution.py:230
  513.1 39.7 %all-reduce.1 = (f32[1]{0:T(128)}, f32[1]{0:T(128)}, f32[1]{0:T(128)}, f32[1]{0:T(128)}) all-reduce(f32[1]{0:T(128)} %bitcast.38, f32[1]{0:T(128)} %bitcast.37, f32[1]{0:T(128)} %bitcast.36, f32[1]{0:T(128)} %bitcast.35), channel_id=1, replica_groups=mesh['dp'=8,'mp'=4] {'dp','mp'}, use_global_device_ids=true, to_apply=%region_51.52 | all-reduce | flops 4 | bytes 32 | tf_op jit(solution)/shard_map/pmax | solution.py:111
  556.7 21.5 %all-reduce = f32[2,3,64]{2,1,0:T(4,128)S(1)} all-reduce(f32[2,3,64]{2,1,0:T(4,128)S(1)} %pad_maximum_fusion.2), channel_id=9, replica_groups=mesh['dp'=8,'mp'=4] {'dp'}, use_global_device_ids=true, to_apply=%region_33.34.clone | all-reduce | flops 384 | bytes 3072
  583.6 34.4 %reduce-scatter.31.cloned.1.call-done = f32[96,192]{1,0:T(8,128)} async-done(((f32[768,192]{1,0:T(8,128)}), f32[96,192]{1,0:T(8,128)}) %reduce-scatter.31.cloned.1.call-update) | async-done | bytes 73744
  619.6 67.8 %reduce-scatter.29.cloned.1.call-done = f32[96,576]{1,0:T(8,128)} async-done(((f32[768,576]{1,0:T(8,128)}), f32[96,576]{1,0:T(8,128)}) %reduce-scatter.29.cloned.1.call-update) | async-done | bytes 221200
  689.3 71.0 %reduce-scatter.33.cloned.1.call-done = f32[96,768]{1,0:T(8,128)} async-done(((f32[768,768]{1,0:T(8,128)}), f32[96,768]{1,0:T(8,128)}) %reduce-scatter.33.cloned.1.call-update) | async-done | bytes 294928
  760.4 72.4 %reduce-scatter.27.cloned.1.call-done = f32[96,768]{1,0:T(8,128)} async-done(((f32[768,768]{1,0:T(8,128)}), f32[96,768]{1,0:T(8,128)}) %reduce-scatter.27.cloned.1.call-update) | async-done | bytes 294928 | tf_op jit(solution)/shard_map/reduce_scatter | solution.py:270
  (275 shorter events, 152.4 us)
Async XLA Ops:
  8.0 217.9 %reduce-scatter.21.cloned.1.call-start = ((), (), s32[]{:S(2)}) async-start(), calls=%async_computation.9 | async-start | bytes 3932160 | tf_op jit(solution)/shard_map/reduce_scatter | solution.py:172
  12.0 84.8 %copy-start.1 = (bf16[1024,768]{1,0:T(8,128)(2,1)S(1)}, bf16[1024,768]{1,0:T(8,128)(2,1)}, u32[]{:S(2)}) copy-start(bf16[1024,768]{1,0:T(8,128)(2,1)} %param.16) | copy-start | bytes 4718596
  187.9 62.4 %all-gather.12.cloned.1.call-start = ((), (), s32[]{:S(2)}) async-start(), calls=%async_computation.12 | async-start | bytes 1327104 | tf_op jit(solution)/shard_map/all_gather | solution.py:139
  188.5 85.6 %all-gather.10.cloned.1.call-start = ((), (), s32[]{:S(2)}) async-start(), calls=%async_computation.11 | async-start | bytes 1327104 | tf_op jit(solution)/shard_map/all_gather | solution.py:138
  189.0 105.1 %all-gather.8.cloned.1.call-start = ((), (), s32[]{:S(2)}) async-start(), calls=%async_computation.10 | async-start | bytes 1966080 | tf_op jit(solution)/shard_map/all_gather | solution.py:176
  229.4 114.9 %reduce-scatter.23.cloned.1.call-start = ((), (), s32[]{:S(2)}) async-start(), calls=%async_computation.13 | async-start | bytes 3932160 | tf_op jit(solution)/shard_map/reduce_scatter | solution.py:185
  251.8 49.3 %copy-start.12 = (bf16[768,768]{1,0:T(8,128)(2,1)}, bf16[768,768]{1,0:T(8,128)(2,1)S(1)}, u32[]{:S(2)}) copy-start(bf16[768,768]{1,0:T(8,128)(2,1)S(1)} %copy.107) | copy-start | bytes 3538948
  306.2 39.7 %copy-start = (bf16[256,768]{1,0:T(8,128)(2,1)S(1)}, bf16[256,768]{1,0:T(8,128)(2,1)}, u32[]{:S(2)}) copy-start(bf16[256,768]{1,0:T(8,128)(2,1)} %param.27) | copy-start | bytes 1179652
  306.2 60.8 %all-gather.14.cloned.1.call-start = ((), (), s32[]{:S(2)}) async-start(), calls=%async_computation.14 | async-start | bytes 1966080 | tf_op jit(solution)/shard_map/all_gather | solution.py:205
  347.3 70.1 %reduce-scatter.25.cloned.1.call-start = ((), (), s32[]{:S(2)}) async-start(), calls=%async_computation.15 | async-start | bytes 3932160 | tf_op jit(solution)/shard_map/reduce_scatter | solution.py:218
  367.0 8.8 %copy-start.31 = (bf16[768,768]{1,0:T(8,128)(2,1)S(1)}, bf16[768,768]{1,0:T(8,128)(2,1)}, u32[]{:S(2)}) copy-start(bf16[768,768]{1,0:T(8,128)(2,1)} %all-gather.10.cloned.1.call-done) | copy-start | bytes 3538948
  379.5 62.7 %all-gather.16.cloned.1.call-start = ((), (), s32[]{:S(2)}) async-start(), calls=%async_computation.16 | async-start | bytes 1966080 | tf_op jit(solution)/shard_map/all_gather | solution.py:223
  422.3 89.5 %reduce-scatter.35.cloned.1.call-start = ((), (), s32[]{:S(2)}) async-start(), calls=%async_computation.22 | async-start | bytes 147456
  424.2 20.2 %copy-start.10 = (bf16[192,768]{1,0:T(8,128)(2,1)S(1)}, bf16[192,768]{1,0:T(8,128)(2,1)}, u32[]{:S(2)}) copy-start(bf16[192,768]{1,0:T(8,128)(2,1)} %copy.104) | copy-start | bytes 884740
  427.5 151.3 %reduce-scatter.37.cloned.1.call-start = ((), (), s32[]{:S(2)}) async-start(), calls=%async_computation.23 | async-start | bytes 442368
  467.4 18.4 %copy-start.5 = (bf16[3,1024,192]{1,2,0:T(8,128)(2,1)}, bf16[3,1024,192]{1,2,0:T(8,128)(2,1)S(1)}, u32[]{:S(2)}) copy-start(bf16[3,1024,192]{1,2,0:T(8,128)(2,1)S(1)} %constant_dynamic-update-slice_fusion) | copy-start | bytes 3538948
  467.4 7.0 copy-start.4
  474.4 105.9 %all-reduce.5.cloned.1.call-start = ((), (), s32[]{:S(2)}) async-start(), calls=%async_computation.17 | async-start | bytes 3145728 | tf_op jit(solution)/shard_map/psum | solution.py:246
  479.9 138.1 %reduce-scatter.31.cloned.1.call-start = ((), (), s32[]{:S(2)}) async-start(), calls=%async_computation.20 | async-start | bytes 884736
  485.5 202.0 %reduce-scatter.29.cloned.1.call-start = ((), (), s32[]{:S(2)}) async-start(), calls=%async_computation.19 | async-start | bytes 2211840
  496.4 264.0 %reduce-scatter.33.cloned.1.call-start = ((), (), s32[]{:S(2)}) async-start(), calls=%async_computation.21 | async-start | bytes 2654208
  503.0 329.8 %reduce-scatter.27.cloned.1.call-start = ((), (), s32[]{:S(2)}) async-start(), calls=%async_computation.18 | async-start | bytes 2654208 | tf_op jit(solution)/shard_map/reduce_scatter | solution.py:270
  509.4 43.5 %copy-start.22 = (f32[4]{0:T(128)S(1)}, f32[4]{0:T(128)}, u32[]{:S(2)}) copy-start(f32[4]{0:T(128)} %param.24) | copy-start | bytes 52
  509.4 46.7 %copy-start.6 = (bf16[3,1024,192]{1,2,0:T(8,128)(2,1)S(1)}, bf16[3,1024,192]{1,2,0:T(8,128)(2,1)}, u32[]{:S(2)}) copy-start(bf16[3,1024,192]{1,2,0:T(8,128)(2,1)} %copy-done.5) | copy-start | bytes 3538948
  (35 other events, 75.7 us)
Sparse Core Ops, SparseCore 0:
  188.0 37.8 reduce-scatter.20
  306.3 37.9 reduce-scatter.22
  422.4 19.7 all-gather.15
  480.0 43.4 all-reduce.4
Sparse Core Ops, SparseCore 1:
  190.8 41.2 all-gather.11
  234.3 39.7 all-gather.9
  276.1 17.9 all-gather.7
  347.4 19.5 all-gather.13
  379.6 37.8 reduce-scatter.24
  427.6 60.9 reduce-scatter.34
  492.1 60.6 reduce-scatter.36
  556.3 61.7 reduce-scatter.30
  621.3 66.0 reduce-scatter.28
  691.9 68.4 reduce-scatter.32
  764.7 68.0 reduce-scatter.26
where the time goes:
time: 850 us; the launch traced here: 841 us
  waiting for transfers between devices  402 us (47%)
  blocking collectives  253 us (30%)
  matrix products  64.2 us (8%)
  local copies, waits for them, and re-layouts  52.2 us (6%)
  other arithmetic  48.4 us (6%)
  between operations  17.5 us (2%)
    unnamed x20, waiting for transfers between devices  175 us
    reduce_scatter x1, waiting for transfers between devices, per_device(): lax.psum_scatter(grad_up_w * slope(gathered[2].astype(jnp.float32), w_pea...  72.4 us
    pmax x1, blocking collectives, peak_all(): return lax.pmax(peak_of(values), ('dp', 'mp'))  39.7 us
    all_gather x1, blocking collectives, per_device(): lax.all_gather(w_qkv, 'dp', axis=1, tiled=True)  38.6 us
    pmax x1, blocking collectives, per_device(): lax.pmax((peak_of(w_qkv), peak_of(w_out), peak_of(w_up), peak_of(w_down))...  38.5 us
    reduce_scatter x1, waiting for transfers between devices, per_device(): lax.psum_scatter(product(act_quant, down_q), 'mp', scatter_dimension=0, t...  38 us
    reduce_scatter x1, waiting for transfers between devices, per_device(): lax.psum_scatter(partial_hid, 'mp', scatter_dimension=0, tiled=True)  37.9 us
    all_gather x1, blocking collectives, per_device(): lax.all_gather(w_out, 'dp', axis=1, tiled=True)  31 us
  transfers between devices with their start and end apart: 15, of which 11 were waited for; matrix products, arithmetic and copies ran while one was open for 11% of the time, Pallas kernels for 0%

commit v1 on v0

--- a/solution.py
+++ b/solution.py
@@ -1,6 +1,8 @@
 import jax
 import jax.numpy as jnp
 from jax import lax
+from jax.experimental import pallas as pl
+from jax.experimental.pallas import tpu as pltpu
 from jax.sharding import PartitionSpec as P
 
 HD = 64
@@ -301,6 +303,965 @@
     )
 
 
+BF = jnp.bfloat16
+F32 = jnp.float32
+MESH = pl.DeviceIdType.MESH
+WIDE = 768
+PIECE = 96
+CUT = 48
+OWN = 256
+HERE = 384
+
+
+def nn(left, right):
+    return lax.dot_general(left, right, (((1,), (0,)), ((), ())), preferred_element_type=F32)
+
+
+def nt(left, right):
+    return lax.dot_general(left, right, (((1,), (1,)), ((), ())), preferred_element_type=F32)
+
+
+def mul8(value, step):
+    return pl.multiple_of(value, step)
+
+
+def loop(count, body):
+    def step(index, carry):
+        body(index)
+        return carry
+
+    lax.fori_loop(0, count, step, 0)
+
+
+def layer_kernel(
+    tok,
+    w_qkv,
+    w_out,
+    w_up,
+    w_down,
+    b_qv,
+    b_up,
+    vectors,
+    ranges,
+    mask,
+    long_rows,
+    grad_out,
+    o_layer,
+    o_tok,
+    o_qkv,
+    o_out,
+    o_up,
+    o_down,
+    o_bqv,
+    o_bup,
+    o_vec,
+    o_rng,
+    wts,
+    wff,
+    wc,
+    wo,
+    rdx,
+    rdy,
+    rxx,
+    ryy,
+    rzz,
+    sm,
+    smc,
+    vec,
+    bup,
+    bqv,
+    xq,
+    xqt,
+    bias,
+    qs,
+    ks,
+    vs,
+    kt,
+    vt,
+    probs,
+    ds,
+    ctxt,
+    cq,
+    slc,
+    exa_s,
+    exa_r,
+    exb_s,
+    exb_r,
+    hq,
+    hqt,
+    r1,
+    n1,
+    rstd1,
+    sl1,
+    aq,
+    fac,
+    gu,
+    gf,
+    rowt,
+    gr2,
+    gc,
+    gct,
+    dsum,
+    grads,
+    gqt,
+    gwo,
+    tot,
+    tot_c,
+    tot_x,
+    tot_y,
+    tot_z,
+    zs,
+    zr,
+    xs,
+    xr,
+    ys,
+    yr,
+    dxs,
+    dxr,
+    dys,
+    dyr,
+    rs_s,
+    rs_r,
+    sm_s,
+    sm_r,
+    ex_s,
+    ex_r,
+    tt_s,
+    tt_r,
+    gx_s,
+    gx_r,
+):
+    dp = lax.axis_index("dp")
+    mp = lax.axis_index("mp")
+    z, y = dp // 2, dp % 2
+    x, c = mp // 2, mp % 2
+    nx, ny, nc = 1 - x, 1 - y, 1 - c
+    to_x = (dp, nx * 2 + c)
+    to_y = (z * 2 + ny, mp)
+    to_c = (dp, x * 2 + nc)
+    to_z = [None] + [((z + k) % 4 * 2 + y, mp) for k in (1, 2, 3)]
+    zk = [z] + [(z + 4 - k) % 4 for k in (1, 2, 3)]
+    zf = [z] + [(z + k) % 4 for k in (1, 2, 3)]
+    mine = mul8(c * OWN, OWN)
+    theirs = mul8(nc * OWN, OWN)
+    started = {}
+
+    def copy(src, dst, send, recv, device):
+        return pltpu.make_async_remote_copy(
+            src_ref=src, dst_ref=dst, send_sem=send, recv_sem=recv, device_id=device, device_id_type=MESH
+        )
+
+    def send(group, *args):
+        made = copy(*args)
+        made.start()
+        started.setdefault(group, []).append(made)
+
+    def sent(group):
+        for made in started.pop(group, []):
+            made.wait_send()
+
+    range_of = [ranges[i] for i in range(4)]
+    inv_of = [1.0 / r for r in range_of]
+
+    wts[1, x, z, y] = w_up[...]
+    wts[2, x, z, y] = w_down[...].T
+    turned = w_out[...].T
+    for j, part in enumerate((w_qkv[0], w_qkv[1], w_qkv[2], turned)):
+        wts[0, x, z, y, :, j * 128 : j * 128 + 128] = part[:, 0:128]
+        wts[0, x, z, y, :, 512 + j * 64 : 576 + j * 64] = part[:, 128:192]
+
+    sm[x, z, y] = jnp.zeros((16, 128), F32)
+    sm[x, z, y, 0:6, 0:96] = vectors[...].astype(F32)
+    sm[x, z, y, 6:9, 0:32] = b_up[...].astype(F32)
+    sm[x, z, y, 9:12, 0:8] = b_qv[0].astype(F32)
+    sm[x, z, y, 12:15, 0:8] = b_qv[1].astype(F32)
+    lane = lax.broadcasted_iota(jnp.int32, (1, 128), 1)
+    peak_row = jnp.zeros((1, 128), F32)
+    for g, ref in enumerate((w_qkv, w_out, w_up, w_down)):
+        most = jnp.abs(ref[...].astype(F32))
+        if most.ndim == 3:
+            most = jnp.max(most, axis=0)
+        most = jnp.max(jnp.max(most, axis=0, keepdims=True), axis=1, keepdims=True)
+        peak_row = jnp.where(lane == g, most, peak_row)
+    sm[x, z, y, 15:16] = peak_row
+
+    barrier = pltpu.get_barrier_semaphore()
+    for device in (to_c, to_x, to_y, *to_z[1:]):
+        pl.semaphore_signal(barrier, inc=1, device_id=device, device_id_type=MESH)
+    pl.semaphore_wait(barrier, 6)
+
+    def ag_z_send(g):
+        for k in (1, 2, 3):
+            own = wts.at[g, x, z, y]
+            send(("ag", g), own, own, zs.at[g, k - 1], zr.at[g, k - 1], to_z[k])
+
+    def ag_xy_send(g, k):
+        own = wts.at[g, x, zk[k], y]
+        if k > 0:
+            copy(own, own, zs.at[g, k - 1], zr.at[g, k - 1], to_z[k]).wait_recv()
+        send(("ag", g), own, own, xs.at[g, k], xr.at[g, k], to_x)
+        send(("ag", g), own, own, ys.at[g, k], yr.at[g, k], to_y)
+
+    def ag_diag(g, k):
+        got = wts.at[g, x, zk[k], ny]
+        copy(got, got, ys.at[g, k], yr.at[g, k], to_y).wait_recv()
+        half = wts.at[g, x, zk[k], ny, pl.ds(0, CUT)]
+        send(("ag", g), half, half, dxs.at[g, k], dxr.at[g, k], to_x)
+        got = wts.at[g, nx, zk[k], y]
+        copy(got, got, xs.at[g, k], xr.at[g, k], to_x).wait_recv()
+        half = wts.at[g, nx, zk[k], y, pl.ds(CUT, PIECE - CUT)]
+        send(("ag", g), half, half, dys.at[g, k], dyr.at[g, k], to_y)
+
+    def ag_last(g, k):
+        half = wts.at[g, nx, zk[k], ny, pl.ds(0, CUT)]
+        copy(half, half, dxs.at[g, k], dxr.at[g, k], to_x).wait_recv()
+        half = wts.at[g, nx, zk[k], ny, pl.ds(CUT, PIECE - CUT)]
+        copy(half, half, dys.at[g, k], dyr.at[g, k], to_y).wait_recv()
+
+    small_c = copy(sm.at[x, z, y], smc, sm_s.at[0], sm_r.at[0], to_c)
+    small_c.start()
+    ag_z_send(0)
+    ag_xy_send(0, 0)
+
+    base = mul8(x * 512, 512)
+
+    def do_tokens(i):
+        rows = pl.ds(mul8(i * 128, 128), 128)
+        v = tok[pl.ds(mul8(base + i * 128, 128), 128), :].astype(F32)
+        xq[rows, :] = (range_of[0] * jnp.tanh(v * inv_of[0])).astype(BF)
+
+    loop(4, do_tokens)
+    small_c.wait()
+    sm[x, z, y, 15:16] = jnp.maximum(sm[x, z, y, 15:16], smc[15:16])
+    small_x = copy(sm.at[x, z, y], sm.at[x, z, y], sm_s.at[1], sm_r.at[1], to_x)
+    small_x.start()
+    ag_xy_send(0, 1)
+
+    def do_turn(j):
+        cols = pl.ds(mul8(j * 128, 128), 128)
+        xqt[cols, :] = xq[:, cols].T
+
+    loop(6, do_turn)
+    copy(sm.at[nx, z, y], sm.at[nx, z, y], sm_s.at[1], sm_r.at[1], to_x).wait_recv()
+    small_y = copy(sm.at[:, z, y], sm.at[:, z, y], sm_s.at[2], sm_r.at[2], to_y)
+    small_y.start()
+    ag_diag(0, 0)
+    ag_xy_send(0, 2)
+
+    long_flag = long_rows[x].astype(F32)
+    for r in range(4):
+        row = mask[pl.ds(x * 4 + r, 1), :].astype(F32)
+        column = jnp.broadcast_to(row, (128, 128)).T
+        for s in range(4):
+            seen = column * (1.0 if r == s else long_flag)
+            bias[r * 128 : r * 128 + 128, s * 128 : s * 128 + 128] = jnp.where(seen > 0.5, 0.0, -1e30)
+
+    copy(sm.at[:, z, ny], sm.at[:, z, ny], sm_s.at[2], sm_r.at[2], to_y).wait_recv()
+    small_z = []
+    for k in (1, 2, 3):
+        made = copy(sm.at[:, z], sm.at[:, z], sm_s.at[2 + k], sm_r.at[2 + k], to_z[k])
+        made.start()
+        small_z.append(made)
+    ag_diag(0, 1)
+    ag_xy_send(0, 3)
+    ag_z_send(1)
+    ag_diag(0, 2)
+    for k in (1, 2, 3):
+        copy(sm.at[:, zk[k]], sm.at[:, zk[k]], sm_s.at[2 + k], sm_r.at[2 + k], to_z[k]).wait_recv()
+    ag_diag(0, 3)
+    small_x.wait_send()
+    small_y.wait_send()
+    for made in small_z:
+        made.wait_send()
+
+    peaks = jnp.max(jnp.max(jnp.max(sm[:, :, :, 15:16, :], axis=0), axis=0), axis=0)
+    w_peak = [jnp.max(jnp.where(lane == g, peaks, 0.0)) for g in range(4)]
+    w_inv = [1.0 / r for r in w_peak]
+
+    def spread(xx, width, step):
+        total = None
+        for place in range(8):
+            tile = sm[xx, place // 2, place % 2]
+            if width > 128:
+                tile = jnp.concatenate([tile, jnp.zeros((16, width - 128), F32)], axis=1)
+            if place:
+                tile = pltpu.roll(tile, place * step, 1)
+            total = tile if total is None else total + tile
+        return total
+
+    vec[...] = spread(0, WIDE, 96)
+    heads = []
+    for xx in range(2):
+        wide = spread(xx, 256, 32)
+        for h in range(3):
+            bup[xx : xx + 1, h * 256 : h * 256 + 256] = wide[6 + h : 7 + h, :]
+        narrow = spread(xx, 128, 8)
+        heads.append((narrow, pltpu.roll(narrow, 64, 1)))
+    for j, first in enumerate((9, 12)):
+        for xx in range(2):
+            bqv[j : j + 1, xx * 128 : xx * 128 + 128] = (
+                heads[xx][0][first : first + 1] + heads[xx][1][first + 1 : first + 2]
+            )
+        bqv[j : j + 1, 256:384] = heads[0][0][first + 2 : first + 3] + heads[1][1][first + 2 : first + 3]
+
+    for k in range(4):
+        ag_xy_send(1, k)
+    ag_z_send(2)
+    for k in range(4):
+        ag_last(0, k)
+
+    left = lax.broadcasted_iota(jnp.int32, (PIECE, 128), 1) < 64
+
+    def squash_heads(place):
+        rows = pl.ds(mul8(place * PIECE, PIECE), PIECE)
+        tiles = []
+        for xx in range(2):
+            v = wts[0, xx, place // 2, place % 2].astype(F32)
+            inner = [w_peak[0] * jnp.tanh(v[:, t * 128 : t * 128 + 128] * w_inv[0]) for t in (0, 1, 2)]
+            inner.append(w_peak[1] * jnp.tanh(v[:, 384:512] * w_inv[1]))
+            mixed = jnp.where(left, w_peak[0], w_peak[1])
+            mixed_inv = jnp.where(left, w_inv[0], w_inv[1])
+            inner.append(w_peak[0] * jnp.tanh(v[:, 512:640] * w_inv[0]))
+            inner.append(mixed * jnp.tanh(v[:, 640:768] * mixed_inv))
+            tiles.append(inner)
+        for t in range(3):
+            for xx in range(2):
+                wc[rows, t * HERE + xx * 128 : t * HERE + xx * 128 + 128] = tiles[xx][t].astype(BF)
+        for xx in range(2):
+            wo[rows, xx * 128 : xx * 128 + 128] = tiles[xx][3].astype(BF)
+        for t, first, second in ((4, 0, 1), (5, 2, 3)):
+            one, two = tiles[0][t], tiles[1][t]
+            wc[rows, first * HERE + 256 : first * HERE + 384] = jnp.where(left, one, pltpu.roll(two, 64, 1)).astype(BF)
+            other = jnp.where(left, pltpu.roll(one, 64, 1), two).astype(BF)
+            if second == 1:
+                wc[rows, HERE + 256 : HERE + 384] = other
+            else:
+                wo[rows, 256:384] = other
+
+    loop(8, squash_heads)
+
+    def squash_ff(g, xx):
+        def body(place):
+            v = wts[g, xx, place // 2, place % 2].astype(F32)
+            wff[g - 1, xx, pl.ds(mul8(place * PIECE, PIECE), PIECE), :] = (
+                w_peak[g + 1] * jnp.tanh(v * w_inv[g + 1])
+            ).astype(BF)
+
+        loop(8, body)
+
+    for j, held in enumerate((qs, ks, vs)):
+
+        def project(i, j=j, held=held):
+            rows = pl.ds(mul8(i * 256, 256), 256)
+            got = nn(xq[rows, :], wc[:, j * HERE : (j + 1) * HERE])
+            if j == 0:
+                got = (got + bqv[0:1, :]) * 0.125
+            elif j == 2:
+                got = got + bqv[1:2, :]
+            held[rows, :] = got.astype(BF)
+
+        loop(2, project)
+    for p in range(3):
+        cols = slice(p * 128, p * 128 + 128)
+        kt[cols, :] = ks[:, cols].T
+        vt[cols, :] = vs[:, cols].T
+    ag_diag(1, 0)
+
+    half_of = lax.broadcasted_iota(jnp.int32, (1, 128), 1) // 64
+
+    def attend(p):
+        cols = pl.ds(mul8(p * 128, 128), 128)
+        for e in range(2):
+            feats = pl.ds(mul8(p * 128 + e * 64, 64), 64)
+            for n in range(2):
+                q = qs[n * 256 : n * 256 + 256, cols]
+                q = jnp.where(half_of == e, q, jnp.zeros_like(q))
+                s = nt(ks[:, cols], q) + bias[:, n * 256 : n * 256 + 256]
+                s = jnp.exp(s - jnp.max(s, axis=0, keepdims=True))
+                s = (s * (1.0 / jnp.sum(s, axis=0, keepdims=True))).astype(BF)
+                probs[p * 2 + e, :, n * 256 : n * 256 + 256] = s
+                ctxt[feats, n * 256 : n * 256 + 256] = nn(vt[feats, :], s)
+
+    for p in range(3):
+        attend(p)
+        ag_diag(1, p + 1)
+
+    for p in range(3):
+        cols = slice(p * 128, p * 128 + 128)
+        bent = jnp.tanh(ctxt[cols, :].T * inv_of[1])
+        cq[:, cols] = (range_of[1] * bent).astype(BF)
+        slc[:, cols] = 1.0 - bent * bent
+    tot[0] = jnp.zeros((16, WIDE), F32)
+    most = jnp.max(jnp.max(jnp.abs(ctxt[...]), axis=0, keepdims=True), axis=1, keepdims=True)
+    tot[0, 10:11, :] = jnp.broadcast_to(most, (1, WIDE))
+
+    def out_part(start, held):
+        def body(n):
+            cols = pl.ds(mul8(n * 256, 256), 256)
+            held[:, cols] = nt(cq[pl.ds(start, OWN), :], wo[cols, :])
+
+        loop(3, body)
+
+    out_part(theirs, exa_s)
+    ex1 = copy(exa_s, exa_r, ex_s.at[0], ex_r.at[0], to_c)
+    ex1.start()
+    for k in range(4):
+        ag_xy_send(2, k)
+    out_part(mine, r1)
+    ex1.wait()
+
+    def sum_rows(v):
+        return jnp.sum(v, axis=0, keepdims=True)
+
+    def mean_of(v):
+        return jnp.sum(v, axis=-1, keepdims=True) * (1.0 / WIDE)
+
+    def first_norm(i):
+        rows = pl.ds(mul8(i * 64, 64), 64)
+        v = tok[pl.ds(mul8(base + mine + i * 64, 64), 64), :].astype(F32)
+        v = v + (r1[rows, :] + exa_r[rows, :] + vec[0:1, :])
+        r1[rows, :] = v
+        center = v - mean_of(v)
+        factor = lax.rsqrt(mean_of(center * center) + 1e-12)
+        normed = center * factor
+        n1[rows, :] = normed
+        rstd1[rows, :] = factor
+        h = normed * vec[2:3, :] + vec[3:4, :]
+        tot[0, 11:12, :] = jnp.maximum(tot[0, 11:12, :], jnp.max(jnp.abs(h), axis=0, keepdims=True))
+        bent = jnp.tanh(h * inv_of[2])
+        sl1[rows, :] = 1.0 - bent * bent
+        hq[pl.ds(mul8(mine + i * 64, 64), 64), :] = (range_of[2] * bent).astype(BF)
+
+    loop(4, first_norm)
+
+    def share_rows(held, number):
+        own = held.at[pl.ds(mine, OWN)]
+        made = copy(own, own, ex_s.at[number], ex_r.at[number], to_c)
+        made.start()
+        started.setdefault("share", []).append(made)
+
+    def got_rows(held, number):
+        other = held.at[pl.ds(theirs, OWN)]
+        copy(other, other, ex_s.at[number], ex_r.at[number], to_c).wait_recv()
+
+    def turn_rows(held, out, start):
+        def body(j):
+            cols = pl.ds(mul8(j * 128, 128), 128)
+            out[cols, pl.ds(start, OWN)] = held[pl.ds(start, OWN), cols].T
+
+        loop(6, body)
+
+    share_rows(hq, 1)
+    for k in range(4):
+        ag_last(1, k)
+    squash_ff(1, 0)
+    squash_ff(1, 1)
+    ag_diag(2, 0)
+    got_rows(hq, 1)
+    turn_rows(hq, hqt, 0)
+    turn_rows(hq, hqt, OWN)
+
+    def expand(xx):
+        def body(j):
+            n, i = j // 2, j % 2
+            cols = pl.ds(mul8(n * 256, 256), 256)
+            wide = pl.ds(mul8(xx * WIDE + n * 256, 256), 256)
+            rows = pl.ds(mul8(i * 256, 256), 256)
+            u = nn(hq[rows, :], wff[0, xx, :, cols]) + bup[xx : xx + 1, cols]
+            cdf = 0.5 * (1.0 + lax.erf(u * 0.7071067811865476))
+            a = u * cdf
+            tot[0, 12:13, 0:256] = jnp.maximum(tot[0, 12:13, 0:256], jnp.max(jnp.abs(a), axis=0, keepdims=True))
+            bent = jnp.tanh(a * inv_of[3])
+            aq[rows, wide] = (range_of[3] * bent).astype(BF)
+            pdf = 0.3989422804014327 * jnp.exp(-0.5 * u * u)
+            fac[rows, wide] = ((1.0 - bent * bent) * (cdf + u * pdf)).astype(fac.dtype)
+
+        loop(6, body)
+
+    expand(0)
+    ag_diag(2, 1)
+    expand(1)
+    ag_diag(2, 2)
+    ag_diag(2, 3)
+
+    def down_part(start, held, xx, first):
+        def body(n):
+            cols = pl.ds(mul8(n * 256, 256), 256)
+            got = nt(aq[pl.ds(start, OWN), pl.ds(mul8(xx * WIDE, WIDE), WIDE)], wff[1, xx, cols, :])
+            held[:, cols] = got if first else held[:, cols] + got
+
+        loop(3, body)
+
+    squash_ff(2, x)
+    down_part(theirs, exb_s, x, True)
+    down_part(mine, gr2, x, True)
+    for k in range(4):
+        ag_last(2, k)
+    squash_ff(2, nx)
+    down_part(theirs, exb_s, nx, False)
+    ex2 = copy(exb_s, exb_r, ex_s.at[2], ex_r.at[2], to_c)
+    ex2.start()
+    down_part(mine, gr2, nx, False)
+    ex2.wait()
+
+    def second_norm(i):
+        rows = pl.ds(mul8(i * 64, 64), 64)
+        v = r1[rows, :] + (gr2[rows, :] + exb_r[rows, :] + vec[1:2, :])
+        center = v - mean_of(v)
+        factor = lax.rsqrt(mean_of(center * center) + 1e-12)
+        normed = center * factor
+        o_layer[rows, :] = (normed * vec[4:5, :] + vec[5:6, :]).astype(BF)
+        gy = grad_out[rows, :].astype(F32)
+        tot[0, 4:5, :] += sum_rows(gy * normed)
+        tot[0, 5:6, :] += sum_rows(gy)
+        gn = gy * vec[4:5, :]
+        back = factor * (gn - mean_of(gn) - normed * mean_of(gn * normed))
+        gr2[rows, :] = back
+        low = back.astype(BF)
+        tot[0, 1:2, :] += sum_rows(low.astype(F32))
+        gf[pl.ds(mul8(mine + i * 64, 64), 64), :] = low
+
+    loop(4, second_norm)
+    share_rows(gf, 3)
+    turn_rows(gf, rowt, mine)
+    for g in range(3):
+        sent(("ag", g))
+    got_rows(gf, 3)
+    turn_rows(gf, rowt, theirs)
+
+    def rs_send(g, number, src, dst, device):
+        send("rs", src, dst, rs_s.at[g, number], rs_r.at[g, number], device)
+
+    def rs_wait(g, number, dst, device):
+        copy(dst, dst, rs_s.at[g, number], rs_r.at[g, number], device).wait_recv()
+
+    top, low_half = pl.ds(0, CUT), pl.ds(CUT, PIECE - CUT)
+
+    def rs_first(g):
+        rs_send(g, 0, wts.at[g, nx, :, ny, top], rdx.at[g], to_x)
+        rs_send(g, 1, wts.at[g, nx, :, ny, low_half], rdy.at[g], to_y)
+        rs_send(g, 2, wts.at[g, nx, :, y, top], rxx.at[g, :, top], to_x)
+
+    def rs_second(g):
+        rs_send(g, 3, wts.at[g, x, :, ny, low_half], ryy.at[g, :, low_half], to_y)
+
+    def rs_third(g):
+        rs_wait(g, 0, rdx.at[g], to_x)
+
+        def add_x(i):
+            wts[g, x, i, ny, top] = (wts[g, x, i, ny, top].astype(F32) + rdx[g, i].astype(F32)).astype(BF)
+
+        loop(4, add_x)
+        rs_send(g, 4, wts.at[g, x, :, ny, top], ryy.at[g, :, top], to_y)
+        rs_wait(g, 1, rdy.at[g], to_y)
+
+        def add_y(i):
+            wts[g, nx, i, y, low_half] = (
+                wts[g, nx, i, y, low_half].astype(F32) + rdy[g, i].astype(F32)
+            ).astype(BF)
+
+        loop(4, add_y)
+        rs_send(g, 5, wts.at[g, nx, :, y, low_half], rxx.at[g, :, low_half], to_x)
+
+    def plane(g, zz):
+        return wts[g, x, zz, y].astype(F32) + rxx[g, zz].astype(F32) + ryy[g, zz].astype(F32)
+
+    def rs_fourth(g):
+        rs_wait(g, 2, rxx.at[g, :, top], to_x)
+        rs_wait(g, 3, ryy.at[g, :, low_half], to_y)
+        rs_wait(g, 4, ryy.at[g, :, top], to_y)
+        rs_wait(g, 5, rxx.at[g, :, low_half], to_x)
+        for k in (1, 2, 3):
+            wts[g, x, zf[k], y] = plane(g, zf[k]).astype(BF)
+            rs_send(g, 5 + k, wts.at[g, x, zf[k], y], rzz.at[g, k - 1], to_z[k])
+
+    def rs_total(g):
+        for k in (1, 2, 3):
+            rs_wait(g, 5 + k, rzz.at[g, k - 1], to_z[k])
+        total = plane(g, z)
+        for k in range(3):
+            total = total + rzz[g, k].astype(F32)
+        return total
+
+    def ff_grad(g, turned, held, xx):
+        def body(j):
+            n, i = j // 2, j % 2
+            cols = pl.ds(mul8(n * 256, 256), 256)
+            wide = pl.ds(mul8(xx * WIDE + n * 256, 256), 256)
+            got = nn(turned[pl.ds(mul8(i * HERE, HERE), HERE), :], held[:, wide])
+            wts[g, xx, pl.ds(i * 2, 2), :, :, cols] = got.reshape(2, 2, PIECE, 256).astype(BF)
+
+        loop(6, body)
+
+    ff_grad(2, rowt, aq, nx)
+    rs_first(2)
+    ff_grad(2, rowt, aq, x)
+    rs_second(2)
+
+    for xx in range(2):
+
+        def hidden_grad(j, xx=xx):
+            n, i = j // 2, j % 2
+            cols = pl.ds(mul8(n * 256, 256), 256)
+            wide = pl.ds(mul8(xx * WIDE + n * 256, 256), 256)
+            rows = pl.ds(mul8(i * 256, 256), 256)
+            got = (nn(gf[rows, :], wff[1, xx, :, cols]) * fac[rows, wide].astype(F32)).astype(BF)
+            gu[rows, wide] = got
+            tot[0, 6 + xx : 7 + xx, cols] += sum_rows(got.astype(F32))
+
+        loop(6, hidden_grad)
+    ff_grad(1, hqt, gu, nx)
+    rs_first(1)
+    ff_grad(1, hqt, gu, x)
+    rs_second(1)
+
+    def up_part(start, held):
+        def body(n):
+            cols = pl.ds(mul8(n * 256, 256), 256)
+            held[:, cols] = nt(gu[pl.ds(start, OWN), 0:WIDE], wff[0, 0, cols, :]) + nt(
+                gu[pl.ds(start, OWN), WIDE : 2 * WIDE], wff[0, 1, cols, :]
+            )
+
+        loop(3, body)
+
+    up_part(theirs, exa_s)
+    ex3 = copy(exa_s, exa_r, ex_s.at[4], ex_r.at[4], to_c)
+    ex3.start()
+    up_part(mine, r1)
+    rs_third(2)
+    ex3.wait()
+
+    def first_back(i):
+        rows = pl.ds(mul8(i * 64, 64), 64)
+        normed = n1[rows, :]
+        gh = (r1[rows, :] + exa_r[rows, :]) * sl1[rows, :]
+        tot[0, 2:3, :] += sum_rows(gh * normed)
+        tot[0, 3:4, :] += sum_rows(gh)
+        gn = gh * vec[2:3, :]
+        back = rstd1[rows, :] * (gn - mean_of(gn) - normed * mean_of(gn * normed)) + gr2[rows, :]
+        gr2[rows, :] = back
+        low = back.astype(BF)
+        tot[0, 0:1, :] += sum_rows(low.astype(F32))
+        gf[pl.ds(mul8(mine + i * 64, 64), 64), :] = low
+
+    sent("share")
+    loop(4, first_back)
+    share_rows(gf, 5)
+    turn_rows(gf, rowt, mine)
+    got_rows(gf, 5)
+    turn_rows(gf, rowt, theirs)
+
+    def out_grad(i):
+        rows = pl.ds(mul8(i * 256, 256), 256)
+        gwo[rows, :] = nn(rowt[rows, :], cq[...])
+
+    loop(3, out_grad)
+
+    def ctx_grad(i):
+        rows = pl.ds(mul8(i * 256, 256), 256)
+        gc[rows, :] = (nn(gf[rows, :], wo[...]) * slc[rows, :]).astype(BF)
+
+    loop(2, ctx_grad)
+    for p in range(3):
+        cols = slice(p * 128, p * 128 + 128)
+        gct[cols, :] = gc[:, cols].T
+        for e in range(2):
+            feats = slice(p * 128 + e * 64, p * 128 + e * 64 + 64)
+            dsum[p * 2 + e : p * 2 + e + 1, :] = sum_rows(gct[feats, :].astype(F32) * ctxt[feats, :])
+    rs_third(1)
+
+    row_half = lax.broadcasted_iota(jnp.int32, (128, 1), 0) // 64
+
+    def attend_back(p):
+        cols = pl.ds(mul8(p * 128, 128), 128)
+        grad_k = grad_v = None
+        for e in range(2):
+            feats = pl.ds(mul8(p * 128 + e * 64, 64), 64)
+            for n in range(2):
+                part = slice(n * 256, n * 256 + 256)
+                g = gct[cols, part]
+                g = jnp.where(row_half == e, g, jnp.zeros_like(g))
+                dpr = nn(vs[:, cols], g)
+                ds[:, part] = (probs[p * 2 + e, :, part].astype(F32) * (dpr - dsum[pl.ds(p * 2 + e, 1), part])).astype(BF)
+            g = gc[:, cols]
+            g = jnp.where(half_of == e, g, jnp.zeros_like(g))
+            more_v = nn(probs[p * 2 + e], g)
+            q = qs[:, cols]
+            q = jnp.where(half_of == e, q, jnp.zeros_like(q))
+            more_k = nn(ds[...], q)
+            grad_v = more_v if e == 0 else grad_v + more_v
+            grad_k = more_k if e == 0 else grad_k + more_k
+            gqt[feats, :] = nn(kt[feats, :], ds[...])
+        grads[:, pl.ds(mul8(HERE + p * 128, 128), 128)] = grad_k.astype(BF)
+        grads[:, pl.ds(mul8(2 * HERE + p * 128, 128), 128)] = grad_v.astype(BF)
+        grads[:, cols] = (gqt[cols, :].astype(BF).astype(F32) * 0.125).T.astype(BF)
+
+    attend_back(0)
+    attend_back(1)
+    rs_fourth(2)
+    attend_back(2)
+    for j, part in ((0, 0), (2, HERE)):
+        tot[0, 8:9, part : part + HERE] = sum_rows(grads[:, j * HERE : (j + 1) * HERE].astype(F32))
+
+    left_two = lax.broadcasted_iota(jnp.int32, (2 * PIECE, 128), 1) < 64
+
+    def head_grad(i):
+        rows = pl.ds(mul8(i * 2 * PIECE, 2 * PIECE), 2 * PIECE)
+        gq, gk, gv = (nn(xqt[rows, :], grads[:, j * HERE : (j + 1) * HERE]) for j in range(3))
+        parts = (gq, gk, gv, gwo[rows, :])
+
+        def put(xx, t, v):
+            wts[0, xx, i, :, :, t * 128 : t * 128 + 128] = v.reshape(2, PIECE, 128).astype(BF)
+
+        for xx in range(2):
+            for t in range(4):
+                put(xx, t, parts[t][:, xx * 128 : xx * 128 + 128])
+        for t, first, second in ((4, gq, gk), (5, gv, gwo[rows, :])):
+            one, two = first[:, 256:384], second[:, 256:384]
+            put(0, t, jnp.where(left_two, one, pltpu.roll(two, 64, 1)))
+            put(1, t, jnp.where(left_two, pltpu.roll(one, 64, 1), two))
+
+    loop(4, head_grad)
+    rs_first(0)
+    rs_second(0)
+
+    def token_part(start, held):
+        def body(n):
+            cols = pl.ds(mul8(n * 256, 256), 256)
+            held[:, cols] = nt(grads[pl.ds(start, OWN), :], wc[cols, :])
+
+        loop(3, body)
+
+    token_part(theirs, exb_s)
+    ex4 = copy(exb_s, exb_r, ex_s.at[6], ex_r.at[6], to_c)
+    ex4.start()
+    token_part(mine, r1)
+    rs_fourth(1)
+
+    def most_x(i):
+        v = jnp.abs(tok[pl.ds(mul8(base + i * 128, 128), 128), :].astype(F32))
+        tot[0, 9:10, :] = jnp.maximum(tot[0, 9:10, :], jnp.max(v, axis=0, keepdims=True))
+
+    loop(4, most_x)
+    row_of = lax.broadcasted_iota(jnp.int32, (16, 1), 0)
+    small = copy(tot.at[0], tot_c, tt_s.at[0], tt_r.at[0], to_c)
+    small.start()
+    ex4.wait()
+
+    def token_grad(i):
+        rows = pl.ds(mul8(i * 64, 64), 64)
+        v = tok[pl.ds(mul8(base + mine + i * 64, 64), 64), :].astype(F32)
+        bent = jnp.tanh(v * inv_of[0])
+        got = gr2[rows, :] + (r1[rows, :] + exb_r[rows, :]) * (1.0 - bent * bent)
+        o_tok[pl.ds(mul8(mp * OWN + i * 64, 64), 64), :] = got.astype(BF)
+
+    loop(4, token_grad)
+    own = o_tok.at[pl.ds(mul8(mp * OWN, OWN), OWN)]
+    send("tok", own, own, gx_s.at[0], gx_r.at[0], to_x)
+    send("tok", own, own, gx_s.at[1], gx_r.at[1], to_c)
+
+    small.wait()
+    mixed = jnp.where(row_of < 6, tot[0] + tot_c[...], jnp.maximum(tot[0], tot_c[...]))
+    tot[1] = jnp.where((row_of >= 6) & (row_of < 9), tot[0], mixed)
+    small = copy(tot.at[1], tot_x, tt_s.at[1], tt_r.at[1], to_x)
+    small.start()
+    rs_third(0)
+    small.wait()
+    tot[2] = jnp.where(row_of < 9, tot[1] + tot_x[...], jnp.maximum(tot[1], tot_x[...]))
+    small = copy(tot.at[2], tot_y, tt_s.at[2], tt_r.at[2], to_y)
+    small.start()
+    o_up[...] = rs_total(1) * _slope(w_up[...], w_inv[2])
+    small.wait()
+    tot[3] = jnp.where(row_of < 9, tot[2] + tot_y[...], jnp.maximum(tot[2], tot_y[...]))
+    smalls = []
+    for k in (1, 2, 3):
+        made = copy(tot.at[3], tot_z.at[k - 1], tt_s.at[2 + k], tt_r.at[2 + k], to_z[k])
+        made.start()
+        smalls.append(made)
+    o_down[...] = rs_total(2).T * _slope(w_down[...], w_inv[3])
+    rs_fourth(0)
+
+    far = o_tok.at[pl.ds(mul8((nx * 2 + c) * OWN, OWN), OWN)]
+    copy(far, far, gx_s.at[0], gx_r.at[0], to_x).wait_recv()
+    send("tok", far, far, gx_s.at[2], gx_r.at[2], to_c)
+
+    for made in smalls:
+        made.wait()
+    done = tot[3]
+    for k in range(3):
+        done = jnp.where(row_of < 9, done + tot_z[k], jnp.maximum(done, tot_z[k]))
+    back = pltpu.roll(done, (8 - dp) * 96, 1)
+    o_vec[...] = back[0:6, 0:96]
+    ups = jnp.where(x == 0, done[6:7, :], done[7:8, :])
+    for h in range(3):
+        tile = jnp.broadcast_to(ups[:, h * 256 : h * 256 + 256], (8, 256))
+        o_bup[h : h + 1, :] = pltpu.roll(tile, (8 - dp) * 32, 1)[0:1, 0:32]
+    for j in range(2):
+        row = jnp.broadcast_to(done[8:9, j * HERE : (j + 1) * HERE], (8, HERE))
+        pair = jnp.where(x == 0, row[:, 0:128], row[:, 128:256])
+        for h, tile, shift in ((0, pair, 0), (1, pair, 64), (2, row[:, 256:384], 64 * x)):
+            o_bqv[j, h : h + 1, :] = pltpu.roll(tile, (256 - shift - dp * 8) % 128, 1)[0:1, 0:8]
+    for i in range(4):
+        o_rng[i] = 0.9 * range_of[i] + 0.1 * jnp.max(done[9 + i : 10 + i, :])
+
+    total = rs_total(0)
+    for j in range(4):
+        main = total[:, j * 128 : j * 128 + 128]
+        pair = total[:, 512 + j // 2 * 128 : 640 + j // 2 * 128]
+        if j % 2:
+            pair = pltpu.roll(pair, 64, 1)
+        whole = jnp.concatenate([main, pair], axis=1)[:, 0:192]
+        if j < 3:
+            o_qkv[j] = whole * _slope(w_qkv[j], w_inv[0])
+        else:
+            o_out[...] = whole.T * _slope(w_out[...], w_inv[1])
+    near = o_tok.at[pl.ds(mul8((x * 2 + nc) * OWN, OWN), OWN)]
+    copy(near, near, gx_s.at[1], gx_r.at[1], to_c).wait_recv()
+    far = o_tok.at[pl.ds(mul8((nx * 2 + nc) * OWN, OWN), OWN)]
+    copy(far, far, gx_s.at[2], gx_r.at[2], to_c).wait_recv()
+    for group in list(started):
+        sent(group)
+
+
+def _slope(values, inverse):
+    bent = jnp.tanh(values.astype(F32) * inverse)
+    return 1.0 - bent * bent
+
+
+def layer_on_chips(
+    tokens, w_qkv, w_out, w_up, w_down, b_qv, b_up, vectors, ema_ranges, key_mask, long_rows, grad_out
+):
+    vmem = pltpu.VMEM
+    rows = tokens.shape[0]
+    half = rows // 2
+
+    def buffer(*shape, dtype=BF):
+        return vmem(shape, dtype)
+
+    def f32(*shape):
+        return vmem(shape, F32)
+
+    sems = pltpu.SemaphoreType.DMA
+    scratch = [
+        buffer(3, 2, 4, 2, PIECE, WIDE),
+        buffer(2, 2, WIDE, WIDE),
+        buffer(WIDE, 3 * HERE),
+        buffer(WIDE, HERE),
+        buffer(3, 4, CUT, WIDE),
+        buffer(3, 4, PIECE - CUT, WIDE),
+        buffer(3, 4, PIECE, WIDE),
+        buffer(3, 4, PIECE, WIDE),
+        buffer(3, 3, PIECE, WIDE),
+        f32(2, 4, 2, 16, 128),
+        f32(16, 128),
+        f32(16, WIDE),
+        f32(8, WIDE),
+        f32(8, HERE),
+        buffer(half, WIDE),
+        buffer(WIDE, half),
+        f32(half, half),
+        buffer(half, HERE),
+        buffer(half, HERE),
+        buffer(half, HERE),
+        buffer(HERE, half),
+        buffer(HERE, half),
+        buffer(6, half, half),
+        buffer(half, half),
+        f32(HERE, half),
+        buffer(half, HERE),
+        f32(half, HERE),
+        f32(OWN, WIDE),
+        f32(OWN, WIDE),
+        f32(OWN, WIDE),
+        f32(OWN, WIDE),
+        buffer(half, WIDE),
+        buffer(WIDE, half),
+        f32(OWN, WIDE),
+        f32(OWN, WIDE),
+        f32(OWN, 1),
+        f32(OWN, WIDE),
+        buffer(half, 2 * WIDE),
+        buffer(half, 2 * WIDE),
+        buffer(half, 2 * WIDE),
+        buffer(half, WIDE),
+        buffer(WIDE, half),
+        f32(OWN, WIDE),
+        buffer(half, HERE),
+        buffer(HERE, half),
+        f32(8, half),
+        buffer(half, 3 * HERE),
+        f32(HERE, half),
+        f32(WIDE, HERE),
+        f32(4, 16, WIDE),
+        f32(16, WIDE),
+        f32(16, WIDE),
+        f32(16, WIDE),
+        f32(3, 16, WIDE),
+        sems((3, 3)),
+        sems((3, 3)),
+        sems((3, 4)),
+        sems((3, 4)),
+        sems((3, 4)),
+        sems((3, 4)),
+        sems((3, 4)),
+        sems((3, 4)),
+        sems((3, 4)),
+        sems((3, 4)),
+        sems((3, 9)),
+        sems((3, 9)),
+        sems((6,)),
+        sems((6,)),
+        sems((7,)),
+        sems((7,)),
+        sems((6,)),
+        sems((6,)),
+        sems((3,)),
+        sems((3,)),
+    ]
+    whole = pl.BlockSpec(memory_space=vmem)
+    scalars = pl.BlockSpec(memory_space=pltpu.SMEM)
+    shape = jax.ShapeDtypeStruct
+    outs = pl.pallas_call(
+        layer_kernel,
+        out_shape=[
+            shape(grad_out.shape, BF),
+            shape(tokens.shape, BF),
+            shape(w_qkv.shape, F32),
+            shape(w_out.shape, F32),
+            shape(w_up.shape, F32),
+            shape(w_down.shape, F32),
+            shape(b_qv.shape, F32),
+            shape(b_up.shape, F32),
+            shape(vectors.shape, F32),
+            shape(ema_ranges.shape, F32),
+        ],
+        in_specs=[whole] * 8 + [scalars, whole, scalars, whole],
+        out_specs=[whole] * 9 + [scalars],
+        scratch_shapes=scratch,
+        compiler_params=pltpu.CompilerParams(
+            collective_id=0, has_side_effects=True, vmem_limit_bytes=VMEM_LIMIT
+        ),
+        name="encoder_layer",
+    )(
+        tokens,
+        w_qkv,
+        w_out,
+        w_up,
+        w_down,
+        b_qv,
+        b_up,
+        vectors,
+        ema_ranges,
+        key_mask.reshape(rows // 128, 128),
+        long_rows,
+        grad_out,
+    )
+    return (outs[0], outs[1].astype(F32), *outs[2:])
+
+
+VMEM_LIMIT = 64 * 1024 * 1024
+
+
 def solution(mesh):
     placed = (
         P("dp", None),
@@ -316,8 +1277,9 @@
         P("dp"),
         P(("dp", "mp"), None),
     )
+    on_chips = dict(mesh.shape) == {"dp": 8, "mp": 4}
     return jax.shard_map(
-        per_device,
+        layer_on_chips if on_chips else per_device,
         mesh=mesh,
         in_specs=placed,
         out_specs=(

time: 850 us -> 181 us (0.21); the launches traced: 841 us -> 181 us
  waiting for transfers between devices: 402 us -> 0 us
  blocking collectives: 253 us -> 0 us
  Pallas kernels: 0 us -> 166 us
  matrix products: 64.2 us -> 0 us
  other arithmetic: 48.4 us -> 3.38 us
  local copies, waits for them, and re-layouts: 52.2 us -> 10.6 us
  between operations: 17.5 us -> 0.67 us
    unnamed x20 -> x0, waiting for transfers between devices: 175 us -> none
    pallas_call x0 -> x1, Pallas kernels: none -> 166 us  [layer_on_chips(): pl.pallas_call(layer_kernel, out_shape=[shape(grad_out.shape, BF), shape(...]
    reduce_scatter x4 -> x0, waiting for transfers between devices: 157 us -> none  [the longest x1 72.4 us: per_device(): lax.psum_scatter(grad_up_w * slope(gathered[2].astype(jnp.float32), w_pea...]
    all_gather x5 -> x0, blocking collectives: 147 us -> none  [the longest x1 38.6 us: per_device(): lax.all_gather(w_qkv, 'dp', axis=1, tiled=True)]
    pmax x2 -> x0, blocking collectives: 78.2 us -> none  [the longest x1 39.7 us: peak_all(): return lax.pmax(peak_of(values), ('dp', 'mp'))]
    all_gather x5 -> x0, waiting for transfers between devices: 70.3 us -> none  [the longest x1 22.2 us: per_device(): lax.all_gather(w_up, 'dp', axis=0, tiled=True)]
    dot_general x26 -> x0, matrix products: 64.2 us -> none  [the longest x3 14.1 us: contract_cols(): lax.dot_general(left, right, (((1,), (1,)), ((), ())), preferred_element_...]
    unnamed x1 -> x0, blocking collectives: 21.5 us -> none
  transfers between devices with their start and end apart: 15 -> 0, of which waited for: 11 -> 0; matrix products, arithmetic and copies ran while one was open for 11% -> 0% of each run, Pallas kernels for 0% -> 0%
where the time goes in v1:
time: 181 us
  Pallas kernels  166 us (92%)
  local copies, waits for them, and re-layouts  10.6 us (6%)
  other arithmetic  3.38 us (2%)
    pallas_call x1, Pallas kernels, layer_on_chips(): pl.pallas_call(layer_kernel, out_shape=[shape(grad_out.shape, BF), shape(...  166 us
    unnamed x25, local copies, waits for them, and re-layouts  10.6 us

profile of v1, /device:TPU:0, one launch (start us, length us, event | category | flops | bytes accessed | tf_op | source)
XLA Modules:
  0.0 180.5 jit_solution(16026432655306428847)
XLA Ops:
  0.6 1.3 copy.23.b_qv
  1.9 1.7 copy.22.w_down
  3.6 165.9 %encoder_layer.1 = (bf16[256,768]{1,0:T(8,128)(2,1)}, bf16[1024,768]{1,0:T(8,128)(2,1)}, f32[3,96,192]{2,1,0:T(8,128)}, f32[192,96]{1,0:T(8,128)}, f32[96,768]{1...) custom-call(bf16[1024,768]{1,0:T(8,128)(2,1)} %tok.1, ...), custom_call_target="tpu_custom_call" | custom-call | tf_op jit(solution)/shard_map/encoder_layer/pallas_call | solution.py:1224
  169.5 1.3 copy.25
  170.8 1.9 %copy.24 = f32[768,96]{0,1:T(8,128)} copy(f32[768,96]{1,0:T(8,128)} %get-tuple-element.35) | data formatting | bytes 589824
  172.6 0.0 copy-start
  172.6 0.0 copy-start.2
  172.6 0.0 copy-start.3
  172.6 3.4 %convert_element_type.3 = f32[1024,768]{1,0:T(8,128)} convert(bf16[1024,768]{1,0:T(8,128)(2,1)} %get-tuple-element.21) | non-fusion elementwise | flops 786432 | bytes 4718592 | tf_op jit(solution)/shard_map/convert_element_type | solution.py:1259
  176.0 0.0 copy-done
  176.0 0.0 copy-start.6
  176.0 0.7 copy.33
  176.8 0.0 copy-done.2
  176.8 0.7 copy.34
  177.5 0.0 copy-done.3
  177.5 0.6 copy.35
  178.1 0.0 copy-done.1
  178.1 0.7 copy.36
  178.9 0.0 copy-done.5
  178.9 0.6 copy.37
  179.4 0.0 copy-done.4
  179.4 0.6 copy.38
  180.0 0.0 copy-done.6
  180.0 0.5 copy.39
  (3 shorter events, 0.0 us)
Async XLA Ops:
  172.6 3.4 %copy-start = (bf16[256,768]{1,0:T(8,128)(2,1)S(1)}, bf16[256,768]{1,0:T(8,128)(2,1)}, u32[]{:S(2)}) copy-start(bf16[256,768]{1,0:T(8,128)(2,1)} %get-tuple-element.50) | copy-start | bytes 1179652
  172.6 4.2 %copy-start.2 = (f32[3,96,192]{2,1,0:T(8,128)S(1)}, f32[3,96,192]{2,1,0:T(8,128)}, u32[]{:S(2)}) copy-start(f32[3,96,192]{2,1,0:T(8,128)} %get-tuple-element.52) | copy-start | bytes 663556
  172.6 4.9 %copy-start.3 = (f32[192,96]{1,0:T(8,128)S(1)}, f32[192,96]{1,0:T(8,128)}, u32[]{:S(2)}) copy-start(f32[192,96]{1,0:T(8,128)} %get-tuple-element.53) | copy-start | bytes 221188
  176.0 2.1 %copy-start.1 = (f32[96,768]{1,0:T(8,128)S(1)}, f32[96,768]{1,0:T(8,128)}, u32[]{:S(2)}) copy-start(f32[96,768]{1,0:T(8,128)} %get-tuple-element.54) | copy-start | bytes 884740
  176.0 2.8 %copy-start.5 = (f32[3,32]{1,0:T(4,128)S(1)}, f32[3,32]{1,0:T(4,128)}, u32[]{:S(2)}) copy-start(f32[3,32]{1,0:T(4,128)} %get-tuple-element.57) | copy-start | bytes 1156
  176.0 3.4 %copy-start.4 = (f32[6,96]{1,0:T(8,128)S(1)}, f32[6,96]{1,0:T(8,128)}, u32[]{:S(2)}) copy-start(f32[6,96]{1,0:T(8,128)} %get-tuple-element.58) | copy-start | bytes 6916
  176.0 4.0 %copy-start.6 = (f32[4]{0:T(128)S(1)}, f32[4]{0:T(128)}, u32[]{:S(2)}) copy-start(f32[4]{0:T(128)} %get-tuple-element.59) | copy-start | bytes 52

commit v2 on v1

--- a/solution.py
+++ b/solution.py
@@ -308,7 +308,8 @@
 MESH = pl.DeviceIdType.MESH
 WIDE = 768
 PIECE = 96
-CUT = 48
+AG_CUTS = ((16, 32, 48), (16, 48, 32), (16, 32, 48))
+RS_CUTS = ((16, 48, 32), (32, 32, 32), (32, 32, 32))
 OWN = 256
 HERE = 384
 
@@ -364,7 +365,11 @@
     rdy,
     rxx,
     ryy,
-    rzz,
+    rz,
+    rzf,
+    rz2,
+    rzf2,
+    rst,
     sm,
     smc,
     vec,
@@ -411,7 +416,13 @@
     tot_y,
     tot_z,
     zs,
+    zf,
     zr,
+    z2s,
+    z2f,
+    z2r,
+    sts,
+    str_,
     xs,
     xr,
     ys,
@@ -422,6 +433,8 @@
     dyr,
     rs_s,
     rs_r,
+    rf_s,
+    rf_r,
     sm_s,
     sm_r,
     ex_s,
@@ -439,9 +452,12 @@
     to_x = (dp, nx * 2 + c)
     to_y = (z * 2 + ny, mp)
     to_c = (dp, x * 2 + nc)
+    to_xy = (z * 2 + ny, nx * 2 + c)
     to_z = [None] + [((z + k) % 4 * 2 + y, mp) for k in (1, 2, 3)]
-    zk = [z] + [(z + 4 - k) % 4 for k in (1, 2, 3)]
-    zf = [z] + [(z + k) % 4 for k in (1, 2, 3)]
+    from_z = [z] + [(z + 4 - k) % 4 for k in (1, 2, 3)]
+    zk = [z, z + 1 - 2 * (z % 2), 2 - z // 2, 3 - 3 * (z // 2)]
+    outer = (z * z - 3 * z + 2) // 2
+    to_zk = [None] + [(zk[k] * 2 + y, mp) for k in (1, 2, 3)]
     mine = mul8(c * OWN, OWN)
     theirs = mul8(nc * OWN, OWN)
     started = {}
@@ -454,17 +470,28 @@
     def send(group, *args):
         made = copy(*args)
         made.start()
-        started.setdefault(group, []).append(made)
+        started.setdefault(group, []).append((made, None))
+
+    def send_if(which, group, *args):
+        made = copy(*args)
+        pl.when(outer == which)(made.start)
+        started.setdefault(group, []).append((made, which))
 
     def sent(group):
-        for made in started.pop(group, []):
-            made.wait_send()
+        for made, which in started.pop(group, []):
+            if which is None:
+                made.wait_send()
+            else:
+                pl.when(outer == which)(made.wait_send)
 
     range_of = [ranges[i] for i in range(4)]
     inv_of = [1.0 / r for r in range_of]
 
+    barrier = pltpu.get_barrier_semaphore()
+    for device in (to_c, to_x, to_y, to_xy, *to_z[1:]):
+        pl.semaphore_signal(barrier, inc=1, device_id=device, device_id_type=MESH)
     wts[1, x, z, y] = w_up[...]
-    wts[2, x, z, y] = w_down[...].T
+    wts[2, x, z, y] = w_down[...]
     turned = w_out[...].T
     for j, part in enumerate((w_qkv[0], w_qkv[1], w_qkv[2], turned)):
         wts[0, x, z, y, :, j * 128 : j * 128 + 128] = part[:, 0:128]
@@ -473,8 +500,8 @@
     sm[x, z, y] = jnp.zeros((16, 128), F32)
     sm[x, z, y, 0:6, 0:96] = vectors[...].astype(F32)
     sm[x, z, y, 6:9, 0:32] = b_up[...].astype(F32)
-    sm[x, z, y, 9:12, 0:8] = b_qv[0].astype(F32)
-    sm[x, z, y, 12:15, 0:8] = b_qv[1].astype(F32)
+    sm[x, z, y, 9:12, 0:8] = b_qv[:, 0, :].astype(F32)
+    sm[x, z, y, 12:15, 0:8] = b_qv[:, 1, :].astype(F32)
     lane = lax.broadcasted_iota(jnp.int32, (1, 128), 1)
     peak_row = jnp.zeros((1, 128), F32)
     for g, ref in enumerate((w_qkv, w_out, w_up, w_down)):
@@ -485,41 +512,68 @@
         peak_row = jnp.where(lane == g, most, peak_row)
     sm[x, z, y, 15:16] = peak_row
 
-    barrier = pltpu.get_barrier_semaphore()
-    for device in (to_c, to_x, to_y, *to_z[1:]):
-        pl.semaphore_signal(barrier, inc=1, device_id=device, device_id_type=MESH)
-    pl.semaphore_wait(barrier, 6)
+    pl.semaphore_wait(barrier, 7)
+
+    def ag_rows(g, xx, zz, yy, part):
+        strip, one, two = AG_CUTS[g]
+        first = (0, strip, strip + one, strip)[part]
+        return wts.at[g, xx, zz, yy, pl.ds(first, (strip, one, two, one + two)[part])]
+
+    def ag_strips(g, zz):
+        return wts.at[g, :, zz, :, pl.ds(0, AG_CUTS[g][0])]
+
+    def ag_strip_xy(g):
+        own = ag_rows(g, x, z, y, 0)
+        for i, device in enumerate((to_x, to_y, to_xy)):
+            send(("ag", g), own, own, sts.at[g, i], str_.at[g, i], device)
+
+    def ag_strip_z(g):
+        for i, (xx, yy, device) in enumerate(((nx, y, to_x), (x, ny, to_y), (nx, ny, to_xy))):
+            got = ag_rows(g, xx, z, yy, 0)
+            copy(got, got, sts.at[g, i], str_.at[g, i], device).wait_recv()
+        own = ag_strips(g, z)
+        send(("ag", g), own, own, z2s.at[g, 0], z2r.at[g, 0], to_zk[1])
+        send(("ag", g), own, own, z2s.at[g, 1], z2r.at[g, 1 + outer], to_zk[2])
+
+    def ag_strip_got(g, k):
+        got = ag_strips(g, zk[k])
+        copy(got, got, z2s.at[g, 0], z2r.at[g, k - 1], to_zk[k]).wait_recv()
+        if k > 1:
+            send_if(0, ("ag", g), got, got, z2f.at[g, k - 2], z2r.at[g, k - 1], to_zk[1])
 
     def ag_z_send(g):
-        for k in (1, 2, 3):
-            own = wts.at[g, x, z, y]
-            send(("ag", g), own, own, zs.at[g, k - 1], zr.at[g, k - 1], to_z[k])
+        own = ag_rows(g, x, z, y, 3)
+        send(("ag", g), own, own, zs.at[g, 0], zr.at[g, 0], to_zk[1])
+        send(("ag", g), own, own, zs.at[g, 1], zr.at[g, 1 + outer], to_zk[2])
 
     def ag_xy_send(g, k):
-        own = wts.at[g, x, zk[k], y]
+        own = ag_rows(g, x, zk[k], y, 3)
         if k > 0:
-            copy(own, own, zs.at[g, k - 1], zr.at[g, k - 1], to_z[k]).wait_recv()
+            copy(own, own, zs.at[g, 0], zr.at[g, k - 1], to_zk[k]).wait_recv()
+            if k > 1:
+                send_if(0, ("ag", g), own, own, zf.at[g, k - 2], zr.at[g, k - 1], to_zk[1])
         send(("ag", g), own, own, xs.at[g, k], xr.at[g, k], to_x)
         send(("ag", g), own, own, ys.at[g, k], yr.at[g, k], to_y)
 
     def ag_diag(g, k):
-        got = wts.at[g, x, zk[k], ny]
+        got = ag_rows(g, x, zk[k], ny, 3)
         copy(got, got, ys.at[g, k], yr.at[g, k], to_y).wait_recv()
-        half = wts.at[g, x, zk[k], ny, pl.ds(0, CUT)]
+        half = ag_rows(g, x, zk[k], ny, 1)
         send(("ag", g), half, half, dxs.at[g, k], dxr.at[g, k], to_x)
-        got = wts.at[g, nx, zk[k], y]
+        got = ag_rows(g, nx, zk[k], y, 3)
         copy(got, got, xs.at[g, k], xr.at[g, k], to_x).wait_recv()
-        half = wts.at[g, nx, zk[k], y, pl.ds(CUT, PIECE - CUT)]
+        half = ag_rows(g, nx, zk[k], y, 2)
         send(("ag", g), half, half, dys.at[g, k], dyr.at[g, k], to_y)
 
     def ag_last(g, k):
-        half = wts.at[g, nx, zk[k], ny, pl.ds(0, CUT)]
+        half = ag_rows(g, nx, zk[k], ny, 1)
         copy(half, half, dxs.at[g, k], dxr.at[g, k], to_x).wait_recv()
-        half = wts.at[g, nx, zk[k], ny, pl.ds(CUT, PIECE - CUT)]
+        half = ag_rows(g, nx, zk[k], ny, 2)
         copy(half, half, dys.at[g, k], dyr.at[g, k], to_y).wait_recv()
 
     small_c = copy(sm.at[x, z, y], smc, sm_s.at[0], sm_r.at[0], to_c)
     small_c.start()
+    ag_strip_xy(0)
     ag_z_send(0)
     ag_xy_send(0, 0)
 
@@ -535,6 +589,7 @@
     sm[x, z, y, 15:16] = jnp.maximum(sm[x, z, y, 15:16], smc[15:16])
     small_x = copy(sm.at[x, z, y], sm.at[x, z, y], sm_s.at[1], sm_r.at[1], to_x)
     small_x.start()
+    ag_strip_z(0)
     ag_xy_send(0, 1)
 
     def do_turn(j):
@@ -564,11 +619,15 @@
         small_z.append(made)
     ag_diag(0, 1)
     ag_xy_send(0, 3)
+    ag_strip_xy(1)
     ag_z_send(1)
+    for k in (1, 2, 3):
+        ag_strip_got(0, k)
     ag_diag(0, 2)
+    ag_xy_send(1, 0)
+    ag_diag(0, 3)
     for k in (1, 2, 3):
-        copy(sm.at[:, zk[k]], sm.at[:, zk[k]], sm_s.at[2 + k], sm_r.at[2 + k], to_z[k]).wait_recv()
-    ag_diag(0, 3)
+        copy(sm.at[:, from_z[k]], sm.at[:, from_z[k]], sm_s.at[2 + k], sm_r.at[2 + k], to_z[k]).wait_recv()
     small_x.wait_send()
     small_y.wait_send()
     for made in small_z:
@@ -604,9 +663,8 @@
             )
         bqv[j : j + 1, 256:384] = heads[0][0][first + 2 : first + 3] + heads[1][1][first + 2 : first + 3]
 
-    for k in range(4):
-        ag_xy_send(1, k)
-    ag_z_send(2)
+    ag_xy_send(1, 1)
+    ag_strip_z(1)
     for k in range(4):
         ag_last(0, k)
 
@@ -639,6 +697,7 @@
                 wo[rows, 256:384] = other
 
     loop(8, squash_heads)
+    ag_xy_send(1, 2)
 
     def squash_ff(g, xx):
         def body(place):
@@ -661,6 +720,9 @@
             held[rows, :] = got.astype(BF)
 
         loop(2, project)
+    ag_xy_send(1, 3)
+    ag_strip_xy(2)
+    ag_z_send(2)
     for p in range(3):
         cols = slice(p * 128, p * 128 + 128)
         kt[cols, :] = ks[:, cols].T
@@ -682,9 +744,16 @@
                 probs[p * 2 + e, :, n * 256 : n * 256 + 256] = s
                 ctxt[feats, n * 256 : n * 256 + 256] = nn(vt[feats, :], s)
 
-    for p in range(3):
-        attend(p)
-        ag_diag(1, p + 1)
+    attend(0)
+    ag_diag(1, 1)
+    for k in (1, 2, 3):
+        ag_strip_got(1, k)
+    attend(1)
+    ag_xy_send(2, 0)
+    ag_strip_z(2)
+    attend(2)
+    ag_diag(1, 2)
+    ag_xy_send(2, 1)
 
     for p in range(3):
         cols = slice(p * 128, p * 128 + 128)
@@ -694,6 +763,8 @@
     tot[0] = jnp.zeros((16, WIDE), F32)
     most = jnp.max(jnp.max(jnp.abs(ctxt[...]), axis=0, keepdims=True), axis=1, keepdims=True)
     tot[0, 10:11, :] = jnp.broadcast_to(most, (1, WIDE))
+    ag_diag(1, 3)
+    ag_xy_send(2, 2)
 
     def out_part(start, held):
         def body(n):
@@ -705,8 +776,7 @@
     out_part(theirs, exa_s)
     ex1 = copy(exa_s, exa_r, ex_s.at[0], ex_r.at[0], to_c)
     ex1.start()
-    for k in range(4):
-        ag_xy_send(2, k)
+    ag_xy_send(2, 3)
     out_part(mine, r1)
     ex1.wait()
 
@@ -738,7 +808,7 @@
         own = held.at[pl.ds(mine, OWN)]
         made = copy(own, own, ex_s.at[number], ex_r.at[number], to_c)
         made.start()
-        started.setdefault("share", []).append(made)
+        started.setdefault("share", []).append((made, None))
 
     def got_rows(held, number):
         other = held.at[pl.ds(theirs, OWN)]
@@ -780,6 +850,8 @@
 
     expand(0)
     ag_diag(2, 1)
+    for k in (1, 2, 3):
+        ag_strip_got(2, k)
     expand(1)
     ag_diag(2, 2)
     ag_diag(2, 3)
@@ -832,56 +904,134 @@
     def rs_send(g, number, src, dst, device):
         send("rs", src, dst, rs_s.at[g, number], rs_r.at[g, number], device)
 
+    def rs_send_if(which, g, number, src, dst, device, slot):
+        send_if(which, "rs", src, dst, rf_s.at[g, number], slot, device)
+
     def rs_wait(g, number, dst, device):
         copy(dst, dst, rs_s.at[g, number], rs_r.at[g, number], device).wait_recv()
 
-    top, low_half = pl.ds(0, CUT), pl.ds(CUT, PIECE - CUT)
+    def rs_rows(g, part):
+        strip, one, two = RS_CUTS[g]
+        return pl.ds((0, strip, strip + one, strip)[part], (strip, one, two, one + two)[part])
+
+    def rs_part(g, part):
+        _, one, two = RS_CUTS[g]
+        return pl.ds((0, 0, one, 0)[part], (0, one, two, one + two)[part])
 
     def rs_first(g):
-        rs_send(g, 0, wts.at[g, nx, :, ny, top], rdx.at[g], to_x)
-        rs_send(g, 1, wts.at[g, nx, :, ny, low_half], rdy.at[g], to_y)
-        rs_send(g, 2, wts.at[g, nx, :, y, top], rxx.at[g, :, top], to_x)
+        one, two = rs_part(g, 1), rs_part(g, 2)
+        rs_send(g, 0, wts.at[g, nx, :, ny, rs_rows(g, 1)], rdx.at[g, :, one], to_x)
+        rs_send(g, 1, wts.at[g, nx, :, ny, rs_rows(g, 2)], rdy.at[g, :, pl.ds(0, RS_CUTS[g][2])], to_y)
+        rs_send(g, 2, wts.at[g, nx, :, y, rs_rows(g, 1)], rxx.at[g, :, one], to_x)
 
     def rs_second(g):
-        rs_send(g, 3, wts.at[g, x, :, ny, low_half], ryy.at[g, :, low_half], to_y)
+        rs_send(g, 3, wts.at[g, x, :, ny, rs_rows(g, 2)], ryy.at[g, :, rs_part(g, 2)], to_y)
 
     def rs_third(g):
-        rs_wait(g, 0, rdx.at[g], to_x)
+        one, two = rs_part(g, 1), rs_part(g, 2)
+        far = pl.ds(0, RS_CUTS[g][2])
+        rs_wait(g, 0, rdx.at[g, :, one], to_x)
 
         def add_x(i):
-            wts[g, x, i, ny, top] = (wts[g, x, i, ny, top].astype(F32) + rdx[g, i].astype(F32)).astype(BF)
+            here = rs_rows(g, 1)
+            wts[g, x, i, ny, here] = (wts[g, x, i, ny, here].astype(F32) + rdx[g, i, one].astype(F32)).astype(BF)
 
         loop(4, add_x)
-        rs_send(g, 4, wts.at[g, x, :, ny, top], ryy.at[g, :, top], to_y)
-        rs_wait(g, 1, rdy.at[g], to_y)
+        rs_send(g, 4, wts.at[g, x, :, ny, rs_rows(g, 1)], ryy.at[g, :, one], to_y)
+        rs_wait(g, 1, rdy.at[g, :, far], to_y)
 
         def add_y(i):
-            wts[g, nx, i, y, low_half] = (
-                wts[g, nx, i, y, low_half].astype(F32) + rdy[g, i].astype(F32)
-            ).astype(BF)
+            here = rs_rows(g, 2)
+            wts[g, nx, i, y, here] = (wts[g, nx, i, y, here].astype(F32) + rdy[g, i, far].astype(F32)).astype(BF)
 
         loop(4, add_y)
-        rs_send(g, 5, wts.at[g, nx, :, y, low_half], rxx.at[g, :, low_half], to_x)
+        rs_send(g, 5, wts.at[g, nx, :, y, rs_rows(g, 2)], rxx.at[g, :, two], to_x)
 
     def plane(g, zz):
-        return wts[g, x, zz, y].astype(F32) + rxx[g, zz].astype(F32) + ryy[g, zz].astype(F32)
+        rest, here = rs_rows(g, 3), rs_part(g, 3)
+        return wts[g, x, zz, y, rest].astype(F32) + rxx[g, zz, here].astype(F32) + ryy[g, zz, here].astype(F32)
 
     def rs_fourth(g):
-        rs_wait(g, 2, rxx.at[g, :, top], to_x)
-        rs_wait(g, 3, ryy.at[g, :, low_half], to_y)
-        rs_wait(g, 4, ryy.at[g, :, top], to_y)
-        rs_wait(g, 5, rxx.at[g, :, low_half], to_x)
-        for k in (1, 2, 3):
-            wts[g, x, zf[k], y] = plane(g, zf[k]).astype(BF)
-            rs_send(g, 5 + k, wts.at[g, x, zf[k], y], rzz.at[g, k - 1], to_z[k])
+        one, two, both, rest = rs_part(g, 1), rs_part(g, 2), rs_part(g, 3), rs_rows(g, 3)
+        rs_wait(g, 2, rxx.at[g, :, one], to_x)
+        rs_wait(g, 3, ryy.at[g, :, two], to_y)
+        rs_wait(g, 4, ryy.at[g, :, one], to_y)
+        rs_wait(g, 5, rxx.at[g, :, two], to_x)
+        for k in (2, 3):
+            wts[g, x, zk[k], y, rest] = plane(g, zk[k]).astype(BF)
+            rs_send_if(
+                1, g, k - 2, wts.at[g, x, zk[k], y, rest], rzf.at[g, k - 2, both], to_zk[1], rf_r.at[g, k - 2]
+            )
+        wts[g, x, zk[1], y, rest] = plane(g, zk[1]).astype(BF)
+        rs_send(g, 6, wts.at[g, x, zk[1], y, rest], rz.at[g, 0, both], to_zk[1])
+
+    def rs_fifth(g):
+        both, rest = rs_part(g, 3), rs_rows(g, 3)
+
+        @pl.when(outer == 0)
+        def _():
+            for k in (2, 3):
+                copy(
+                    rzf.at[g, k - 2, both], rzf.at[g, k - 2, both], rf_s.at[g, 0], rf_r.at[g, k - 2], to_zk[1]
+                ).wait_recv()
+                wts[g, x, zk[k], y, rest] = (
+                    wts[g, x, zk[k], y, rest].astype(F32) + rzf[g, k - 2, both].astype(F32)
+                ).astype(BF)
+
+        for k in (2, 3):
+            rs_send_if(
+                0, g, k, wts.at[g, x, zk[k], y, rest], rz.at[g, 1, both], to_zk[k], rs_r.at[g, 7]
+            )
+
+    def strips(g, zz):
+        return wts.at[g, :, zz, :, pl.ds(0, RS_CUTS[g][0])]
+
+    def rs_strip_z(g):
+        here = pl.ds(0, RS_CUTS[g][0])
+        for k in (2, 3):
+            rs_send_if(1, g, 2 + k, strips(g, zk[k]), rzf2.at[g, k - 2, :, :, here], to_zk[1], rf_r.at[g, k])
+        rs_send(g, 8, strips(g, zk[1]), rz2.at[g, 0, :, :, here], to_zk[1])
+
+    def rs_strip_fwd(g):
+        here = pl.ds(0, RS_CUTS[g][0])
+
+        @pl.when(outer == 0)
+        def _():
+            for k in (2, 3):
+                held = rzf2.at[g, k - 2, :, :, here]
+                copy(held, held, rf_s.at[g, 0], rf_r.at[g, k], to_zk[1]).wait_recv()
+                wts[g, :, zk[k], :, here] = (
+                    wts[g, :, zk[k], :, here].astype(F32) + rzf2[g, k - 2, :, :, here].astype(F32)
+                ).astype(BF)
+
+        for k in (2, 3):
+            rs_send_if(0, g, 4 + k, strips(g, zk[k]), rz2.at[g, 1, :, :, here], to_zk[k], rs_r.at[g, 9])
+
+    def rs_strip_xy(g):
+        here = pl.ds(0, RS_CUTS[g][0])
+        for k in (0, 1):
+            rs_wait(g, 8 + k, rz2.at[g, k, :, :, here], to_zk[1 + k])
+        wts[g, :, z, :, here] = (
+            wts[g, :, z, :, here].astype(F32)
+            + rz2[g, 0, :, :, here].astype(F32)
+            + rz2[g, 1, :, :, here].astype(F32)
+        ).astype(BF)
+        for i, (xx, yy, device) in enumerate(((nx, y, to_x), (x, ny, to_y), (nx, ny, to_xy))):
+            rs_send(g, 10 + i, wts.at[g, xx, z, yy, here], rst.at[g, i, here], device)
 
     def rs_total(g):
-        for k in (1, 2, 3):
-            rs_wait(g, 5 + k, rzz.at[g, k - 1], to_z[k])
+        here, both = pl.ds(0, RS_CUTS[g][0]), rs_part(g, 3)
+        for k in (0, 1):
+            rs_wait(g, 6 + k, rz.at[g, k, both], to_zk[1 + k])
+        for i, device in enumerate((to_x, to_y, to_xy)):
+            rs_wait(g, 10 + i, rst.at[g, i, here], device)
+        strip = wts[g, x, z, y, here].astype(F32)
+        for i in range(3):
+            strip = strip + rst[g, i, here].astype(F32)
         total = plane(g, z)
-        for k in range(3):
-            total = total + rzz[g, k].astype(F32)
-        return total
+        for k in range(2):
+            total = total + rz[g, k, both].astype(F32)
+        return jnp.concatenate([strip, total], axis=0)
 
     def ff_grad(g, turned, held, xx):
         def body(j):
@@ -897,6 +1047,7 @@
     rs_first(2)
     ff_grad(2, rowt, aq, x)
     rs_second(2)
+    rs_strip_z(2)
 
     for xx in range(2):
 
@@ -914,6 +1065,7 @@
     rs_first(1)
     ff_grad(1, hqt, gu, x)
     rs_second(1)
+    rs_strip_z(1)
 
     def up_part(start, held):
         def body(n):
@@ -968,7 +1120,7 @@
         for e in range(2):
             feats = slice(p * 128 + e * 64, p * 128 + e * 64 + 64)
             dsum[p * 2 + e : p * 2 + e + 1, :] = sum_rows(gct[feats, :].astype(F32) * ctxt[feats, :])
-    rs_third(1)
+    rs_strip_fwd(2)
 
     row_half = lax.broadcasted_iota(jnp.int32, (128, 1), 0) // 64
 
@@ -998,8 +1150,8 @@
 
     attend_back(0)
     attend_back(1)
-    rs_fourth(2)
     attend_back(2)
+    rs_third(1)
     for j, part in ((0, 0), (2, HERE)):
         tot[0, 8:9, part : part + HERE] = sum_rows(grads[:, j * HERE : (j + 1) * HERE].astype(F32))
 
@@ -1022,8 +1174,18 @@
             put(1, t, jnp.where(left_two, pltpu.roll(one, 64, 1), two))
 
     loop(4, head_grad)
+
+    def most_x(i):
+        v = jnp.abs(tok[pl.ds(mul8(base + i * 128, 128), 128), :].astype(F32))
+        tot[0, 9:10, :] = jnp.maximum(tot[0, 9:10, :], jnp.max(v, axis=0, keepdims=True))
+
+    loop(4, most_x)
+    row_of = lax.broadcasted_iota(jnp.int32, (16, 1), 0)
+    small = copy(tot.at[0], tot_c, tt_s.at[0], tt_r.at[0], to_c)
+    small.start()
     rs_first(0)
     rs_second(0)
+    rs_strip_z(0)
 
     def token_part(start, held):
         def body(n):
@@ -1035,17 +1197,16 @@
     token_part(theirs, exb_s)
     ex4 = copy(exb_s, exb_r, ex_s.at[6], ex_r.at[6], to_c)
     ex4.start()
+    small.wait()
+    mixed = jnp.where(row_of < 6, tot[0] + tot_c[...], jnp.maximum(tot[0], tot_c[...]))
+    tot[1] = jnp.where((row_of >= 6) & (row_of < 9), tot[0], mixed)
+    small = copy(tot.at[1], tot_x, tt_s.at[1], tt_r.at[1], to_x)
+    small.start()
     token_part(mine, r1)
-    rs_fourth(1)
-
-    def most_x(i):
-        v = jnp.abs(tok[pl.ds(mul8(base + i * 128, 128), 128), :].astype(F32))
-        tot[0, 9:10, :] = jnp.maximum(tot[0, 9:10, :], jnp.max(v, axis=0, keepdims=True))
-
-    loop(4, most_x)
-    row_of = lax.broadcasted_iota(jnp.int32, (16, 1), 0)
-    small = copy(tot.at[0], tot_c, tt_s.at[0], tt_r.at[0], to_c)
-    small.start()
+    rs_fourth(2)
+    rs_strip_fwd(1)
+    rs_strip_xy(2)
+    rs_fifth(2)
     ex4.wait()
 
     def token_grad(i):
@@ -1056,21 +1217,19 @@
         o_tok[pl.ds(mul8(mp * OWN + i * 64, 64), 64), :] = got.astype(BF)
 
     loop(4, token_grad)
+    rs_third(0)
     own = o_tok.at[pl.ds(mul8(mp * OWN, OWN), OWN)]
+    send("tok", own, own, gx_s.at[1], gx_r.at[1], to_c)
     send("tok", own, own, gx_s.at[0], gx_r.at[0], to_x)
-    send("tok", own, own, gx_s.at[1], gx_r.at[1], to_c)
-
-    small.wait()
-    mixed = jnp.where(row_of < 6, tot[0] + tot_c[...], jnp.maximum(tot[0], tot_c[...]))
-    tot[1] = jnp.where((row_of >= 6) & (row_of < 9), tot[0], mixed)
-    small = copy(tot.at[1], tot_x, tt_s.at[1], tt_r.at[1], to_x)
-    small.start()
-    rs_third(0)
+    rs_strip_fwd(0)
     small.wait()
     tot[2] = jnp.where(row_of < 9, tot[1] + tot_x[...], jnp.maximum(tot[1], tot_x[...]))
     small = copy(tot.at[2], tot_y, tt_s.at[2], tt_r.at[2], to_y)
     small.start()
-    o_up[...] = rs_total(1) * _slope(w_up[...], w_inv[2])
+    rs_fourth(1)
+    rs_strip_xy(1)
+    rs_fifth(1)
+    rs_strip_xy(0)
     small.wait()
     tot[3] = jnp.where(row_of < 9, tot[2] + tot_y[...], jnp.maximum(tot[2], tot_y[...]))
     smalls = []
@@ -1078,8 +1237,10 @@
         made = copy(tot.at[3], tot_z.at[k - 1], tt_s.at[2 + k], tt_r.at[2 + k], to_z[k])
         made.start()
         smalls.append(made)
-    o_down[...] = rs_total(2).T * _slope(w_down[...], w_inv[3])
+    o_down[...] = rs_total(2) * _slope(w_down[...], w_inv[3])
     rs_fourth(0)
+    rs_fifth(0)
+    o_up[...] = rs_total(1) * _slope(w_up[...], w_inv[2])
 
     far = o_tok.at[pl.ds(mul8((nx * 2 + c) * OWN, OWN), OWN)]
     copy(far, far, gx_s.at[0], gx_r.at[0], to_x).wait_recv()
@@ -1100,7 +1261,7 @@
         row = jnp.broadcast_to(done[8:9, j * HERE : (j + 1) * HERE], (8, HERE))
         pair = jnp.where(x == 0, row[:, 0:128], row[:, 128:256])
         for h, tile, shift in ((0, pair, 0), (1, pair, 64), (2, row[:, 256:384], 64 * x)):
-            o_bqv[j, h : h + 1, :] = pltpu.roll(tile, (256 - shift - dp * 8) % 128, 1)[0:1, 0:8]
+            o_bqv[h, j : j + 1, :] = pltpu.roll(tile, (256 - shift - dp * 8) % 128, 1)[0:1, 0:8]
     for i in range(4):
         o_rng[i] = 0.9 * range_of[i] + 0.1 * jnp.max(done[9 + i : 10 + i, :])
 
@@ -1147,11 +1308,15 @@
         buffer(2, 2, WIDE, WIDE),
         buffer(WIDE, 3 * HERE),
         buffer(WIDE, HERE),
-        buffer(3, 4, CUT, WIDE),
-        buffer(3, 4, PIECE - CUT, WIDE),
-        buffer(3, 4, PIECE, WIDE),
-        buffer(3, 4, PIECE, WIDE),
-        buffer(3, 3, PIECE, WIDE),
+        buffer(3, 4, 48, WIDE),
+        buffer(3, 4, 32, WIDE),
+        buffer(3, 4, 80, WIDE),
+        buffer(3, 4, 80, WIDE),
+        buffer(3, 2, 80, WIDE),
+        buffer(3, 2, 80, WIDE),
+        buffer(3, 2, 2, 2, 32, WIDE),
+        buffer(3, 2, 2, 2, 32, WIDE),
+        buffer(3, 3, 32, WIDE),
         f32(2, 4, 2, 16, 128),
         f32(16, 128),
         f32(16, WIDE),
@@ -1197,6 +1362,12 @@
         f32(16, WIDE),
         f32(16, WIDE),
         f32(3, 16, WIDE),
+        sems((3, 2)),
+        sems((3, 2)),
+        sems((3, 3)),
+        sems((3, 2)),
+        sems((3, 2)),
+        sems((3, 3)),
         sems((3, 3)),
         sems((3, 3)),
         sems((3, 4)),
@@ -1207,8 +1378,10 @@
         sems((3, 4)),
         sems((3, 4)),
         sems((3, 4)),
-        sems((3, 9)),
-        sems((3, 9)),
+        sems((3, 13)),
+        sems((3, 13)),
+        sems((3, 8)),
+        sems((3, 4)),
         sems((6,)),
         sems((6,)),
         sems((7,)),
@@ -1229,8 +1402,8 @@
             shape(w_qkv.shape, F32),
             shape(w_out.shape, F32),
             shape(w_up.shape, F32),
-            shape(w_down.shape, F32),
-            shape(b_qv.shape, F32),
+            shape(w_down.shape[::-1], F32),
+            shape((b_qv.shape[1], b_qv.shape[0], b_qv.shape[2]), F32),
             shape(b_up.shape, F32),
             shape(vectors.shape, F32),
             shape(ema_ranges.shape, F32),
@@ -1247,8 +1420,8 @@
         w_qkv,
         w_out,
         w_up,
-        w_down,
-        b_qv,
+        w_down.T,
+        b_qv.transpose(1, 0, 2),
         b_up,
         vectors,
         ema_ranges,
@@ -1256,7 +1429,45 @@
         long_rows,
         grad_out,
     )
-    return (outs[0], outs[1].astype(F32), *outs[2:])
+    outs = finish(outs)
+    return (*outs[:5], outs[5].T, outs[6].transpose(1, 0, 2), *outs[7:])
+
+
+def finish_kernel(*refs):
+    ins, outs, held, wide, sem = refs[:10], refs[10:20], refs[20:29], refs[29], refs[30]
+    parts = [pl.ds(i * OWN, OWN) for i in range(ins[1].shape[0] // OWN)]
+    arriving = [pltpu.make_async_copy(ins[1].at[p], held[1].at[p], sem.at[9 + i]) for i, p in enumerate(parts)]
+    moved = [i for i in range(9) if i != 1]
+    arriving += [pltpu.make_async_copy(ins[i], held[i], sem.at[i]) for i in moved]
+    leaving = [pltpu.make_async_copy(wide.at[p], outs[1].at[p], sem.at[9 + i]) for i, p in enumerate(parts)]
+    leaving += [pltpu.make_async_copy(held[i], outs[i], sem.at[i]) for i in moved]
+    for made in arriving:
+        made.start()
+    for i in range(4):
+        outs[9][i] = ins[9][i]
+    for i, (here, there) in enumerate(zip(arriving, leaving)):
+        here.wait()
+        if i < len(parts):
+            wide[parts[i], :] = held[1][parts[i], :].astype(F32)
+        there.start()
+    for made in leaving:
+        made.wait()
+
+
+def finish(held):
+    shape = jax.ShapeDtypeStruct
+    far = pl.BlockSpec(memory_space=pltpu.HBM)
+    scalars = pl.BlockSpec(memory_space=pltpu.SMEM)
+    return pl.pallas_call(
+        finish_kernel,
+        out_shape=[shape(v.shape, F32 if i == 1 else v.dtype) for i, v in enumerate(held)],
+        in_specs=[far] * 9 + [scalars],
+        out_specs=[far] * 9 + [scalars],
+        scratch_shapes=[pltpu.VMEM(v.shape, v.dtype) for v in held[:9]]
+        + [pltpu.VMEM(held[1].shape, F32), pltpu.SemaphoreType.DMA((9 + held[1].shape[0] // OWN,))],
+        compiler_params=pltpu.CompilerParams(vmem_limit_bytes=VMEM_LIMIT),
+        name="write_results",
+    )(*held)
 
 
 VMEM_LIMIT = 64 * 1024 * 1024

time: 181 us -> 153 us (0.85)
  Pallas kernels: 166 us -> 152 us
  local copies, waits for them, and re-layouts: 10.6 us -> 0 us
  other arithmetic: 3.38 us -> 0 us
    pallas_call x1, Pallas kernels: 166 us -> 148 us  [layer_on_chips(): pl.pallas_call(layer_kernel, out_shape=[shape(grad_out.shape, BF), shape(...]
    unnamed x25 -> x0, local copies, waits for them, and re-layouts: 10.6 us -> none
    pallas_call x0 -> x1, Pallas kernels: none -> 4.46 us  [finish(): pl.pallas_call(finish_kernel, out_shape=[shape(v.shape, F32 if i == 1 els...]
    convert_element_type x1 -> x0, other arithmetic: 3.38 us -> none  [layer_on_chips(): return (outs[0], outs[1].astype(F32), *outs[2:])]
where the time goes in v2:
time: 153 us
  Pallas kernels  152 us (99%)
    pallas_call x1, Pallas kernels, layer_on_chips(): pl.pallas_call(layer_kernel, out_shape=[shape(grad_out.shape, BF), shape(...  148 us
    pallas_call x1, Pallas kernels, finish(): pl.pallas_call(finish_kernel, out_shape=[shape(v.shape, F32 if i == 1 els...  4.46 us

profile of v2, /device:TPU:0, one launch (start us, length us, event | category | flops | bytes accessed | tf_op | source)
XLA Modules:
  0.0 152.9 jit_solution(18250707607144932091)
XLA Ops:
  0.6 147.6 %encoder_layer.1 = (bf16[256,768]{1,0:T(8,128)(2,1)}, bf16[1024,768]{1,0:T(8,128)(2,1)}, f32[3,96,192]{2,1,0:T(8,128)}, f32[192,96]{1,0:T(8,128)}, f32[96,768]{1...) custom-call(bf16[1024,768]{1,0:T(8,128)(2,1)} %tok.1, ...), custom_call_target="tpu_custom_call" | custom-call | tf_op jit(solution)/shard_map/encoder_layer/pallas_call | solution.py:1397
  148.3 4.5 %write_results.1 = (bf16[256,768]{1,0:T(8,128)(2,1)}, f32[1024,768]{1,0:T(8,128)}, f32[3,96,192]{2,1,0:T(8,128)}, f32[192,96]{1,0:T(8,128)}, f32[96,768]{1,0:T(8...) custom-call(bf16[256,768]{1,0:T(8,128)(2,1)} %get-tuple-element.30.refs_0_,, ...), custom_call_target="tpu_custom_call" | custom-call | tf_op jit(solution)/shard_map/write_results/pallas_call | solution.py:1461

commit v3 on v2

--- a/solution.py
+++ b/solution.py
@@ -308,8 +308,8 @@
 MESH = pl.DeviceIdType.MESH
 WIDE = 768
 PIECE = 96
-AG_CUTS = ((16, 32, 48), (16, 48, 32), (16, 32, 48))
-RS_CUTS = ((16, 48, 32), (32, 32, 32), (32, 32, 32))
+AG_CUTS = ((0, 48, 48), (16, 32, 48), (32, 32, 32))
+RS_CUTS = ((16, 32, 48), (16, 32, 48), (32, 32, 32))
 OWN = 256
 HERE = 384
 
@@ -335,6 +335,28 @@
 
 
 def layer_kernel(
+    h_tok,
+    h_qkv,
+    h_out,
+    h_up,
+    h_down,
+    h_bqv,
+    h_bup,
+    h_vec,
+    ranges,
+    h_mask,
+    long_rows,
+    h_grad,
+    r_layer,
+    r_tok,
+    r_qkv,
+    r_out,
+    r_up,
+    r_down,
+    r_bqv,
+    r_bup,
+    r_vec,
+    o_rng,
     tok,
     w_qkv,
     w_out,
@@ -343,9 +365,7 @@
     b_qv,
     b_up,
     vectors,
-    ranges,
     mask,
-    long_rows,
     grad_out,
     o_layer,
     o_tok,
@@ -356,7 +376,6 @@
     o_bqv,
     o_bup,
     o_vec,
-    o_rng,
     wts,
     wff,
     wc,
@@ -443,6 +462,8 @@
     tt_r,
     gx_s,
     gx_r,
+    in_s,
+    out_s,
 ):
     dp = lax.axis_index("dp")
     mp = lax.axis_index("mp")
@@ -484,12 +505,41 @@
             else:
                 pl.when(outer == which)(made.wait_send)
 
+    base = mul8(x * 512, 512)
+    arriving = [
+        pltpu.make_async_copy(there, here, in_s.at[i])
+        for i, (there, here) in enumerate(
+            (
+                (h_up, w_up),
+                (h_down, w_down),
+                (h_qkv, w_qkv),
+                (h_out, w_out),
+                (h_vec, vectors),
+                (h_bup, b_up),
+                (h_bqv, b_qv),
+                (h_tok.at[pl.ds(base, 512)], tok),
+                (h_mask, mask),
+                (h_grad, grad_out),
+            )
+        )
+    ]
+    for made in arriving:
+        made.start()
+    leaving = []
+
+    def leave(here, there):
+        made = pltpu.make_async_copy(here, there, out_s.at[len(leaving)])
+        made.start()
+        leaving.append(made)
+
     range_of = [ranges[i] for i in range(4)]
     inv_of = [1.0 / r for r in range_of]
 
     barrier = pltpu.get_barrier_semaphore()
     for device in (to_c, to_x, to_y, to_xy, *to_z[1:]):
         pl.semaphore_signal(barrier, inc=1, device_id=device, device_id_type=MESH)
+    for made in arriving[:7]:
+        made.wait()
     wts[1, x, z, y] = w_up[...]
     wts[2, x, z, y] = w_down[...]
     turned = w_out[...].T
@@ -535,23 +585,45 @@
         send(("ag", g), own, own, z2s.at[g, 0], z2r.at[g, 0], to_zk[1])
         send(("ag", g), own, own, z2s.at[g, 1], z2r.at[g, 1 + outer], to_zk[2])
 
-    def ag_strip_got(g, k):
-        got = ag_strips(g, zk[k])
-        copy(got, got, z2s.at[g, 0], z2r.at[g, k - 1], to_zk[k]).wait_recv()
-        if k > 1:
+    def ag_strip_fwd(g):
+        @pl.when(outer == 0)
+        def _():
+            for k in (2, 3):
+                got = ag_strips(g, zk[k])
+                copy(got, got, z2s.at[g, 0], z2r.at[g, k - 1], to_zk[k]).wait_recv()
+
+        for k in (2, 3):
+            got = ag_strips(g, zk[k])
             send_if(0, ("ag", g), got, got, z2f.at[g, k - 2], z2r.at[g, k - 1], to_zk[1])
+
+    def ag_strip_got(g):
+        got = ag_strips(g, zk[1])
+        copy(got, got, z2s.at[g, 0], z2r.at[g, 0], to_zk[1]).wait_recv()
+
+        @pl.when(outer == 1)
+        def _():
+            for k in (2, 3):
+                got = ag_strips(g, zk[k])
+                copy(got, got, z2s.at[g, 0], z2r.at[g, k - 1], to_zk[1]).wait_recv()
 
     def ag_z_send(g):
         own = ag_rows(g, x, z, y, 3)
         send(("ag", g), own, own, zs.at[g, 0], zr.at[g, 0], to_zk[1])
         send(("ag", g), own, own, zs.at[g, 1], zr.at[g, 1 + outer], to_zk[2])
 
+    def ag_z_fwd(g, k):
+        got = ag_rows(g, x, zk[k], y, 3)
+        pl.when(outer == 0)(copy(got, got, zs.at[g, 0], zr.at[g, k - 1], to_zk[k]).wait_recv)
+        send_if(0, ("ag", g), got, got, zf.at[g, k - 2], zr.at[g, k - 1], to_zk[1])
+
     def ag_xy_send(g, k):
         own = ag_rows(g, x, zk[k], y, 3)
         if k > 0:
-            copy(own, own, zs.at[g, 0], zr.at[g, k - 1], to_zk[k]).wait_recv()
+            arrived = copy(own, own, zs.at[g, 0], zr.at[g, k - 1], to_zk[1]).wait_recv
             if k > 1:
-                send_if(0, ("ag", g), own, own, zf.at[g, k - 2], zr.at[g, k - 1], to_zk[1])
+                pl.when(outer == 1)(arrived)
+            else:
+                arrived()
         send(("ag", g), own, own, xs.at[g, k], xr.at[g, k], to_x)
         send(("ag", g), own, own, ys.at[g, k], yr.at[g, k], to_y)
 
@@ -573,35 +645,38 @@
 
     small_c = copy(sm.at[x, z, y], smc, sm_s.at[0], sm_r.at[0], to_c)
     small_c.start()
-    ag_strip_xy(0)
     ag_z_send(0)
     ag_xy_send(0, 0)
-
-    base = mul8(x * 512, 512)
-
-    def do_tokens(i):
-        rows = pl.ds(mul8(i * 128, 128), 128)
-        v = tok[pl.ds(mul8(base + i * 128, 128), 128), :].astype(F32)
-        xq[rows, :] = (range_of[0] * jnp.tanh(v * inv_of[0])).astype(BF)
-
-    loop(4, do_tokens)
     small_c.wait()
     sm[x, z, y, 15:16] = jnp.maximum(sm[x, z, y, 15:16], smc[15:16])
     small_x = copy(sm.at[x, z, y], sm.at[x, z, y], sm_s.at[1], sm_r.at[1], to_x)
     small_x.start()
-    ag_strip_z(0)
-    ag_xy_send(0, 1)
+    ag_strip_xy(1)
+    ag_xy_send(1, 0)
+
+    for made in arriving[7:]:
+        made.wait()
+
+    def do_tokens(i):
+        rows = pl.ds(mul8(i * 128, 128), 128)
+        v = tok[pl.ds(mul8(i * 128, 128), 128), :].astype(F32)
+        xq[rows, :] = (range_of[0] * jnp.tanh(v * inv_of[0])).astype(BF)
+
+    loop(4, do_tokens)
+    copy(sm.at[nx, z, y], sm.at[nx, z, y], sm_s.at[1], sm_r.at[1], to_x).wait_recv()
+    small_y = copy(sm.at[:, z, y], sm.at[:, z, y], sm_s.at[2], sm_r.at[2], to_y)
+    small_y.start()
+    ag_strip_xy(2)
+    ag_xy_send(2, 0)
+    ag_z_send(1)
 
     def do_turn(j):
         cols = pl.ds(mul8(j * 128, 128), 128)
         xqt[cols, :] = xq[:, cols].T
 
     loop(6, do_turn)
-    copy(sm.at[nx, z, y], sm.at[nx, z, y], sm_s.at[1], sm_r.at[1], to_x).wait_recv()
-    small_y = copy(sm.at[:, z, y], sm.at[:, z, y], sm_s.at[2], sm_r.at[2], to_y)
-    small_y.start()
-    ag_diag(0, 0)
-    ag_xy_send(0, 2)
+    ag_xy_send(0, 1)
+    ag_z_fwd(0, 2)
 
     long_flag = long_rows[x].astype(F32)
     for r in range(4):
@@ -617,15 +692,16 @@
         made = copy(sm.at[:, z], sm.at[:, z], sm_s.at[2 + k], sm_r.at[2 + k], to_z[k])
         made.start()
         small_z.append(made)
+    ag_z_fwd(0, 3)
+    ag_xy_send(0, 2)
+    ag_strip_z(1)
+    ag_xy_send(0, 3)
+    ag_diag(0, 0)
     ag_diag(0, 1)
-    ag_xy_send(0, 3)
-    ag_strip_xy(1)
-    ag_z_send(1)
-    for k in (1, 2, 3):
-        ag_strip_got(0, k)
+    ag_z_send(2)
+    ag_xy_send(1, 1)
+    ag_z_fwd(1, 2)
     ag_diag(0, 2)
-    ag_xy_send(1, 0)
-    ag_diag(0, 3)
     for k in (1, 2, 3):
         copy(sm.at[:, from_z[k]], sm.at[:, from_z[k]], sm_s.at[2 + k], sm_r.at[2 + k], to_z[k]).wait_recv()
     small_x.wait_send()
@@ -663,8 +739,10 @@
             )
         bqv[j : j + 1, 256:384] = heads[0][0][first + 2 : first + 3] + heads[1][1][first + 2 : first + 3]
 
-    ag_xy_send(1, 1)
-    ag_strip_z(1)
+    ag_z_fwd(1, 3)
+    ag_strip_z(2)
+    ag_strip_fwd(1)
+    ag_diag(0, 3)
     for k in range(4):
         ag_last(0, k)
 
@@ -698,6 +776,7 @@
 
     loop(8, squash_heads)
     ag_xy_send(1, 2)
+    ag_xy_send(1, 3)
 
     def squash_ff(g, xx):
         def body(place):
@@ -710,24 +789,21 @@
 
     for j, held in enumerate((qs, ks, vs)):
 
-        def project(i, j=j, held=held):
-            rows = pl.ds(mul8(i * 256, 256), 256)
-            got = nn(xq[rows, :], wc[:, j * HERE : (j + 1) * HERE])
-            if j == 0:
-                got = (got + bqv[0:1, :]) * 0.125
-            elif j == 2:
-                got = got + bqv[1:2, :]
-            held[rows, :] = got.astype(BF)
-
-        loop(2, project)
-    ag_xy_send(1, 3)
-    ag_strip_xy(2)
-    ag_z_send(2)
+        got = nn(xq[...], wc[:, j * HERE : (j + 1) * HERE])
+        if j == 0:
+            got = (got + bqv[0:1, :]) * 0.125
+        elif j == 2:
+            got = got + bqv[1:2, :]
+        held[...] = got.astype(BF)
+    ag_diag(1, 0)
+    ag_z_fwd(2, 2)
+    ag_z_fwd(2, 3)
     for p in range(3):
         cols = slice(p * 128, p * 128 + 128)
         kt[cols, :] = ks[:, cols].T
         vt[cols, :] = vs[:, cols].T
-    ag_diag(1, 0)
+    ag_diag(1, 1)
+    ag_xy_send(2, 1)
 
     half_of = lax.broadcasted_iota(jnp.int32, (1, 128), 1) // 64
 
@@ -745,15 +821,13 @@
                 ctxt[feats, n * 256 : n * 256 + 256] = nn(vt[feats, :], s)
 
     attend(0)
-    ag_diag(1, 1)
-    for k in (1, 2, 3):
-        ag_strip_got(1, k)
+    ag_xy_send(2, 2)
     attend(1)
-    ag_xy_send(2, 0)
-    ag_strip_z(2)
+    ag_diag(1, 2)
+    ag_strip_fwd(2)
     attend(2)
-    ag_diag(1, 2)
-    ag_xy_send(2, 1)
+    ag_xy_send(2, 3)
+    ag_diag(1, 3)
 
     for p in range(3):
         cols = slice(p * 128, p * 128 + 128)
@@ -763,20 +837,14 @@
     tot[0] = jnp.zeros((16, WIDE), F32)
     most = jnp.max(jnp.max(jnp.abs(ctxt[...]), axis=0, keepdims=True), axis=1, keepdims=True)
     tot[0, 10:11, :] = jnp.broadcast_to(most, (1, WIDE))
-    ag_diag(1, 3)
-    ag_xy_send(2, 2)
 
     def out_part(start, held):
-        def body(n):
-            cols = pl.ds(mul8(n * 256, 256), 256)
-            held[:, cols] = nt(cq[pl.ds(start, OWN), :], wo[cols, :])
-
-        loop(3, body)
+        held[...] = nt(cq[pl.ds(start, OWN), :], wo[...])
 
     out_part(theirs, exa_s)
     ex1 = copy(exa_s, exa_r, ex_s.at[0], ex_r.at[0], to_c)
     ex1.start()
-    ag_xy_send(2, 3)
+    ag_diag(2, 0)
     out_part(mine, r1)
     ex1.wait()
 
@@ -788,7 +856,7 @@
 
     def first_norm(i):
         rows = pl.ds(mul8(i * 64, 64), 64)
-        v = tok[pl.ds(mul8(base + mine + i * 64, 64), 64), :].astype(F32)
+        v = tok[pl.ds(mul8(mine + i * 64, 64), 64), :].astype(F32)
         v = v + (r1[rows, :] + exa_r[rows, :] + vec[0:1, :])
         r1[rows, :] = v
         center = v - mean_of(v)
@@ -815,54 +883,44 @@
         copy(other, other, ex_s.at[number], ex_r.at[number], to_c).wait_recv()
 
     def turn_rows(held, out, start):
-        def body(j):
-            cols = pl.ds(mul8(j * 128, 128), 128)
-            out[cols, pl.ds(start, OWN)] = held[pl.ds(start, OWN), cols].T
-
-        loop(6, body)
+        out[:, pl.ds(start, OWN)] = held[pl.ds(start, OWN), :].T
 
     share_rows(hq, 1)
-    for k in range(4):
-        ag_last(1, k)
-    squash_ff(1, 0)
-    squash_ff(1, 1)
-    ag_diag(2, 0)
+    ag_strip_got(1)
+    ag_diag(2, 1)
     got_rows(hq, 1)
     turn_rows(hq, hqt, 0)
     turn_rows(hq, hqt, OWN)
+    squash_ff(1, x)
 
     def expand(xx):
-        def body(j):
-            n, i = j // 2, j % 2
-            cols = pl.ds(mul8(n * 256, 256), 256)
-            wide = pl.ds(mul8(xx * WIDE + n * 256, 256), 256)
+        wide = pl.ds(mul8(xx * WIDE, WIDE), WIDE)
+
+        def body(i):
             rows = pl.ds(mul8(i * 256, 256), 256)
-            u = nn(hq[rows, :], wff[0, xx, :, cols]) + bup[xx : xx + 1, cols]
+            u = nn(hq[rows, :], wff[0, xx]) + bup[pl.ds(xx, 1), :]
             cdf = 0.5 * (1.0 + lax.erf(u * 0.7071067811865476))
             a = u * cdf
-            tot[0, 12:13, 0:256] = jnp.maximum(tot[0, 12:13, 0:256], jnp.max(jnp.abs(a), axis=0, keepdims=True))
+            tot[0, 12:13, :] = jnp.maximum(tot[0, 12:13, :], jnp.max(jnp.abs(a), axis=0, keepdims=True))
             bent = jnp.tanh(a * inv_of[3])
             aq[rows, wide] = (range_of[3] * bent).astype(BF)
             pdf = 0.3989422804014327 * jnp.exp(-0.5 * u * u)
             fac[rows, wide] = ((1.0 - bent * bent) * (cdf + u * pdf)).astype(fac.dtype)
 
-        loop(6, body)
-
-    expand(0)
-    ag_diag(2, 1)
-    for k in (1, 2, 3):
-        ag_strip_got(2, k)
-    expand(1)
+        loop(2, body)
+
+    expand(x)
     ag_diag(2, 2)
+    for k in range(4):
+        ag_last(1, k)
+    squash_ff(1, nx)
+    expand(nx)
     ag_diag(2, 3)
+    ag_strip_got(2)
 
     def down_part(start, held, xx, first):
-        def body(n):
-            cols = pl.ds(mul8(n * 256, 256), 256)
-            got = nt(aq[pl.ds(start, OWN), pl.ds(mul8(xx * WIDE, WIDE), WIDE)], wff[1, xx, cols, :])
-            held[:, cols] = got if first else held[:, cols] + got
-
-        loop(3, body)
+        got = nt(aq[pl.ds(start, OWN), pl.ds(mul8(xx * WIDE, WIDE), WIDE)], wff[1, xx])
+        held[...] = got if first else held[...] + got
 
     squash_ff(2, x)
     down_part(theirs, exb_s, x, True)
@@ -894,6 +952,7 @@
         gf[pl.ds(mul8(mine + i * 64, 64), 64), :] = low
 
     loop(4, second_norm)
+    leave(o_layer, r_layer)
     share_rows(gf, 3)
     turn_rows(gf, rowt, mine)
     for g in range(3):
@@ -918,18 +977,24 @@
         _, one, two = RS_CUTS[g]
         return pl.ds((0, 0, one, 0)[part], (0, one, two, one + two)[part])
 
-    def rs_first(g):
+    far_z, near_z = pl.ds(2 - z // 2 * 2, 2), pl.ds(z // 2 * 2, 2)
+
+    def rs_first(g, near):
         one, two = rs_part(g, 1), rs_part(g, 2)
         rs_send(g, 0, wts.at[g, nx, :, ny, rs_rows(g, 1)], rdx.at[g, :, one], to_x)
         rs_send(g, 1, wts.at[g, nx, :, ny, rs_rows(g, 2)], rdy.at[g, :, pl.ds(0, RS_CUTS[g][2])], to_y)
-        rs_send(g, 2, wts.at[g, nx, :, y, rs_rows(g, 1)], rxx.at[g, :, one], to_x)
-
-    def rs_second(g):
-        rs_send(g, 3, wts.at[g, x, :, ny, rs_rows(g, 2)], ryy.at[g, :, rs_part(g, 2)], to_y)
-
-    def rs_third(g):
+        rs_send(g, 2, wts.at[g, nx, far_z, y, rs_rows(g, 1)], rxx.at[g, far_z, one], to_x)
+        if near:
+            rs_send(g, 15, wts.at[g, nx, near_z, y, rs_rows(g, 1)], rxx.at[g, near_z, one], to_x)
+
+    def rs_second(g, near):
+        two = rs_part(g, 2)
+        rs_send(g, 3, wts.at[g, x, far_z, ny, rs_rows(g, 2)], ryy.at[g, far_z, two], to_y)
+        if near:
+            rs_send(g, 16, wts.at[g, x, near_z, ny, rs_rows(g, 2)], ryy.at[g, near_z, two], to_y)
+
+    def rs_third_x(g, near):
         one, two = rs_part(g, 1), rs_part(g, 2)
-        far = pl.ds(0, RS_CUTS[g][2])
         rs_wait(g, 0, rdx.at[g, :, one], to_x)
 
         def add_x(i):
@@ -937,7 +1002,14 @@
             wts[g, x, i, ny, here] = (wts[g, x, i, ny, here].astype(F32) + rdx[g, i, one].astype(F32)).astype(BF)
 
         loop(4, add_x)
-        rs_send(g, 4, wts.at[g, x, :, ny, rs_rows(g, 1)], ryy.at[g, :, one], to_y)
+        rs_send(g, 4, wts.at[g, x, far_z, ny, rs_rows(g, 1)], ryy.at[g, far_z, one], to_y)
+        rs_send(g, 13, wts.at[g, x, near_z, ny, rs_rows(g, 1)], ryy.at[g, near_z, one], to_y)
+        if not near:
+            rs_send(g, 16, wts.at[g, x, near_z, ny, rs_rows(g, 2)], ryy.at[g, near_z, two], to_y)
+
+    def rs_third_y(g, near):
+        one, two = rs_part(g, 1), rs_part(g, 2)
+        far = pl.ds(0, RS_CUTS[g][2])
         rs_wait(g, 1, rdy.at[g, :, far], to_y)
 
         def add_y(i):
@@ -945,7 +1017,10 @@
             wts[g, nx, i, y, here] = (wts[g, nx, i, y, here].astype(F32) + rdy[g, i, far].astype(F32)).astype(BF)
 
         loop(4, add_y)
-        rs_send(g, 5, wts.at[g, nx, :, y, rs_rows(g, 2)], rxx.at[g, :, two], to_x)
+        rs_send(g, 5, wts.at[g, nx, far_z, y, rs_rows(g, 2)], rxx.at[g, far_z, two], to_x)
+        rs_send(g, 14, wts.at[g, nx, near_z, y, rs_rows(g, 2)], rxx.at[g, near_z, two], to_x)
+        if not near:
+            rs_send(g, 15, wts.at[g, nx, near_z, y, rs_rows(g, 1)], rxx.at[g, near_z, one], to_x)
 
     def plane(g, zz):
         rest, here = rs_rows(g, 3), rs_part(g, 3)
@@ -953,58 +1028,60 @@
 
     def rs_fourth(g):
         one, two, both, rest = rs_part(g, 1), rs_part(g, 2), rs_part(g, 3), rs_rows(g, 3)
-        rs_wait(g, 2, rxx.at[g, :, one], to_x)
-        rs_wait(g, 3, ryy.at[g, :, two], to_y)
-        rs_wait(g, 4, ryy.at[g, :, one], to_y)
-        rs_wait(g, 5, rxx.at[g, :, two], to_x)
-        for k in (2, 3):
+        rs_wait(g, 2, rxx.at[g, far_z, one], to_x)
+        rs_wait(g, 3, ryy.at[g, far_z, two], to_y)
+        rs_wait(g, 4, ryy.at[g, far_z, one], to_y)
+        rs_wait(g, 5, rxx.at[g, far_z, two], to_x)
+        for k in (3, 2):
             wts[g, x, zk[k], y, rest] = plane(g, zk[k]).astype(BF)
             rs_send_if(
                 1, g, k - 2, wts.at[g, x, zk[k], y, rest], rzf.at[g, k - 2, both], to_zk[1], rf_r.at[g, k - 2]
             )
+
+    def rs_near(g):
+        one, two, both, rest = rs_part(g, 1), rs_part(g, 2), rs_part(g, 3), rs_rows(g, 3)
+        rs_wait(g, 13, ryy.at[g, near_z, one], to_y)
+        rs_wait(g, 14, rxx.at[g, near_z, two], to_x)
+        rs_wait(g, 15, rxx.at[g, near_z, one], to_x)
+        rs_wait(g, 16, ryy.at[g, near_z, two], to_y)
         wts[g, x, zk[1], y, rest] = plane(g, zk[1]).astype(BF)
         rs_send(g, 6, wts.at[g, x, zk[1], y, rest], rz.at[g, 0, both], to_zk[1])
 
     def rs_fifth(g):
         both, rest = rs_part(g, 3), rs_rows(g, 3)
-
-        @pl.when(outer == 0)
-        def _():
-            for k in (2, 3):
-                copy(
-                    rzf.at[g, k - 2, both], rzf.at[g, k - 2, both], rf_s.at[g, 0], rf_r.at[g, k - 2], to_zk[1]
-                ).wait_recv()
+        for k in (3, 2):
+
+            @pl.when(outer == 0)
+            def _(k=k):
+                held = rzf.at[g, k - 2, both]
+                copy(held, held, rf_s.at[g, 0], rf_r.at[g, k - 2], to_zk[1]).wait_recv()
                 wts[g, x, zk[k], y, rest] = (
                     wts[g, x, zk[k], y, rest].astype(F32) + rzf[g, k - 2, both].astype(F32)
                 ).astype(BF)
 
-        for k in (2, 3):
-            rs_send_if(
-                0, g, k, wts.at[g, x, zk[k], y, rest], rz.at[g, 1, both], to_zk[k], rs_r.at[g, 7]
-            )
+            rs_send_if(0, g, k, wts.at[g, x, zk[k], y, rest], rz.at[g, 1, both], to_zk[k], rs_r.at[g, 7])
 
     def strips(g, zz):
         return wts.at[g, :, zz, :, pl.ds(0, RS_CUTS[g][0])]
 
     def rs_strip_z(g):
         here = pl.ds(0, RS_CUTS[g][0])
-        for k in (2, 3):
+        for k in (3, 2):
             rs_send_if(1, g, 2 + k, strips(g, zk[k]), rzf2.at[g, k - 2, :, :, here], to_zk[1], rf_r.at[g, k])
         rs_send(g, 8, strips(g, zk[1]), rz2.at[g, 0, :, :, here], to_zk[1])
 
     def rs_strip_fwd(g):
         here = pl.ds(0, RS_CUTS[g][0])
-
-        @pl.when(outer == 0)
-        def _():
-            for k in (2, 3):
+        for k in (3, 2):
+
+            @pl.when(outer == 0)
+            def _(k=k):
                 held = rzf2.at[g, k - 2, :, :, here]
                 copy(held, held, rf_s.at[g, 0], rf_r.at[g, k], to_zk[1]).wait_recv()
                 wts[g, :, zk[k], :, here] = (
                     wts[g, :, zk[k], :, here].astype(F32) + rzf2[g, k - 2, :, :, here].astype(F32)
                 ).astype(BF)
 
-        for k in (2, 3):
             rs_send_if(0, g, 4 + k, strips(g, zk[k]), rz2.at[g, 1, :, :, here], to_zk[k], rs_r.at[g, 9])
 
     def rs_strip_xy(g):
@@ -1016,8 +1093,12 @@
             + rz2[g, 0, :, :, here].astype(F32)
             + rz2[g, 1, :, :, here].astype(F32)
         ).astype(BF)
-        for i, (xx, yy, device) in enumerate(((nx, y, to_x), (x, ny, to_y), (nx, ny, to_xy))):
-            rs_send(g, 10 + i, wts.at[g, xx, z, yy, here], rst.at[g, i, here], device)
+        rs_send(g, 10, wts.at[g, nx, z, y, here], rst.at[g, 0, here], to_x)
+        rs_send(g, 12, wts.at[g, nx, z, ny, here], rst.at[g, 2, here], to_xy)
+
+    def rs_strip_y(g):
+        here = pl.ds(0, RS_CUTS[g][0])
+        rs_send(g, 11, wts.at[g, x, z, ny, here], rst.at[g, 1, here], to_y)
 
     def rs_total(g):
         here, both = pl.ds(0, RS_CUTS[g][0]), rs_part(g, 3)
@@ -1034,53 +1115,41 @@
         return jnp.concatenate([strip, total], axis=0)
 
     def ff_grad(g, turned, held, xx):
-        def body(j):
-            n, i = j // 2, j % 2
-            cols = pl.ds(mul8(n * 256, 256), 256)
-            wide = pl.ds(mul8(xx * WIDE + n * 256, 256), 256)
-            got = nn(turned[pl.ds(mul8(i * HERE, HERE), HERE), :], held[:, wide])
-            wts[g, xx, pl.ds(i * 2, 2), :, :, cols] = got.reshape(2, 2, PIECE, 256).astype(BF)
-
-        loop(6, body)
+        got = nn(turned[...], held[:, pl.ds(mul8(xx * WIDE, WIDE), WIDE)])
+        wts[g, xx] = got.reshape(4, 2, PIECE, WIDE).astype(BF)
 
     ff_grad(2, rowt, aq, nx)
-    rs_first(2)
+    rs_first(2, True)
     ff_grad(2, rowt, aq, x)
-    rs_second(2)
+    rs_second(2, True)
     rs_strip_z(2)
 
     for xx in range(2):
 
-        def hidden_grad(j, xx=xx):
-            n, i = j // 2, j % 2
-            cols = pl.ds(mul8(n * 256, 256), 256)
-            wide = pl.ds(mul8(xx * WIDE + n * 256, 256), 256)
+        def hidden_grad(i, xx=xx):
+            wide = slice(xx * WIDE, xx * WIDE + WIDE)
             rows = pl.ds(mul8(i * 256, 256), 256)
-            got = (nn(gf[rows, :], wff[1, xx, :, cols]) * fac[rows, wide].astype(F32)).astype(BF)
+            got = (nn(gf[rows, :], wff[1, xx]) * fac[rows, wide].astype(F32)).astype(BF)
             gu[rows, wide] = got
-            tot[0, 6 + xx : 7 + xx, cols] += sum_rows(got.astype(F32))
-
-        loop(6, hidden_grad)
-    ff_grad(1, hqt, gu, nx)
-    rs_first(1)
-    ff_grad(1, hqt, gu, x)
-    rs_second(1)
-    rs_strip_z(1)
-
+            tot[0, 6 + xx : 7 + xx, :] += sum_rows(got.astype(F32))
+
+        loop(2, hidden_grad)
     def up_part(start, held):
-        def body(n):
-            cols = pl.ds(mul8(n * 256, 256), 256)
-            held[:, cols] = nt(gu[pl.ds(start, OWN), 0:WIDE], wff[0, 0, cols, :]) + nt(
-                gu[pl.ds(start, OWN), WIDE : 2 * WIDE], wff[0, 1, cols, :]
-            )
-
-        loop(3, body)
+        held[...] = nt(gu[pl.ds(start, OWN), 0:WIDE], wff[0, 0]) + nt(
+            gu[pl.ds(start, OWN), WIDE : 2 * WIDE], wff[0, 1]
+        )
 
     up_part(theirs, exa_s)
     ex3 = copy(exa_s, exa_r, ex_s.at[4], ex_r.at[4], to_c)
     ex3.start()
     up_part(mine, r1)
-    rs_third(2)
+    ff_grad(1, hqt, gu, nx)
+    rs_third_x(2, True)
+    rs_third_y(2, True)
+    rs_first(1, True)
+    ff_grad(1, hqt, gu, x)
+    rs_second(1, True)
+    rs_strip_z(1)
     ex3.wait()
 
     def first_back(i):
@@ -1103,24 +1172,14 @@
     got_rows(gf, 5)
     turn_rows(gf, rowt, theirs)
 
-    def out_grad(i):
-        rows = pl.ds(mul8(i * 256, 256), 256)
-        gwo[rows, :] = nn(rowt[rows, :], cq[...])
-
-    loop(3, out_grad)
-
-    def ctx_grad(i):
-        rows = pl.ds(mul8(i * 256, 256), 256)
-        gc[rows, :] = (nn(gf[rows, :], wo[...]) * slc[rows, :]).astype(BF)
-
-    loop(2, ctx_grad)
+    gwo[...] = nn(rowt[...], cq[...])
+    gc[...] = (nn(gf[...], wo[...]) * slc[...]).astype(BF)
     for p in range(3):
         cols = slice(p * 128, p * 128 + 128)
         gct[cols, :] = gc[:, cols].T
         for e in range(2):
             feats = slice(p * 128 + e * 64, p * 128 + e * 64 + 64)
             dsum[p * 2 + e : p * 2 + e + 1, :] = sum_rows(gct[feats, :].astype(F32) * ctxt[feats, :])
-    rs_strip_fwd(2)
 
     row_half = lax.broadcasted_iota(jnp.int32, (128, 1), 0) // 64
 
@@ -1151,85 +1210,85 @@
     attend_back(0)
     attend_back(1)
     attend_back(2)
-    rs_third(1)
+    rs_strip_fwd(2)
+    rs_fourth(2)
+    rs_near(2)
     for j, part in ((0, 0), (2, HERE)):
         tot[0, 8:9, part : part + HERE] = sum_rows(grads[:, j * HERE : (j + 1) * HERE].astype(F32))
 
-    left_two = lax.broadcasted_iota(jnp.int32, (2 * PIECE, 128), 1) < 64
+    left_four = lax.broadcasted_iota(jnp.int32, (4 * PIECE, 128), 1) < 64
 
     def head_grad(i):
-        rows = pl.ds(mul8(i * 2 * PIECE, 2 * PIECE), 2 * PIECE)
+        rows = pl.ds(mul8(i * 4 * PIECE, 4 * PIECE), 4 * PIECE)
         gq, gk, gv = (nn(xqt[rows, :], grads[:, j * HERE : (j + 1) * HERE]) for j in range(3))
         parts = (gq, gk, gv, gwo[rows, :])
 
         def put(xx, t, v):
-            wts[0, xx, i, :, :, t * 128 : t * 128 + 128] = v.reshape(2, PIECE, 128).astype(BF)
+            wts[0, xx, pl.ds(i * 2, 2), :, :, t * 128 : t * 128 + 128] = v.reshape(2, 2, PIECE, 128).astype(BF)
 
         for xx in range(2):
             for t in range(4):
                 put(xx, t, parts[t][:, xx * 128 : xx * 128 + 128])
         for t, first, second in ((4, gq, gk), (5, gv, gwo[rows, :])):
             one, two = first[:, 256:384], second[:, 256:384]
-            put(0, t, jnp.where(left_two, one, pltpu.roll(two, 64, 1)))
-            put(1, t, jnp.where(left_two, pltpu.roll(one, 64, 1), two))
-
-    loop(4, head_grad)
+            put(0, t, jnp.where(left_four, one, pltpu.roll(two, 64, 1)))
+            put(1, t, jnp.where(left_four, pltpu.roll(one, 64, 1), two))
 
     def most_x(i):
-        v = jnp.abs(tok[pl.ds(mul8(base + i * 128, 128), 128), :].astype(F32))
+        v = jnp.abs(tok[pl.ds(mul8(i * 128, 128), 128), :].astype(F32))
         tot[0, 9:10, :] = jnp.maximum(tot[0, 9:10, :], jnp.max(v, axis=0, keepdims=True))
 
     loop(4, most_x)
     row_of = lax.broadcasted_iota(jnp.int32, (16, 1), 0)
     small = copy(tot.at[0], tot_c, tt_s.at[0], tt_r.at[0], to_c)
     small.start()
-    rs_first(0)
-    rs_second(0)
-    rs_strip_z(0)
-
-    def token_part(start, held):
-        def body(n):
-            cols = pl.ds(mul8(n * 256, 256), 256)
-            held[:, cols] = nt(grads[pl.ds(start, OWN), :], wc[cols, :])
-
-        loop(3, body)
-
-    token_part(theirs, exb_s)
-    ex4 = copy(exb_s, exb_r, ex_s.at[6], ex_r.at[6], to_c)
-    ex4.start()
+    loop(2, head_grad)
     small.wait()
     mixed = jnp.where(row_of < 6, tot[0] + tot_c[...], jnp.maximum(tot[0], tot_c[...]))
     tot[1] = jnp.where((row_of >= 6) & (row_of < 9), tot[0], mixed)
     small = copy(tot.at[1], tot_x, tt_s.at[1], tt_r.at[1], to_x)
     small.start()
+    rs_first(0, False)
+    rs_second(0, False)
+    rs_strip_z(0)
+
+    def token_part(start, held):
+        held[...] = nt(grads[pl.ds(start, OWN), :], wc[...])
+
+    token_part(theirs, exb_s)
+    ex4 = copy(exb_s, exb_r, ex_s.at[6], ex_r.at[6], to_c)
+    ex4.start()
+    rs_third_x(1, True)
+    rs_third_y(1, True)
     token_part(mine, r1)
-    rs_fourth(2)
-    rs_strip_fwd(1)
-    rs_strip_xy(2)
-    rs_fifth(2)
     ex4.wait()
 
     def token_grad(i):
         rows = pl.ds(mul8(i * 64, 64), 64)
-        v = tok[pl.ds(mul8(base + mine + i * 64, 64), 64), :].astype(F32)
+        v = tok[pl.ds(mul8(mine + i * 64, 64), 64), :].astype(F32)
         bent = jnp.tanh(v * inv_of[0])
         got = gr2[rows, :] + (r1[rows, :] + exb_r[rows, :]) * (1.0 - bent * bent)
         o_tok[pl.ds(mul8(mp * OWN + i * 64, 64), 64), :] = got.astype(BF)
 
     loop(4, token_grad)
-    rs_third(0)
     own = o_tok.at[pl.ds(mul8(mp * OWN, OWN), OWN)]
     send("tok", own, own, gx_s.at[1], gx_r.at[1], to_c)
-    send("tok", own, own, gx_s.at[0], gx_r.at[0], to_x)
-    rs_strip_fwd(0)
+    rs_strip_fwd(1)
     small.wait()
     tot[2] = jnp.where(row_of < 9, tot[1] + tot_x[...], jnp.maximum(tot[1], tot_x[...]))
     small = copy(tot.at[2], tot_y, tt_s.at[2], tt_r.at[2], to_y)
     small.start()
+    rs_strip_xy(2)
+    rs_third_x(0, False)
+    rs_fifth(2)
+    rs_strip_xy(1)
+    rs_third_y(0, False)
+    rs_strip_y(2)
+    rs_strip_y(1)
+    send("tok", own, own, gx_s.at[0], gx_r.at[0], to_x)
+    rs_strip_fwd(0)
     rs_fourth(1)
-    rs_strip_xy(1)
-    rs_fifth(1)
-    rs_strip_xy(0)
+    rs_near(1)
     small.wait()
     tot[3] = jnp.where(row_of < 9, tot[2] + tot_y[...], jnp.maximum(tot[2], tot_y[...]))
     smalls = []
@@ -1237,10 +1296,16 @@
         made = copy(tot.at[3], tot_z.at[k - 1], tt_s.at[2 + k], tt_r.at[2 + k], to_z[k])
         made.start()
         smalls.append(made)
+    rs_fourth(0)
+    rs_strip_xy(0)
+    rs_strip_y(0)
+    rs_fifth(1)
+    rs_near(0)
+    rs_fifth(0)
     o_down[...] = rs_total(2) * _slope(w_down[...], w_inv[3])
-    rs_fourth(0)
-    rs_fifth(0)
+    leave(o_down, r_down)
     o_up[...] = rs_total(1) * _slope(w_up[...], w_inv[2])
+    leave(o_up, r_up)
 
     far = o_tok.at[pl.ds(mul8((nx * 2 + c) * OWN, OWN), OWN)]
     copy(far, far, gx_s.at[0], gx_r.at[0], to_x).wait_recv()
@@ -1265,6 +1330,13 @@
     for i in range(4):
         o_rng[i] = 0.9 * range_of[i] + 0.1 * jnp.max(done[9 + i : 10 + i, :])
 
+    for here, there in ((o_vec, r_vec), (o_bup, r_bup), (o_bqv, r_bqv)):
+        leave(here, there)
+    near = pl.ds(mul8((x * 2 + nc) * OWN, OWN), OWN)
+    copy(o_tok.at[near], o_tok.at[near], gx_s.at[1], gx_r.at[1], to_c).wait_recv()
+    far = pl.ds(mul8((nx * 2 + nc) * OWN, OWN), OWN)
+    copy(o_tok.at[far], o_tok.at[far], gx_s.at[2], gx_r.at[2], to_c).wait_recv()
+    leave(o_tok, r_tok)
     total = rs_total(0)
     for j in range(4):
         main = total[:, j * 128 : j * 128 + 128]
@@ -1276,12 +1348,12 @@
             o_qkv[j] = whole * _slope(w_qkv[j], w_inv[0])
         else:
             o_out[...] = whole.T * _slope(w_out[...], w_inv[1])
-    near = o_tok.at[pl.ds(mul8((x * 2 + nc) * OWN, OWN), OWN)]
-    copy(near, near, gx_s.at[1], gx_r.at[1], to_c).wait_recv()
-    far = o_tok.at[pl.ds(mul8((nx * 2 + nc) * OWN, OWN), OWN)]
-    copy(far, far, gx_s.at[2], gx_r.at[2], to_c).wait_recv()
+    leave(o_qkv, r_qkv)
+    leave(o_out, r_out)
     for group in list(started):
         sent(group)
+    for made in leaving:
+        made.wait()
 
 
 def _slope(values, inverse):
@@ -1303,13 +1375,23 @@
         return vmem(shape, F32)
 
     sems = pltpu.SemaphoreType.DMA
+    ins = (w_qkv, w_out, w_up, w_down.T, b_qv.transpose(1, 0, 2), b_up, vectors)
+    mask = key_mask.reshape(rows // 128, 128)
+    kinds = [
+        jax.ShapeDtypeStruct(grad_out.shape, BF),
+        jax.ShapeDtypeStruct(tokens.shape, BF),
+        *(jax.ShapeDtypeStruct(v.shape, F32) for v in ins),
+    ]
     scratch = [
+        buffer(half, WIDE),
+        *(vmem(v.shape, v.dtype) for v in (*ins, mask, grad_out)),
+        *(vmem(v.shape, v.dtype) for v in kinds),
         buffer(3, 2, 4, 2, PIECE, WIDE),
         buffer(2, 2, WIDE, WIDE),
         buffer(WIDE, 3 * HERE),
         buffer(WIDE, HERE),
         buffer(3, 4, 48, WIDE),
-        buffer(3, 4, 32, WIDE),
+        buffer(3, 4, 48, WIDE),
         buffer(3, 4, 80, WIDE),
         buffer(3, 4, 80, WIDE),
         buffer(3, 2, 80, WIDE),
@@ -1378,8 +1460,8 @@
         sems((3, 4)),
         sems((3, 4)),
         sems((3, 4)),
-        sems((3, 13)),
-        sems((3, 13)),
+        sems((3, 17)),
+        sems((3, 17)),
         sems((3, 8)),
         sems((3, 4)),
         sems((6,)),
@@ -1390,45 +1472,22 @@
         sems((6,)),
         sems((3,)),
         sems((3,)),
+        sems((10,)),
+        sems((9,)),
     ]
-    whole = pl.BlockSpec(memory_space=vmem)
+    far = pl.BlockSpec(memory_space=pltpu.HBM)
     scalars = pl.BlockSpec(memory_space=pltpu.SMEM)
-    shape = jax.ShapeDtypeStruct
     outs = pl.pallas_call(
         layer_kernel,
-        out_shape=[
-            shape(grad_out.shape, BF),
-            shape(tokens.shape, BF),
-            shape(w_qkv.shape, F32),
-            shape(w_out.shape, F32),
-            shape(w_up.shape, F32),
-            shape(w_down.shape[::-1], F32),
-            shape((b_qv.shape[1], b_qv.shape[0], b_qv.shape[2]), F32),
-            shape(b_up.shape, F32),
-            shape(vectors.shape, F32),
-            shape(ema_ranges.shape, F32),
-        ],
-        in_specs=[whole] * 8 + [scalars, whole, scalars, whole],
-        out_specs=[whole] * 9 + [scalars],
+        out_shape=[*kinds, jax.ShapeDtypeStruct(ema_ranges.shape, F32)],
+        in_specs=[far] * 8 + [scalars, far, scalars, far],
+        out_specs=[far] * 9 + [scalars],
         scratch_shapes=scratch,
         compiler_params=pltpu.CompilerParams(
             collective_id=0, has_side_effects=True, vmem_limit_bytes=VMEM_LIMIT
         ),
         name="encoder_layer",
-    )(
-        tokens,
-        w_qkv,
-        w_out,
-        w_up,
-        w_down.T,
-        b_qv.transpose(1, 0, 2),
-        b_up,
-        vectors,
-        ema_ranges,
-        key_mask.reshape(rows // 128, 128),
-        long_rows,
-        grad_out,
-    )
+    )(tokens, *ins, ema_ranges, mask, long_rows, grad_out)
     outs = finish(outs)
     return (*outs[:5], outs[5].T, outs[6].transpose(1, 0, 2), *outs[7:])
 

time: 153 us -> 143 us (0.935)
  Pallas kernels: 152 us -> 142 us
    pallas_call x1, Pallas kernels: 148 us -> 138 us  [layer_on_chips(): pl.pallas_call(layer_kernel, out_shape=[*kinds, jax.ShapeDtypeStruct(ema_...]
where the time goes in v3:
time: 143 us
  Pallas kernels  142 us (99%)
    pallas_call x1, Pallas kernels, layer_on_chips(): pl.pallas_call(layer_kernel, out_shape=[*kinds, jax.ShapeDtypeStruct(ema_...  138 us
    pallas_call x1, Pallas kernels, finish(): pl.pallas_call(finish_kernel, out_shape=[shape(v.shape, F32 if i == 1 els...  4.46 us

profile of v3, /device:TPU:0, one launch (start us, length us, event | category | flops | bytes accessed | tf_op | source)
XLA Modules:
  0.0 143.0 jit_solution(12843815487143399306)
XLA Ops:
  0.6 137.7 %encoder_layer.1 = (bf16[256,768]{1,0:T(8,128)(2,1)}, bf16[1024,768]{1,0:T(8,128)(2,1)}, f32[3,96,192]{2,1,0:T(8,128)}, f32[192,96]{1,0:T(8,128)}, f32[96,768]{1...) custom-call(bf16[1024,768]{1,0:T(8,128)(2,1)} %h_tok.1, ...), custom_call_target="tpu_custom_call" | custom-call | tf_op jit(solution)/shard_map/encoder_layer/pallas_call | solution.py:1480
  138.4 4.5 %write_results.1 = (bf16[256,768]{1,0:T(8,128)(2,1)}, f32[1024,768]{1,0:T(8,128)}, f32[3,96,192]{2,1,0:T(8,128)}, f32[192,96]{1,0:T(8,128)}, f32[96,768]{1,0:T(8...) custom-call(bf16[256,768]{1,0:T(8,128)(2,1)} %get-tuple-element.30.refs_0_,, ...), custom_call_target="tpu_custom_call" | custom-call | tf_op jit(solution)/shard_map/write_results/pallas_call | solution.py:1520

commit v4 on v3

--- a/solution.py
+++ b/solution.py
@@ -309,7 +309,7 @@
 WIDE = 768
 PIECE = 96
 AG_CUTS = ((0, 48, 48), (16, 32, 48), (32, 32, 32))
-RS_CUTS = ((16, 32, 48), (16, 32, 48), (32, 32, 32))
+RS_CUTS = ((16, 32, 48), (32, 32, 32), (32, 32, 32))
 OWN = 256
 HERE = 384
 
@@ -343,9 +343,9 @@
     h_bqv,
     h_bup,
     h_vec,
-    ranges,
+    h_rng,
     h_mask,
-    long_rows,
+    h_long,
     h_grad,
     r_layer,
     r_tok,
@@ -356,7 +356,7 @@
     r_bqv,
     r_bup,
     r_vec,
-    o_rng,
+    r_rng,
     tok,
     w_qkv,
     w_out,
@@ -376,6 +376,9 @@
     o_bqv,
     o_bup,
     o_vec,
+    ranges,
+    long_rows,
+    o_rng,
     wts,
     wff,
     wc,
@@ -505,21 +508,29 @@
             else:
                 pl.when(outer == which)(made.wait_send)
 
+    barrier = pltpu.get_barrier_semaphore()
+    for device in (to_c, to_x, to_y, to_xy, *to_z[1:]):
+        pl.semaphore_signal(barrier, inc=1, device_id=device, device_id_type=MESH)
+
     base = mul8(x * 512, 512)
     arriving = [
         pltpu.make_async_copy(there, here, in_s.at[i])
         for i, (there, here) in enumerate(
             (
+                (h_qkv, w_qkv),
+                (h_out, w_out),
                 (h_up, w_up),
                 (h_down, w_down),
-                (h_qkv, w_qkv),
-                (h_out, w_out),
                 (h_vec, vectors),
                 (h_bup, b_up),
                 (h_bqv, b_qv),
+                (h_rng, ranges),
                 (h_tok.at[pl.ds(base, 512)], tok),
                 (h_mask, mask),
+                (h_long, long_rows),
                 (h_grad, grad_out),
+                (h_up, wts.at[1, x, z, y]),
+                (h_down, wts.at[2, x, z, y]),
             )
         )
     ]
@@ -527,25 +538,123 @@
         made.start()
     leaving = []
 
+    def leave_rows(place):
+        part = pl.ds(mul8(place * OWN, OWN), OWN)
+        leave(o_tok.at[part], r_tok.at[part])
+
     def leave(here, there):
         made = pltpu.make_async_copy(here, there, out_s.at[len(leaving)])
         made.start()
         leaving.append(made)
 
-    range_of = [ranges[i] for i in range(4)]
-    inv_of = [1.0 / r for r in range_of]
-
-    barrier = pltpu.get_barrier_semaphore()
-    for device in (to_c, to_x, to_y, to_xy, *to_z[1:]):
-        pl.semaphore_signal(barrier, inc=1, device_id=device, device_id_type=MESH)
-    for made in arriving[:7]:
-        made.wait()
-    wts[1, x, z, y] = w_up[...]
-    wts[2, x, z, y] = w_down[...]
+    pl.semaphore_wait(barrier, 7)
+
+    def ag_rows(g, xx, zz, yy, part):
+        strip, one, two = AG_CUTS[g]
+        first = (0, strip, strip + one, strip)[part]
+        return wts.at[g, xx, zz, yy, pl.ds(first, (strip, one, two, one + two)[part])]
+
+    def ag_own(g, part):
+        if g == 0:
+            return ag_rows(g, x, z, y, part)
+        strip, one, two = AG_CUTS[g]
+        return (h_up, h_down)[g - 1].at[pl.ds(*((0, strip), None, None, (strip, one + two))[part])]
+
+    def ag_strips(g, zz):
+        return wts.at[g, :, zz, :, pl.ds(0, AG_CUTS[g][0])]
+
+    def ag_strip_xy(g):
+        own = ag_rows(g, x, z, y, 0)
+        for i, device in enumerate((to_x, to_y, to_xy)):
+            send(("ag", g), ag_own(g, 0), own, sts.at[g, i], str_.at[g, i], device)
+
+    def ag_strip_z(g):
+        for i, (xx, yy, device) in enumerate(((nx, y, to_x), (x, ny, to_y), (nx, ny, to_xy))):
+            got = ag_rows(g, xx, z, yy, 0)
+            copy(got, got, sts.at[g, i], str_.at[g, i], device).wait_recv()
+        own = ag_strips(g, z)
+        send(("ag", g), own, own, z2s.at[g, 0], z2r.at[g, 0], to_zk[1])
+        send(("ag", g), own, own, z2s.at[g, 1], z2r.at[g, 1 + outer], to_zk[2])
+
+    def ag_strip_fwd(g):
+        @pl.when(outer == 0)
+        def _():
+            for k in (2, 3):
+                got = ag_strips(g, zk[k])
+                copy(got, got, z2s.at[g, 0], z2r.at[g, k - 1], to_zk[k]).wait_recv()
+
+        for k in (2, 3):
+            got = ag_strips(g, zk[k])
+            send_if(0, ("ag", g), got, got, z2f.at[g, k - 2], z2r.at[g, k - 1], to_zk[1])
+
+    def ag_strip_got(g):
+        got = ag_strips(g, zk[1])
+        copy(got, got, z2s.at[g, 0], z2r.at[g, 0], to_zk[1]).wait_recv()
+
+        @pl.when(outer == 1)
+        def _():
+            for k in (2, 3):
+                got = ag_strips(g, zk[k])
+                copy(got, got, z2s.at[g, 0], z2r.at[g, k - 1], to_zk[1]).wait_recv()
+
+    def ag_z_send(g):
+        own, held = ag_rows(g, x, z, y, 3), ag_own(g, 3)
+        send(("ag", g), held, own, zs.at[g, 0], zr.at[g, 0], to_zk[1])
+        send(("ag", g), held, own, zs.at[g, 1], zr.at[g, 1 + outer], to_zk[2])
+
+    def ag_z_fwd(g, k):
+        got = ag_rows(g, x, zk[k], y, 3)
+        pl.when(outer == 0)(copy(got, got, zs.at[g, 0], zr.at[g, k - 1], to_zk[k]).wait_recv)
+        send_if(0, ("ag", g), got, got, zf.at[g, k - 2], zr.at[g, k - 1], to_zk[1])
+
+    def ag_xy_send(g, k, which=None):
+        own = ag_rows(g, x, zk[k], y, 3)
+        if which is not None:
+            send_if(which, ("ag", g), own, own, xs.at[g, k], xr.at[g, k], to_x)
+            send_if(which, ("ag", g), own, own, ys.at[g, k], yr.at[g, k], to_y)
+            return
+        if k > 0:
+            arrived = copy(own, own, zs.at[g, 0], zr.at[g, k - 1], to_zk[1]).wait_recv
+            if k > 1:
+                pl.when(outer == 1)(arrived)
+            else:
+                arrived()
+        held = own if k else ag_own(g, 3)
+        send(("ag", g), held, own, xs.at[g, k], xr.at[g, k], to_x)
+        send(("ag", g), held, own, ys.at[g, k], yr.at[g, k], to_y)
+
+    def ag_diag(g, k):
+        got = ag_rows(g, x, zk[k], ny, 3)
+        copy(got, got, ys.at[g, k], yr.at[g, k], to_y).wait_recv()
+        half = ag_rows(g, x, zk[k], ny, 1)
+        send(("ag", g), half, half, dxs.at[g, k], dxr.at[g, k], to_x)
+        got = ag_rows(g, nx, zk[k], y, 3)
+        copy(got, got, xs.at[g, k], xr.at[g, k], to_x).wait_recv()
+        half = ag_rows(g, nx, zk[k], y, 2)
+        send(("ag", g), half, half, dys.at[g, k], dyr.at[g, k], to_y)
+
+    def ag_last(g, k):
+        half = ag_rows(g, nx, zk[k], ny, 1)
+        copy(half, half, dxs.at[g, k], dxr.at[g, k], to_x).wait_recv()
+        half = ag_rows(g, nx, zk[k], ny, 2)
+        copy(half, half, dys.at[g, k], dyr.at[g, k], to_y).wait_recv()
+
+    ag_strip_xy(1)
+    ag_xy_send(1, 0)
+
+    arriving[0].wait()
+    arriving[1].wait()
     turned = w_out[...].T
     for j, part in enumerate((w_qkv[0], w_qkv[1], w_qkv[2], turned)):
         wts[0, x, z, y, :, j * 128 : j * 128 + 128] = part[:, 0:128]
         wts[0, x, z, y, :, 512 + j * 64 : 576 + j * 64] = part[:, 128:192]
+    ag_z_send(0)
+    ag_xy_send(0, 0)
+
+    for made in arriving[2:8]:
+        made.wait()
+    range_of = [ranges[i] for i in range(4)]
+    inv_of = [1.0 / r for r in range_of]
 
     sm[x, z, y] = jnp.zeros((16, 128), F32)
     sm[x, z, y, 0:6, 0:96] = vectors[...].astype(F32)
@@ -562,99 +671,17 @@
         peak_row = jnp.where(lane == g, most, peak_row)
     sm[x, z, y, 15:16] = peak_row
 
-    pl.semaphore_wait(barrier, 7)
-
-    def ag_rows(g, xx, zz, yy, part):
-        strip, one, two = AG_CUTS[g]
-        first = (0, strip, strip + one, strip)[part]
-        return wts.at[g, xx, zz, yy, pl.ds(first, (strip, one, two, one + two)[part])]
-
-    def ag_strips(g, zz):
-        return wts.at[g, :, zz, :, pl.ds(0, AG_CUTS[g][0])]
-
-    def ag_strip_xy(g):
-        own = ag_rows(g, x, z, y, 0)
-        for i, device in enumerate((to_x, to_y, to_xy)):
-            send(("ag", g), own, own, sts.at[g, i], str_.at[g, i], device)
-
-    def ag_strip_z(g):
-        for i, (xx, yy, device) in enumerate(((nx, y, to_x), (x, ny, to_y), (nx, ny, to_xy))):
-            got = ag_rows(g, xx, z, yy, 0)
-            copy(got, got, sts.at[g, i], str_.at[g, i], device).wait_recv()
-        own = ag_strips(g, z)
-        send(("ag", g), own, own, z2s.at[g, 0], z2r.at[g, 0], to_zk[1])
-        send(("ag", g), own, own, z2s.at[g, 1], z2r.at[g, 1 + outer], to_zk[2])
-
-    def ag_strip_fwd(g):
-        @pl.when(outer == 0)
-        def _():
-            for k in (2, 3):
-                got = ag_strips(g, zk[k])
-                copy(got, got, z2s.at[g, 0], z2r.at[g, k - 1], to_zk[k]).wait_recv()
-
-        for k in (2, 3):
-            got = ag_strips(g, zk[k])
-            send_if(0, ("ag", g), got, got, z2f.at[g, k - 2], z2r.at[g, k - 1], to_zk[1])
-
-    def ag_strip_got(g):
-        got = ag_strips(g, zk[1])
-        copy(got, got, z2s.at[g, 0], z2r.at[g, 0], to_zk[1]).wait_recv()
-
-        @pl.when(outer == 1)
-        def _():
-            for k in (2, 3):
-                got = ag_strips(g, zk[k])
-                copy(got, got, z2s.at[g, 0], z2r.at[g, k - 1], to_zk[1]).wait_recv()
-
-    def ag_z_send(g):
-        own = ag_rows(g, x, z, y, 3)
-        send(("ag", g), own, own, zs.at[g, 0], zr.at[g, 0], to_zk[1])
-        send(("ag", g), own, own, zs.at[g, 1], zr.at[g, 1 + outer], to_zk[2])
-
-    def ag_z_fwd(g, k):
-        got = ag_rows(g, x, zk[k], y, 3)
-        pl.when(outer == 0)(copy(got, got, zs.at[g, 0], zr.at[g, k - 1], to_zk[k]).wait_recv)
-        send_if(0, ("ag", g), got, got, zf.at[g, k - 2], zr.at[g, k - 1], to_zk[1])
-
-    def ag_xy_send(g, k):
-        own = ag_rows(g, x, zk[k], y, 3)
-        if k > 0:
-            arrived = copy(own, own, zs.at[g, 0], zr.at[g, k - 1], to_zk[1]).wait_recv
-            if k > 1:
-                pl.when(outer == 1)(arrived)
-            else:
-                arrived()
-        send(("ag", g), own, own, xs.at[g, k], xr.at[g, k], to_x)
-        send(("ag", g), own, own, ys.at[g, k], yr.at[g, k], to_y)
-
-    def ag_diag(g, k):
-        got = ag_rows(g, x, zk[k], ny, 3)
-        copy(got, got, ys.at[g, k], yr.at[g, k], to_y).wait_recv()
-        half = ag_rows(g, x, zk[k], ny, 1)
-        send(("ag", g), half, half, dxs.at[g, k], dxr.at[g, k], to_x)
-        got = ag_rows(g, nx, zk[k], y, 3)
-        copy(got, got, xs.at[g, k], xr.at[g, k], to_x).wait_recv()
-        half = ag_rows(g, nx, zk[k], y, 2)
-        send(("ag", g), half, half, dys.at[g, k], dyr.at[g, k], to_y)
-
-    def ag_last(g, k):
-        half = ag_rows(g, nx, zk[k], ny, 1)
-        copy(half, half, dxs.at[g, k], dxr.at[g, k], to_x).wait_recv()
-        half = ag_rows(g, nx, zk[k], ny, 2)
-        copy(half, half, dys.at[g, k], dyr.at[g, k], to_y).wait_recv()
-
     small_c = copy(sm.at[x, z, y], smc, sm_s.at[0], sm_r.at[0], to_c)
     small_c.start()
-    ag_z_send(0)
-    ag_xy_send(0, 0)
+    ag_z_send(1)
     small_c.wait()
     sm[x, z, y, 15:16] = jnp.maximum(sm[x, z, y, 15:16], smc[15:16])
-    small_x = copy(sm.at[x, z, y], sm.at[x, z, y], sm_s.at[1], sm_r.at[1], to_x)
-    small_x.start()
-    ag_strip_xy(1)
-    ag_xy_send(1, 0)
-
-    for made in arriving[7:]:
+    small_xy = ((nx, y, to_x), (x, ny, to_y), (nx, ny, to_xy))
+    for i, (_, _, device) in enumerate(small_xy):
+        send("sm", sm.at[x, z, y], sm.at[x, z, y], sm_s.at[1 + i], sm_r.at[1 + i], device)
+    ag_strip_xy(2)
+
+    for made in arriving[8:]:
         made.wait()
 
     def do_tokens(i):
@@ -663,13 +690,6 @@
         xq[rows, :] = (range_of[0] * jnp.tanh(v * inv_of[0])).astype(BF)
 
     loop(4, do_tokens)
-    copy(sm.at[nx, z, y], sm.at[nx, z, y], sm_s.at[1], sm_r.at[1], to_x).wait_recv()
-    small_y = copy(sm.at[:, z, y], sm.at[:, z, y], sm_s.at[2], sm_r.at[2], to_y)
-    small_y.start()
-    ag_strip_xy(2)
-    ag_xy_send(2, 0)
-    ag_z_send(1)
-
     def do_turn(j):
         cols = pl.ds(mul8(j * 128, 128), 128)
         xqt[cols, :] = xq[:, cols].T
@@ -677,6 +697,7 @@
     loop(6, do_turn)
     ag_xy_send(0, 1)
     ag_z_fwd(0, 2)
+    ag_z_fwd(0, 3)
 
     long_flag = long_rows[x].astype(F32)
     for r in range(4):
@@ -686,28 +707,26 @@
             seen = column * (1.0 if r == s else long_flag)
             bias[r * 128 : r * 128 + 128, s * 128 : s * 128 + 128] = jnp.where(seen > 0.5, 0.0, -1e30)
 
-    copy(sm.at[:, z, ny], sm.at[:, z, ny], sm_s.at[2], sm_r.at[2], to_y).wait_recv()
-    small_z = []
+    for i, (xx, yy, device) in enumerate(small_xy):
+        copy(sm.at[xx, z, yy], sm.at[xx, z, yy], sm_s.at[1 + i], sm_r.at[1 + i], device).wait_recv()
     for k in (1, 2, 3):
-        made = copy(sm.at[:, z], sm.at[:, z], sm_s.at[2 + k], sm_r.at[2 + k], to_z[k])
-        made.start()
-        small_z.append(made)
-    ag_z_fwd(0, 3)
+        send("sm", sm.at[:, z], sm.at[:, z], sm_s.at[3 + k], sm_r.at[3 + k], to_z[k])
+    ag_strip_z(1)
+    ag_z_send(2)
+    ag_diag(0, 0)
+    got = ag_rows(1, x, zk[1], y, 3)
+    copy(got, got, zs.at[1, 0], zr.at[1, 0], to_zk[1]).wait_recv()
+    ag_xy_send(1, 1, 1)
     ag_xy_send(0, 2)
-    ag_strip_z(1)
+    ag_z_fwd(1, 2)
+    ag_diag(0, 1)
     ag_xy_send(0, 3)
-    ag_diag(0, 0)
-    ag_diag(0, 1)
-    ag_z_send(2)
-    ag_xy_send(1, 1)
-    ag_z_fwd(1, 2)
-    ag_diag(0, 2)
+    ag_xy_send(1, 1, 0)
+    ag_z_fwd(1, 3)
+    ag_strip_z(2)
     for k in (1, 2, 3):
-        copy(sm.at[:, from_z[k]], sm.at[:, from_z[k]], sm_s.at[2 + k], sm_r.at[2 + k], to_z[k]).wait_recv()
-    small_x.wait_send()
-    small_y.wait_send()
-    for made in small_z:
-        made.wait_send()
+        copy(sm.at[:, from_z[k]], sm.at[:, from_z[k]], sm_s.at[3 + k], sm_r.at[3 + k], to_z[k]).wait_recv()
+    sent("sm")
 
     peaks = jnp.max(jnp.max(jnp.max(sm[:, :, :, 15:16, :], axis=0), axis=0), axis=0)
     w_peak = [jnp.max(jnp.where(lane == g, peaks, 0.0)) for g in range(4)]
@@ -739,20 +758,23 @@
             )
         bqv[j : j + 1, 256:384] = heads[0][0][first + 2 : first + 3] + heads[1][1][first + 2 : first + 3]
 
-    ag_z_fwd(1, 3)
-    ag_strip_z(2)
+    ag_diag(0, 2)
+    ag_xy_send(2, 0)
     ag_strip_fwd(1)
     ag_diag(0, 3)
-    for k in range(4):
-        ag_last(0, k)
+    ag_xy_send(1, 2)
+    ag_xy_send(1, 3)
+    ag_diag(1, 0)
+    ag_diag(1, 1)
 
     left = lax.broadcasted_iota(jnp.int32, (PIECE, 128), 1) < 64
 
-    def squash_heads(place):
+    def squash_heads(zz, yy):
+        place = zz * 2 + yy
         rows = pl.ds(mul8(place * PIECE, PIECE), PIECE)
         tiles = []
         for xx in range(2):
-            v = wts[0, xx, place // 2, place % 2].astype(F32)
+            v = wts[0, xx, zz, yy].astype(F32)
             inner = [w_peak[0] * jnp.tanh(v[:, t * 128 : t * 128 + 128] * w_inv[0]) for t in (0, 1, 2)]
             inner.append(w_peak[1] * jnp.tanh(v[:, 384:512] * w_inv[1]))
             mixed = jnp.where(left, w_peak[0], w_peak[1])
@@ -774,9 +796,13 @@
             else:
                 wo[rows, 256:384] = other
 
-    loop(8, squash_heads)
-    ag_xy_send(1, 2)
-    ag_xy_send(1, 3)
+    loop(4, lambda zz: squash_heads(zz, y))
+    for k in range(4):
+        ag_last(0, k)
+    loop(4, lambda zz: squash_heads(zz, ny))
+    ag_z_fwd(2, 2)
+    ag_z_fwd(2, 3)
+    ag_diag(1, 2)
 
     def squash_ff(g, xx):
         def body(place):
@@ -795,14 +821,11 @@
         elif j == 2:
             got = got + bqv[1:2, :]
         held[...] = got.astype(BF)
-    ag_diag(1, 0)
-    ag_z_fwd(2, 2)
-    ag_z_fwd(2, 3)
+    ag_diag(1, 3)
     for p in range(3):
         cols = slice(p * 128, p * 128 + 128)
         kt[cols, :] = ks[:, cols].T
         vt[cols, :] = vs[:, cols].T
-    ag_diag(1, 1)
     ag_xy_send(2, 1)
 
     half_of = lax.broadcasted_iota(jnp.int32, (1, 128), 1) // 64
@@ -820,14 +843,13 @@
                 probs[p * 2 + e, :, n * 256 : n * 256 + 256] = s
                 ctxt[feats, n * 256 : n * 256 + 256] = nn(vt[feats, :], s)
 
+    ag_strip_fwd(2)
     attend(0)
     ag_xy_send(2, 2)
+    ag_diag(2, 0)
     attend(1)
-    ag_diag(1, 2)
-    ag_strip_fwd(2)
+    ag_xy_send(2, 3)
     attend(2)
-    ag_xy_send(2, 3)
-    ag_diag(1, 3)
 
     for p in range(3):
         cols = slice(p * 128, p * 128 + 128)
@@ -838,15 +860,25 @@
     most = jnp.max(jnp.max(jnp.abs(ctxt[...]), axis=0, keepdims=True), axis=1, keepdims=True)
     tot[0, 10:11, :] = jnp.broadcast_to(most, (1, WIDE))
 
-    def out_part(start, held):
-        held[...] = nt(cq[pl.ds(start, OWN), :], wo[...])
-
-    out_part(theirs, exa_s)
-    ex1 = copy(exa_s, exa_r, ex_s.at[0], ex_r.at[0], to_c)
-    ex1.start()
-    ag_diag(2, 0)
+    def out_part(start, held, cols=slice(0, WIDE)):
+        held[:, cols] = nt(cq[pl.ds(start, OWN), :], wo[cols, :])
+
+    ex1 = []
+    for i in range(2):
+        cols = slice(i * HERE, i * HERE + HERE)
+        out_part(theirs, exa_s, cols)
+        made = copy(exa_s.at[:, cols], exa_r.at[:, cols], ex_s.at[(0, 9)[i]], ex_r.at[(0, 9)[i]], to_c)
+        made.start()
+        ex1.append(made)
     out_part(mine, r1)
-    ex1.wait()
+    ag_diag(2, 1)
+    ag_strip_got(1)
+    for k in range(4):
+        ag_last(1, k)
+    squash_ff(1, 0)
+    squash_ff(1, 1)
+    for made in ex1:
+        made.wait()
 
     def sum_rows(v):
         return jnp.sum(v, axis=0, keepdims=True)
@@ -855,8 +887,8 @@
         return jnp.sum(v, axis=-1, keepdims=True) * (1.0 / WIDE)
 
     def first_norm(i):
-        rows = pl.ds(mul8(i * 64, 64), 64)
-        v = tok[pl.ds(mul8(mine + i * 64, 64), 64), :].astype(F32)
+        rows = pl.ds(mul8(i * 128, 128), 128)
+        v = tok[pl.ds(mul8(mine + i * 128, 128), 128), :].astype(F32)
         v = v + (r1[rows, :] + exa_r[rows, :] + vec[0:1, :])
         r1[rows, :] = v
         center = v - mean_of(v)
@@ -868,9 +900,17 @@
         tot[0, 11:12, :] = jnp.maximum(tot[0, 11:12, :], jnp.max(jnp.abs(h), axis=0, keepdims=True))
         bent = jnp.tanh(h * inv_of[2])
         sl1[rows, :] = 1.0 - bent * bent
-        hq[pl.ds(mul8(mine + i * 64, 64), 64), :] = (range_of[2] * bent).astype(BF)
-
-    loop(4, first_norm)
+        hq[pl.ds(mul8(mine + i * 128, 128), 128), :] = (range_of[2] * bent).astype(BF)
+
+    def half_rows(start, i):
+        return pl.ds(mul8(start + i * 128, 128), 128)
+
+    for i in range(2):
+        first_norm(i)
+        own = hq.at[half_rows(mine, i)]
+        made = copy(own, own, ex_s.at[(1, 10)[i]], ex_r.at[(1, 10)[i]], to_c)
+        made.start()
+        started.setdefault("share", []).append((made, None))
 
     def share_rows(held, number):
         own = held.at[pl.ds(mine, OWN)]
@@ -885,13 +925,12 @@
     def turn_rows(held, out, start):
         out[:, pl.ds(start, OWN)] = held[pl.ds(start, OWN), :].T
 
-    share_rows(hq, 1)
-    ag_strip_got(1)
-    ag_diag(2, 1)
-    got_rows(hq, 1)
-    turn_rows(hq, hqt, 0)
-    turn_rows(hq, hqt, OWN)
-    squash_ff(1, x)
+    ag_diag(2, 2)
+    turn_rows(hq, hqt, mine)
+    for i in range(2):
+        other = hq.at[half_rows(theirs, i)]
+        copy(other, other, ex_s.at[(1, 10)[i]], ex_r.at[(1, 10)[i]], to_c).wait_recv()
+    turn_rows(hq, hqt, theirs)
 
     def expand(xx):
         wide = pl.ds(mul8(xx * WIDE, WIDE), WIDE)
@@ -910,17 +949,13 @@
         loop(2, body)
 
     expand(x)
-    ag_diag(2, 2)
-    for k in range(4):
-        ag_last(1, k)
-    squash_ff(1, nx)
+    ag_diag(2, 3)
     expand(nx)
-    ag_diag(2, 3)
     ag_strip_got(2)
 
-    def down_part(start, held, xx, first):
-        got = nt(aq[pl.ds(start, OWN), pl.ds(mul8(xx * WIDE, WIDE), WIDE)], wff[1, xx])
-        held[...] = got if first else held[...] + got
+    def down_part(start, held, xx, first, cols=slice(0, WIDE)):
+        got = nt(aq[pl.ds(start, OWN), pl.ds(mul8(xx * WIDE, WIDE), WIDE)], wff[1, xx, cols, :])
+        held[:, cols] = got if first else held[:, cols] + got
 
     squash_ff(2, x)
     down_part(theirs, exb_s, x, True)
@@ -928,14 +963,19 @@
     for k in range(4):
         ag_last(2, k)
     squash_ff(2, nx)
-    down_part(theirs, exb_s, nx, False)
-    ex2 = copy(exb_s, exb_r, ex_s.at[2], ex_r.at[2], to_c)
-    ex2.start()
+    ex2 = []
+    for i in range(2):
+        cols = slice(i * HERE, i * HERE + HERE)
+        down_part(theirs, exb_s, nx, False, cols)
+        made = copy(exb_s.at[:, cols], exb_r.at[:, cols], ex_s.at[(2, 7)[i]], ex_r.at[(2, 7)[i]], to_c)
+        made.start()
+        ex2.append(made)
     down_part(mine, gr2, nx, False)
-    ex2.wait()
+    for made in ex2:
+        made.wait()
 
     def second_norm(i):
-        rows = pl.ds(mul8(i * 64, 64), 64)
+        rows = pl.ds(mul8(i * 128, 128), 128)
         v = r1[rows, :] + (gr2[rows, :] + exb_r[rows, :] + vec[1:2, :])
         center = v - mean_of(v)
         factor = lax.rsqrt(mean_of(center * center) + 1e-12)
@@ -949,15 +989,21 @@
         gr2[rows, :] = back
         low = back.astype(BF)
         tot[0, 1:2, :] += sum_rows(low.astype(F32))
-        gf[pl.ds(mul8(mine + i * 64, 64), 64), :] = low
-
-    loop(4, second_norm)
+        gf[pl.ds(mul8(mine + i * 128, 128), 128), :] = low
+
+    for i in range(2):
+        second_norm(i)
+        own = gf.at[half_rows(mine, i)]
+        made = copy(own, own, ex_s.at[(3, 8)[i]], ex_r.at[(3, 8)[i]], to_c)
+        made.start()
+        started.setdefault("share", []).append((made, None))
     leave(o_layer, r_layer)
-    share_rows(gf, 3)
     turn_rows(gf, rowt, mine)
     for g in range(3):
         sent(("ag", g))
-    got_rows(gf, 3)
+    for i in range(2):
+        other = gf.at[half_rows(theirs, i)]
+        copy(other, other, ex_s.at[(3, 8)[i]], ex_r.at[(3, 8)[i]], to_c).wait_recv()
     turn_rows(gf, rowt, theirs)
 
     def rs_send(g, number, src, dst, device):
@@ -1084,7 +1130,7 @@
 
             rs_send_if(0, g, 4 + k, strips(g, zk[k]), rz2.at[g, 1, :, :, here], to_zk[k], rs_r.at[g, 9])
 
-    def rs_strip_xy(g):
+    def rs_strip_sum(g):
         here = pl.ds(0, RS_CUTS[g][0])
         for k in (0, 1):
             rs_wait(g, 8 + k, rz2.at[g, k, :, :, here], to_zk[1 + k])
@@ -1093,11 +1139,11 @@
             + rz2[g, 0, :, :, here].astype(F32)
             + rz2[g, 1, :, :, here].astype(F32)
         ).astype(BF)
+
+    def rs_strip_send(g):
+        here = pl.ds(0, RS_CUTS[g][0])
+        rs_send(g, 12, wts.at[g, nx, z, ny, here], rst.at[g, 2, here], to_xy)
         rs_send(g, 10, wts.at[g, nx, z, y, here], rst.at[g, 0, here], to_x)
-        rs_send(g, 12, wts.at[g, nx, z, ny, here], rst.at[g, 2, here], to_xy)
-
-    def rs_strip_y(g):
-        here = pl.ds(0, RS_CUTS[g][0])
         rs_send(g, 11, wts.at[g, x, z, ny, here], rst.at[g, 1, here], to_y)
 
     def rs_total(g):
@@ -1273,19 +1319,19 @@
     loop(4, token_grad)
     own = o_tok.at[pl.ds(mul8(mp * OWN, OWN), OWN)]
     send("tok", own, own, gx_s.at[1], gx_r.at[1], to_c)
+    leave_rows(mp)
     rs_strip_fwd(1)
     small.wait()
     tot[2] = jnp.where(row_of < 9, tot[1] + tot_x[...], jnp.maximum(tot[1], tot_x[...]))
     small = copy(tot.at[2], tot_y, tt_s.at[2], tt_r.at[2], to_y)
     small.start()
-    rs_strip_xy(2)
     rs_third_x(0, False)
     rs_fifth(2)
-    rs_strip_xy(1)
     rs_third_y(0, False)
-    rs_strip_y(2)
-    rs_strip_y(1)
     send("tok", own, own, gx_s.at[0], gx_r.at[0], to_x)
+    for g in (2, 1):
+        rs_strip_sum(g)
+        rs_strip_send(g)
     rs_strip_fwd(0)
     rs_fourth(1)
     rs_near(1)
@@ -1297,8 +1343,8 @@
         made.start()
         smalls.append(made)
     rs_fourth(0)
-    rs_strip_xy(0)
-    rs_strip_y(0)
+    rs_strip_sum(0)
+    rs_strip_send(0)
     rs_fifth(1)
     rs_near(0)
     rs_fifth(0)
@@ -1310,6 +1356,7 @@
     far = o_tok.at[pl.ds(mul8((nx * 2 + c) * OWN, OWN), OWN)]
     copy(far, far, gx_s.at[0], gx_r.at[0], to_x).wait_recv()
     send("tok", far, far, gx_s.at[2], gx_r.at[2], to_c)
+    leave_rows(nx * 2 + c)
 
     for made in smalls:
         made.wait()
@@ -1328,15 +1375,14 @@
         for h, tile, shift in ((0, pair, 0), (1, pair, 64), (2, row[:, 256:384], 64 * x)):
             o_bqv[h, j : j + 1, :] = pltpu.roll(tile, (256 - shift - dp * 8) % 128, 1)[0:1, 0:8]
     for i in range(4):
-        o_rng[i] = 0.9 * range_of[i] + 0.1 * jnp.max(done[9 + i : 10 + i, :])
-
-    for here, there in ((o_vec, r_vec), (o_bup, r_bup), (o_bqv, r_bqv)):
+        most = jnp.max(done[9 + i : 10 + i, :], axis=1, keepdims=True)
+        o_rng[i : i + 1, :] = jnp.broadcast_to(0.9 * range_of[i] + 0.1 * most, (1, 128))
+
+    for here, there in ((o_vec, r_vec), (o_bup, r_bup), (o_bqv, r_bqv), (o_rng, r_rng)):
         leave(here, there)
     near = pl.ds(mul8((x * 2 + nc) * OWN, OWN), OWN)
     copy(o_tok.at[near], o_tok.at[near], gx_s.at[1], gx_r.at[1], to_c).wait_recv()
-    far = pl.ds(mul8((nx * 2 + nc) * OWN, OWN), OWN)
-    copy(o_tok.at[far], o_tok.at[far], gx_s.at[2], gx_r.at[2], to_c).wait_recv()
-    leave(o_tok, r_tok)
+    leave_rows(x * 2 + nc)
     total = rs_total(0)
     for j in range(4):
         main = total[:, j * 128 : j * 128 + 128]
@@ -1350,6 +1396,9 @@
             o_out[...] = whole.T * _slope(w_out[...], w_inv[1])
     leave(o_qkv, r_qkv)
     leave(o_out, r_out)
+    far = pl.ds(mul8((nx * 2 + nc) * OWN, OWN), OWN)
+    copy(o_tok.at[far], o_tok.at[far], gx_s.at[2], gx_r.at[2], to_c).wait_recv()
+    leave_rows(nx * 2 + nc)
     for group in list(started):
         sent(group)
     for made in leaving:
@@ -1386,6 +1435,9 @@
         buffer(half, WIDE),
         *(vmem(v.shape, v.dtype) for v in (*ins, mask, grad_out)),
         *(vmem(v.shape, v.dtype) for v in kinds),
+        pltpu.SMEM(ema_ranges.shape, F32),
+        pltpu.SMEM(long_rows.shape, jnp.int32),
+        f32(8, 128),
         buffer(3, 2, 4, 2, PIECE, WIDE),
         buffer(2, 2, WIDE, WIDE),
         buffer(WIDE, 3 * HERE),
@@ -1464,66 +1516,67 @@
         sems((3, 17)),
         sems((3, 8)),
         sems((3, 4)),
-        sems((6,)),
-        sems((6,)),
         sems((7,)),
         sems((7,)),
+        sems((11,)),
+        sems((11,)),
         sems((6,)),
         sems((6,)),
         sems((3,)),
         sems((3,)),
-        sems((10,)),
-        sems((9,)),
+        sems((14,)),
+        sems((13,)),
     ]
     far = pl.BlockSpec(memory_space=pltpu.HBM)
-    scalars = pl.BlockSpec(memory_space=pltpu.SMEM)
     outs = pl.pallas_call(
         layer_kernel,
-        out_shape=[*kinds, jax.ShapeDtypeStruct(ema_ranges.shape, F32)],
-        in_specs=[far] * 8 + [scalars, far, scalars, far],
-        out_specs=[far] * 9 + [scalars],
+        out_shape=[*kinds, jax.ShapeDtypeStruct((8, 128), F32)],
+        in_specs=[far] * 12,
+        out_specs=[far] * 10,
         scratch_shapes=scratch,
         compiler_params=pltpu.CompilerParams(
             collective_id=0, has_side_effects=True, vmem_limit_bytes=VMEM_LIMIT
         ),
         name="encoder_layer",
     )(tokens, *ins, ema_ranges, mask, long_rows, grad_out)
-    outs = finish(outs)
+    outs = finish(outs, ema_ranges)
     return (*outs[:5], outs[5].T, outs[6].transpose(1, 0, 2), *outs[7:])
 
 
 def finish_kernel(*refs):
-    ins, outs, held, wide, sem = refs[:10], refs[10:20], refs[20:29], refs[29], refs[30]
-    parts = [pl.ds(i * OWN, OWN) for i in range(ins[1].shape[0] // OWN)]
-    arriving = [pltpu.make_async_copy(ins[1].at[p], held[1].at[p], sem.at[9 + i]) for i, p in enumerate(parts)]
-    moved = [i for i in range(9) if i != 1]
+    ins, outs, held, wide, sem = refs[:10], refs[10:20], refs[20:30], refs[30], refs[31]
+    step = OWN // 2
+    parts = [pl.ds(i * step, step) for i in range(ins[1].shape[0] // step)]
+    arriving = [pltpu.make_async_copy(ins[1].at[p], held[1].at[p], sem.at[10 + i]) for i, p in enumerate(parts)]
+    moved = [i for i in range(10) if i != 1]
     arriving += [pltpu.make_async_copy(ins[i], held[i], sem.at[i]) for i in moved]
-    leaving = [pltpu.make_async_copy(wide.at[p], outs[1].at[p], sem.at[9 + i]) for i, p in enumerate(parts)]
-    leaving += [pltpu.make_async_copy(held[i], outs[i], sem.at[i]) for i in moved]
+    leaving = [pltpu.make_async_copy(wide.at[p], outs[1].at[p], sem.at[10 + i]) for i, p in enumerate(parts)]
+    leaving += [pltpu.make_async_copy(held[i], outs[i], sem.at[i]) for i in moved[:-1]]
     for made in arriving:
         made.start()
-    for i in range(4):
-        outs[9][i] = ins[9][i]
     for i, (here, there) in enumerate(zip(arriving, leaving)):
         here.wait()
         if i < len(parts):
             wide[parts[i], :] = held[1][parts[i], :].astype(F32)
         there.start()
+    arriving[-1].wait()
+    for i in range(4):
+        outs[9][i] = held[9][i, 0]
     for made in leaving:
         made.wait()
 
 
-def finish(held):
+def finish(held, ranges):
     shape = jax.ShapeDtypeStruct
     far = pl.BlockSpec(memory_space=pltpu.HBM)
-    scalars = pl.BlockSpec(memory_space=pltpu.SMEM)
     return pl.pallas_call(
         finish_kernel,
-        out_shape=[shape(v.shape, F32 if i == 1 else v.dtype) for i, v in enumerate(held)],
-        in_specs=[far] * 9 + [scalars],
-        out_specs=[far] * 9 + [scalars],
-        scratch_shapes=[pltpu.VMEM(v.shape, v.dtype) for v in held[:9]]
-        + [pltpu.VMEM(held[1].shape, F32), pltpu.SemaphoreType.DMA((9 + held[1].shape[0] // OWN,))],
+        out_shape=[shape(v.shape, F32 if i == 1 else v.dtype) for i, v in enumerate(held[:9])]
+        + [shape(ranges.shape, F32)],
+        in_specs=[far] * 10,
+        out_specs=[far] * 9 + [pl.BlockSpec(memory_space=pltpu.SMEM)],
+        scratch_shapes=[pltpu.VMEM(v.shape, v.dtype) for v in held]
+        + [pltpu.VMEM(held[1].shape, F32), pltpu.SemaphoreType.DMA((10 + held[1].shape[0] * 2 // OWN,))],
         compiler_params=pltpu.CompilerParams(vmem_limit_bytes=VMEM_LIMIT),
         name="write_results",
     )(*held)

time: 143 us -> 134 us (0.937)
  Pallas kernels: 142 us -> 133 us
    pallas_call x1, Pallas kernels: 138 us -> 129 us  [layer_on_chips(): pl.pallas_call(layer_kernel, out_shape=[*kinds, jax.ShapeDtypeStruct((8,...]
where the time goes in v4:
time: 134 us; the launch traced here: 133 us
  Pallas kernels  133 us (99%)
    pallas_call x1, Pallas kernels, layer_on_chips(): pl.pallas_call(layer_kernel, out_shape=[*kinds, jax.ShapeDtypeStruct((8,...  129 us
    pallas_call x1, Pallas kernels, finish(): pl.pallas_call(finish_kernel, out_shape=[shape(v.shape, F32 if i == 1 els...  3.74 us

profile of v4, /device:TPU:0, one launch (start us, length us, event | category | flops | bytes accessed | tf_op | source)
XLA Modules:
  0.0 133.4 jit_solution(8616342804032113723)
XLA Ops:
  0.6 128.9 %encoder_layer.1 = (bf16[256,768]{1,0:T(8,128)(2,1)}, bf16[1024,768]{1,0:T(8,128)(2,1)}, f32[3,96,192]{2,1,0:T(8,128)}, f32[192,96]{1,0:T(8,128)}, f32[96,768]{1...) custom-call(bf16[1024,768]{1,0:T(8,128)(2,1)} %h_tok.1, ...), custom_call_target="tpu_custom_call" | custom-call | tf_op jit(solution)/shard_map/encoder_layer/pallas_call | solution.py:1531
  129.5 3.7 %write_results.1 = (bf16[256,768]{1,0:T(8,128)(2,1)}, f32[1024,768]{1,0:T(8,128)}, f32[3,96,192]{2,1,0:T(8,128)}, f32[192,96]{1,0:T(8,128)}, f32[96,768]{1,0:T(8...) custom-call(bf16[256,768]{1,0:T(8,128)(2,1)} %get-tuple-element.30.refs_0_,, ...), custom_call_target="tpu_custom_call" | custom-call | tf_op jit(solution)/shard_map/write_results/pallas_call | solution.py:1572

commit v5 on v4

--- a/solution.py
+++ b/solution.py
@@ -1,3 +1,6 @@
+import functools
+import math
+
 import jax
 import jax.numpy as jnp
 from jax import lax
@@ -309,7 +312,7 @@
 WIDE = 768
 PIECE = 96
 AG_CUTS = ((0, 48, 48), (16, 32, 48), (32, 32, 32))
-RS_CUTS = ((16, 32, 48), (32, 32, 32), (32, 32, 32))
+RS_CUTS = ((16, 32, 48), (32, 16, 48), (32, 32, 32))
 OWN = 256
 HERE = 384
 
@@ -394,6 +397,7 @@
     rst,
     sm,
     smc,
+    smf,
     vec,
     bup,
     bqv,
@@ -437,25 +441,14 @@
     tot_x,
     tot_y,
     tot_z,
-    zs,
-    zf,
+    link_s,
     zr,
-    z2s,
-    z2f,
     z2r,
-    sts,
     str_,
-    xs,
     xr,
-    ys,
     yr,
-    dxs,
-    dxr,
-    dys,
-    dyr,
-    rs_s,
+    dr,
     rs_r,
-    rf_s,
     rf_r,
     sm_s,
     sm_r,
@@ -466,7 +459,6 @@
     gx_s,
     gx_r,
     in_s,
-    out_s,
 ):
     dp = lax.axis_index("dp")
     mp = lax.axis_index("mp")
@@ -478,35 +470,53 @@
     to_c = (dp, x * 2 + nc)
     to_xy = (z * 2 + ny, nx * 2 + c)
     to_z = [None] + [((z + k) % 4 * 2 + y, mp) for k in (1, 2, 3)]
-    from_z = [z] + [(z + 4 - k) % 4 for k in (1, 2, 3)]
     zk = [z, z + 1 - 2 * (z % 2), 2 - z // 2, 3 - 3 * (z // 2)]
     outer = (z * z - 3 * z + 2) // 2
     to_zk = [None] + [(zk[k] * 2 + y, mp) for k in (1, 2, 3)]
     mine = mul8(c * OWN, OWN)
     theirs = mul8(nc * OWN, OWN)
     started = {}
+    moved = {}
 
     def copy(src, dst, send, recv, device):
         return pltpu.make_async_remote_copy(
             src_ref=src, dst_ref=dst, send_sem=send, recv_sem=recv, device_id=device, device_id_type=MESH
         )
 
-    def send(group, *args):
-        made = copy(*args)
+    def send(kind, g, axis, src, dst, recv, device, which=None):
+        made = copy(src, dst, kind.at[g, axis], recv, device)
+        if which is None:
+            made.start()
+        else:
+            pl.when(outer == which)(made.start)
+        rows = math.prod(src.shape[:-1])
+        count = moved.setdefault((id(kind), g, axis), [kind.at[g, axis], 0, 0])
+        for place in (0, 1):
+            if which is None or which == place:
+                count[1 + place] += rows
+
+    def sent(kind):
+        for key in [key for key in moved if key[0] == id(kind)]:
+            sem, inside, ends = moved.pop(key)
+            if inside == ends:
+                got_rows_of(inside, sem)
+            else:
+                pl.when(outer == 0)(functools.partial(got_rows_of, inside, sem))
+                pl.when(outer == 1)(functools.partial(got_rows_of, ends, sem))
+
+    def arrived(ref, sem):
+        copy(ref, ref, link_s.at[0, 0], sem, to_c).wait_recv()
+
+    def got_rows_of(rows, sem):
+        arrived(gwo.at[pl.ds(0, rows)], sem)
+
+    def keep(group, made):
         made.start()
-        started.setdefault(group, []).append((made, None))
-
-    def send_if(which, group, *args):
-        made = copy(*args)
-        pl.when(outer == which)(made.start)
-        started.setdefault(group, []).append((made, which))
-
-    def sent(group):
-        for made, which in started.pop(group, []):
-            if which is None:
-                made.wait_send()
-            else:
-                pl.when(outer == which)(made.wait_send)
+        started.setdefault(group, []).append(made)
+
+    def kept(group):
+        for made in started.pop(group, []):
+            made.wait_send()
 
     barrier = pltpu.get_barrier_semaphore()
     for device in (to_c, to_x, to_y, to_xy, *to_z[1:]):
@@ -543,7 +553,7 @@
         leave(o_tok.at[part], r_tok.at[part])
 
     def leave(here, there):
-        made = pltpu.make_async_copy(here, there, out_s.at[len(leaving)])
+        made = pltpu.make_async_copy(here, there, in_s.at[len(leaving)])
         made.start()
         leaving.append(made)
 
@@ -565,79 +575,62 @@
 
     def ag_strip_xy(g):
         own = ag_rows(g, x, z, y, 0)
-        for i, device in enumerate((to_x, to_y, to_xy)):
-            send(("ag", g), ag_own(g, 0), own, sts.at[g, i], str_.at[g, i], device)
+        for axis, device in ((0, to_x), (1, to_y), (0, to_xy)):
+            send(link_s, g, axis, ag_own(g, 0), own, str_.at[g - 1], device)
 
     def ag_strip_z(g):
-        for i, (xx, yy, device) in enumerate(((nx, y, to_x), (x, ny, to_y), (nx, ny, to_xy))):
-            got = ag_rows(g, xx, z, yy, 0)
-            copy(got, got, sts.at[g, i], str_.at[g, i], device).wait_recv()
+        got_rows_of(3 * AG_CUTS[g][0], str_.at[g - 1])
         own = ag_strips(g, z)
-        send(("ag", g), own, own, z2s.at[g, 0], z2r.at[g, 0], to_zk[1])
-        send(("ag", g), own, own, z2s.at[g, 1], z2r.at[g, 1 + outer], to_zk[2])
+        send(link_s, g, 2, own, own, z2r.at[g - 1, 0], to_zk[1])
+        send(link_s, g, 2, own, own, z2r.at[g - 1, 1 + outer], to_zk[2])
 
     def ag_strip_fwd(g):
-        @pl.when(outer == 0)
-        def _():
-            for k in (2, 3):
-                got = ag_strips(g, zk[k])
-                copy(got, got, z2s.at[g, 0], z2r.at[g, k - 1], to_zk[k]).wait_recv()
-
         for k in (2, 3):
-            got = ag_strips(g, zk[k])
-            send_if(0, ("ag", g), got, got, z2f.at[g, k - 2], z2r.at[g, k - 1], to_zk[1])
+            pl.when(outer == 0)(functools.partial(arrived, ag_strips(g, zk[k]), z2r.at[g - 1, k - 1]))
+        for k in (2, 3):
+            held = ag_strips(g, zk[k])
+            send(link_s, g, 2, held, held, z2r.at[g - 1, k - 1], to_zk[1], 0)
 
     def ag_strip_got(g):
-        got = ag_strips(g, zk[1])
-        copy(got, got, z2s.at[g, 0], z2r.at[g, 0], to_zk[1]).wait_recv()
-
-        @pl.when(outer == 1)
-        def _():
-            for k in (2, 3):
-                got = ag_strips(g, zk[k])
-                copy(got, got, z2s.at[g, 0], z2r.at[g, k - 1], to_zk[1]).wait_recv()
+        arrived(ag_strips(g, zk[1]), z2r.at[g - 1, 0])
+        for k in (2, 3):
+            pl.when(outer == 1)(functools.partial(arrived, ag_strips(g, zk[k]), z2r.at[g - 1, k - 1]))
 
     def ag_z_send(g):
         own, held = ag_rows(g, x, z, y, 3), ag_own(g, 3)
-        send(("ag", g), held, own, zs.at[g, 0], zr.at[g, 0], to_zk[1])
-        send(("ag", g), held, own, zs.at[g, 1], zr.at[g, 1 + outer], to_zk[2])
+        send(link_s, g, 2, held, own, zr.at[g, 0], to_zk[1])
+        send(link_s, g, 2, held, own, zr.at[g, 1 + outer], to_zk[2])
 
     def ag_z_fwd(g, k):
-        got = ag_rows(g, x, zk[k], y, 3)
-        pl.when(outer == 0)(copy(got, got, zs.at[g, 0], zr.at[g, k - 1], to_zk[k]).wait_recv)
-        send_if(0, ("ag", g), got, got, zf.at[g, k - 2], zr.at[g, k - 1], to_zk[1])
+        held = ag_rows(g, x, zk[k], y, 3)
+        pl.when(outer == 0)(functools.partial(arrived, held, zr.at[g, k - 1]))
+        send(link_s, g, 2, held, held, zr.at[g, k - 1], to_zk[1], 0)
+
+    def ag_z_got(g, k):
+        held = ag_rows(g, x, zk[k], y, 3)
+        if k == 1:
+            arrived(held, zr.at[g, 0])
+        elif k > 1:
+            pl.when(outer == 1)(functools.partial(arrived, held, zr.at[g, k - 1]))
 
     def ag_xy_send(g, k, which=None):
         own = ag_rows(g, x, zk[k], y, 3)
-        if which is not None:
-            send_if(which, ("ag", g), own, own, xs.at[g, k], xr.at[g, k], to_x)
-            send_if(which, ("ag", g), own, own, ys.at[g, k], yr.at[g, k], to_y)
-            return
-        if k > 0:
-            arrived = copy(own, own, zs.at[g, 0], zr.at[g, k - 1], to_zk[1]).wait_recv
-            if k > 1:
-                pl.when(outer == 1)(arrived)
-            else:
-                arrived()
+        if which is None:
+            ag_z_got(g, k)
         held = own if k else ag_own(g, 3)
-        send(("ag", g), held, own, xs.at[g, k], xr.at[g, k], to_x)
-        send(("ag", g), held, own, ys.at[g, k], yr.at[g, k], to_y)
+        send(link_s, g, 0, held, own, xr.at[g, k], to_x, which)
+        send(link_s, g, 1, held, own, yr.at[g, k], to_y, which)
 
     def ag_diag(g, k):
-        got = ag_rows(g, x, zk[k], ny, 3)
-        copy(got, got, ys.at[g, k], yr.at[g, k], to_y).wait_recv()
+        arrived(ag_rows(g, x, zk[k], ny, 3), yr.at[g, k])
         half = ag_rows(g, x, zk[k], ny, 1)
-        send(("ag", g), half, half, dxs.at[g, k], dxr.at[g, k], to_x)
-        got = ag_rows(g, nx, zk[k], y, 3)
-        copy(got, got, xs.at[g, k], xr.at[g, k], to_x).wait_recv()
+        send(link_s, g, 0, half, half, dr.at[g], to_x)
+        arrived(ag_rows(g, nx, zk[k], y, 3), xr.at[g, k])
         half = ag_rows(g, nx, zk[k], y, 2)
-        send(("ag", g), half, half, dys.at[g, k], dyr.at[g, k], to_y)
-
-    def ag_last(g, k):
-        half = ag_rows(g, nx, zk[k], ny, 1)
-        copy(half, half, dxs.at[g, k], dxr.at[g, k], to_x).wait_recv()
-        half = ag_rows(g, nx, zk[k], ny, 2)
-        copy(half, half, dys.at[g, k], dyr.at[g, k], to_y).wait_recv()
+        send(link_s, g, 1, half, half, dr.at[g], to_y)
+
+    def ag_last(g):
+        got_rows_of(4 * (PIECE - AG_CUTS[g][0]), dr.at[g])
 
     ag_strip_xy(1)
     ag_xy_send(1, 0)
@@ -656,11 +649,11 @@
     range_of = [ranges[i] for i in range(4)]
     inv_of = [1.0 / r for r in range_of]
 
-    sm[x, z, y] = jnp.zeros((16, 128), F32)
-    sm[x, z, y, 0:6, 0:96] = vectors[...].astype(F32)
-    sm[x, z, y, 6:9, 0:32] = b_up[...].astype(F32)
-    sm[x, z, y, 9:12, 0:8] = b_qv[:, 0, :].astype(F32)
-    sm[x, z, y, 12:15, 0:8] = b_qv[:, 1, :].astype(F32)
+    smf[...] = jnp.zeros((16, 128), F32)
+    smf[0:6, 0:96] = vectors[...].astype(F32)
+    smf[6:9, 0:32] = b_up[...].astype(F32)
+    smf[9:12, 0:8] = b_qv[:, 0, :].astype(F32)
+    smf[12:15, 0:8] = b_qv[:, 1, :].astype(F32)
     lane = lax.broadcasted_iota(jnp.int32, (1, 128), 1)
     peak_row = jnp.zeros((1, 128), F32)
     for g, ref in enumerate((w_qkv, w_out, w_up, w_down)):
@@ -669,16 +662,18 @@
             most = jnp.max(most, axis=0)
         most = jnp.max(jnp.max(most, axis=0, keepdims=True), axis=1, keepdims=True)
         peak_row = jnp.where(lane == g, most, peak_row)
-    sm[x, z, y, 15:16] = peak_row
+    smf[15:16] = peak_row
+    sm[x, z, y] = smf[...].astype(BF)
 
     small_c = copy(sm.at[x, z, y], smc, sm_s.at[0], sm_r.at[0], to_c)
     small_c.start()
     ag_z_send(1)
     small_c.wait()
-    sm[x, z, y, 15:16] = jnp.maximum(sm[x, z, y, 15:16], smc[15:16])
+    smf[15:16] = jnp.maximum(peak_row, smc[...].astype(F32)[15:16])
+    sm[x, z, y] = smf[...].astype(BF)
     small_xy = ((nx, y, to_x), (x, ny, to_y), (nx, ny, to_xy))
     for i, (_, _, device) in enumerate(small_xy):
-        send("sm", sm.at[x, z, y], sm.at[x, z, y], sm_s.at[1 + i], sm_r.at[1 + i], device)
+        copy(sm.at[x, z, y], sm.at[x, z, y], sm_s.at[1], sm_r.at[1], device).start()
     ag_strip_xy(2)
 
     for made in arriving[8:]:
@@ -707,15 +702,13 @@
             seen = column * (1.0 if r == s else long_flag)
             bias[r * 128 : r * 128 + 128, s * 128 : s * 128 + 128] = jnp.where(seen > 0.5, 0.0, -1e30)
 
-    for i, (xx, yy, device) in enumerate(small_xy):
-        copy(sm.at[xx, z, yy], sm.at[xx, z, yy], sm_s.at[1 + i], sm_r.at[1 + i], device).wait_recv()
+    arrived(sm.at[0, 0:3, 0], sm_r.at[1])
     for k in (1, 2, 3):
-        send("sm", sm.at[:, z], sm.at[:, z], sm_s.at[3 + k], sm_r.at[3 + k], to_z[k])
+        copy(sm.at[:, z], sm.at[:, z], sm_s.at[2], sm_r.at[2], to_z[k]).start()
     ag_strip_z(1)
     ag_z_send(2)
     ag_diag(0, 0)
-    got = ag_rows(1, x, zk[1], y, 3)
-    copy(got, got, zs.at[1, 0], zr.at[1, 0], to_zk[1]).wait_recv()
+    ag_z_got(1, 1)
     ag_xy_send(1, 1, 1)
     ag_xy_send(0, 2)
     ag_z_fwd(1, 2)
@@ -724,18 +717,18 @@
     ag_xy_send(1, 1, 0)
     ag_z_fwd(1, 3)
     ag_strip_z(2)
-    for k in (1, 2, 3):
-        copy(sm.at[:, from_z[k]], sm.at[:, from_z[k]], sm_s.at[3 + k], sm_r.at[3 + k], to_z[k]).wait_recv()
-    sent("sm")
-
-    peaks = jnp.max(jnp.max(jnp.max(sm[:, :, :, 15:16, :], axis=0), axis=0), axis=0)
+    arrived(sm.at[:, 0:3], sm_r.at[2])
+    arrived(sm.at[0, 0:3, 0], sm_s.at[1])
+    arrived(sm.at[:, 0:3], sm_s.at[2])
+
+    peaks = jnp.max(sm[...].astype(F32).reshape(16, 16, 128), axis=0)[15:16]
     w_peak = [jnp.max(jnp.where(lane == g, peaks, 0.0)) for g in range(4)]
     w_inv = [1.0 / r for r in w_peak]
 
     def spread(xx, width, step):
         total = None
         for place in range(8):
-            tile = sm[xx, place // 2, place % 2]
+            tile = sm[xx, place // 2, place % 2].astype(F32)
             if width > 128:
                 tile = jnp.concatenate([tile, jnp.zeros((16, width - 128), F32)], axis=1)
             if place:
@@ -766,6 +759,7 @@
     ag_xy_send(1, 3)
     ag_diag(1, 0)
     ag_diag(1, 1)
+    ag_xy_send(2, 1)
 
     left = lax.broadcasted_iota(jnp.int32, (PIECE, 128), 1) < 64
 
@@ -797,21 +791,19 @@
                 wo[rows, 256:384] = other
 
     loop(4, lambda zz: squash_heads(zz, y))
-    for k in range(4):
-        ag_last(0, k)
+    ag_last(0)
     loop(4, lambda zz: squash_heads(zz, ny))
     ag_z_fwd(2, 2)
     ag_z_fwd(2, 3)
-    ag_diag(1, 2)
+
+    def squash_piece(g, xx, zz, yy):
+        v = wts[g, xx, zz, yy].astype(F32)
+        wff[g - 1, xx, pl.ds(mul8((zz * 2 + yy) * PIECE, PIECE), PIECE), :] = (
+            w_peak[g + 1] * jnp.tanh(v * w_inv[g + 1])
+        ).astype(BF)
 
     def squash_ff(g, xx):
-        def body(place):
-            v = wts[g, xx, place // 2, place % 2].astype(F32)
-            wff[g - 1, xx, pl.ds(mul8(place * PIECE, PIECE), PIECE), :] = (
-                w_peak[g + 1] * jnp.tanh(v * w_inv[g + 1])
-            ).astype(BF)
-
-        loop(8, body)
+        loop(8, lambda place: squash_piece(g, xx, place // 2, place % 2))
 
     for j, held in enumerate((qs, ks, vs)):
 
@@ -821,12 +813,11 @@
         elif j == 2:
             got = got + bqv[1:2, :]
         held[...] = got.astype(BF)
-    ag_diag(1, 3)
+    ag_diag(1, 2)
     for p in range(3):
         cols = slice(p * 128, p * 128 + 128)
         kt[cols, :] = ks[:, cols].T
         vt[cols, :] = vs[:, cols].T
-    ag_xy_send(2, 1)
 
     half_of = lax.broadcasted_iota(jnp.int32, (1, 128), 1) // 64
 
@@ -845,10 +836,11 @@
 
     ag_strip_fwd(2)
     attend(0)
+    ag_diag(1, 3)
     ag_xy_send(2, 2)
-    ag_diag(2, 0)
     attend(1)
     ag_xy_send(2, 3)
+    ag_diag(2, 0)
     attend(2)
 
     for p in range(3):
@@ -863,22 +855,17 @@
     def out_part(start, held, cols=slice(0, WIDE)):
         held[:, cols] = nt(cq[pl.ds(start, OWN), :], wo[cols, :])
 
-    ex1 = []
     for i in range(2):
         cols = slice(i * HERE, i * HERE + HERE)
         out_part(theirs, exa_s, cols)
-        made = copy(exa_s.at[:, cols], exa_r.at[:, cols], ex_s.at[(0, 9)[i]], ex_r.at[(0, 9)[i]], to_c)
+        made = copy(exa_s.at[:, cols], exa_r.at[:, cols], ex_s.at[0], ex_r.at[0], to_c)
         made.start()
-        ex1.append(made)
     out_part(mine, r1)
+    ag_strip_got(1)
     ag_diag(2, 1)
-    ag_strip_got(1)
-    for k in range(4):
-        ag_last(1, k)
-    squash_ff(1, 0)
-    squash_ff(1, 1)
-    for made in ex1:
-        made.wait()
+    squash_ff(1, x)
+    arrived(exa_r, ex_r.at[0])
+    arrived(exa_s, ex_s.at[0])
 
     def sum_rows(v):
         return jnp.sum(v, axis=0, keepdims=True)
@@ -908,28 +895,23 @@
     for i in range(2):
         first_norm(i)
         own = hq.at[half_rows(mine, i)]
-        made = copy(own, own, ex_s.at[(1, 10)[i]], ex_r.at[(1, 10)[i]], to_c)
-        made.start()
-        started.setdefault("share", []).append((made, None))
+        copy(own, own, ex_s.at[1], ex_r.at[1], to_c).start()
 
     def share_rows(held, number):
         own = held.at[pl.ds(mine, OWN)]
-        made = copy(own, own, ex_s.at[number], ex_r.at[number], to_c)
-        made.start()
-        started.setdefault("share", []).append((made, None))
+        copy(own, own, ex_s.at[1], ex_r.at[number], to_c).start()
+
+    def shared(held):
+        arrived(held.at[pl.ds(mine, OWN)], ex_s.at[1])
 
     def got_rows(held, number):
-        other = held.at[pl.ds(theirs, OWN)]
-        copy(other, other, ex_s.at[number], ex_r.at[number], to_c).wait_recv()
+        arrived(held.at[pl.ds(theirs, OWN)], ex_r.at[number])
 
     def turn_rows(held, out, start):
         out[:, pl.ds(start, OWN)] = held[pl.ds(start, OWN), :].T
 
-    ag_diag(2, 2)
     turn_rows(hq, hqt, mine)
-    for i in range(2):
-        other = hq.at[half_rows(theirs, i)]
-        copy(other, other, ex_s.at[(1, 10)[i]], ex_r.at[(1, 10)[i]], to_c).wait_recv()
+    arrived(hq.at[pl.ds(theirs, OWN)], ex_r.at[1])
     turn_rows(hq, hqt, theirs)
 
     def expand(xx):
@@ -949,6 +931,9 @@
         loop(2, body)
 
     expand(x)
+    ag_diag(2, 2)
+    ag_last(1)
+    squash_ff(1, nx)
     ag_diag(2, 3)
     expand(nx)
     ag_strip_got(2)
@@ -960,19 +945,17 @@
     squash_ff(2, x)
     down_part(theirs, exb_s, x, True)
     down_part(mine, gr2, x, True)
-    for k in range(4):
-        ag_last(2, k)
-    squash_ff(2, nx)
-    ex2 = []
+    loop(4, lambda zz: squash_piece(2, nx, zz, y))
+    ag_last(2)
+    loop(4, lambda zz: squash_piece(2, nx, zz, ny))
     for i in range(2):
         cols = slice(i * HERE, i * HERE + HERE)
         down_part(theirs, exb_s, nx, False, cols)
-        made = copy(exb_s.at[:, cols], exb_r.at[:, cols], ex_s.at[(2, 7)[i]], ex_r.at[(2, 7)[i]], to_c)
+        made = copy(exb_s.at[:, cols], exb_r.at[:, cols], ex_s.at[0], ex_r.at[2], to_c)
         made.start()
-        ex2.append(made)
     down_part(mine, gr2, nx, False)
-    for made in ex2:
-        made.wait()
+    arrived(exb_r, ex_r.at[2])
+    arrived(exb_s, ex_s.at[0])
 
     def second_norm(i):
         rows = pl.ds(mul8(i * 128, 128), 128)
@@ -991,29 +974,16 @@
         tot[0, 1:2, :] += sum_rows(low.astype(F32))
         gf[pl.ds(mul8(mine + i * 128, 128), 128), :] = low
 
+    shared(hq)
     for i in range(2):
         second_norm(i)
         own = gf.at[half_rows(mine, i)]
-        made = copy(own, own, ex_s.at[(3, 8)[i]], ex_r.at[(3, 8)[i]], to_c)
-        made.start()
-        started.setdefault("share", []).append((made, None))
+        copy(own, own, ex_s.at[1], ex_r.at[3], to_c).start()
     leave(o_layer, r_layer)
     turn_rows(gf, rowt, mine)
-    for g in range(3):
-        sent(("ag", g))
-    for i in range(2):
-        other = gf.at[half_rows(theirs, i)]
-        copy(other, other, ex_s.at[(3, 8)[i]], ex_r.at[(3, 8)[i]], to_c).wait_recv()
+    sent(link_s)
+    arrived(gf.at[pl.ds(theirs, OWN)], ex_r.at[3])
     turn_rows(gf, rowt, theirs)
-
-    def rs_send(g, number, src, dst, device):
-        send("rs", src, dst, rs_s.at[g, number], rs_r.at[g, number], device)
-
-    def rs_send_if(which, g, number, src, dst, device, slot):
-        send_if(which, "rs", src, dst, rf_s.at[g, number], slot, device)
-
-    def rs_wait(g, number, dst, device):
-        copy(dst, dst, rs_s.at[g, number], rs_r.at[g, number], device).wait_recv()
 
     def rs_rows(g, part):
         strip, one, two = RS_CUTS[g]
@@ -1025,73 +995,70 @@
 
     far_z, near_z = pl.ds(2 - z // 2 * 2, 2), pl.ds(z // 2 * 2, 2)
 
-    def rs_first(g, near):
-        one, two = rs_part(g, 1), rs_part(g, 2)
-        rs_send(g, 0, wts.at[g, nx, :, ny, rs_rows(g, 1)], rdx.at[g, :, one], to_x)
-        rs_send(g, 1, wts.at[g, nx, :, ny, rs_rows(g, 2)], rdy.at[g, :, pl.ds(0, RS_CUTS[g][2])], to_y)
-        rs_send(g, 2, wts.at[g, nx, far_z, y, rs_rows(g, 1)], rxx.at[g, far_z, one], to_x)
+    def rs_first(g, planes):
+        one, far = rs_part(g, 1), pl.ds(0, RS_CUTS[g][2])
+        i = 0 if planes is far_z else 2
+        send(link_s, g, 0, wts.at[g, nx, planes, ny, rs_rows(g, 1)], rdx.at[g, planes, one], rs_r.at[g, i], to_x)
+        send(link_s, g, 1, wts.at[g, nx, planes, ny, rs_rows(g, 2)], rdy.at[g, planes, far], rs_r.at[g, i + 1], to_y)
+
+    def rs_direct_x(g, planes, part):
+        i = 4 if planes is far_z else 5
+        src = wts.at[g, nx, planes, y, rs_rows(g, part)]
+        send(link_s, g, 0, src, rxx.at[g, planes, rs_part(g, part)], rs_r.at[g, i], to_x)
+
+    def rs_direct_y(g, planes, part):
+        i = 4 if planes is far_z else 5
+        src = wts.at[g, x, planes, ny, rs_rows(g, part)]
+        send(link_s, g, 1, src, ryy.at[g, planes, rs_part(g, part)], rs_r.at[g, i], to_y)
+
+    def rs_direct(g, near):
+        rs_direct_x(g, far_z, 1)
         if near:
-            rs_send(g, 15, wts.at[g, nx, near_z, y, rs_rows(g, 1)], rxx.at[g, near_z, one], to_x)
+            rs_direct_x(g, near_z, 1)
 
     def rs_second(g, near):
-        two = rs_part(g, 2)
-        rs_send(g, 3, wts.at[g, x, far_z, ny, rs_rows(g, 2)], ryy.at[g, far_z, two], to_y)
+        rs_direct_y(g, far_z, 2)
         if near:
-            rs_send(g, 16, wts.at[g, x, near_z, ny, rs_rows(g, 2)], ryy.at[g, near_z, two], to_y)
+            rs_direct_y(g, near_z, 2)
 
     def rs_third_x(g, near):
-        one, two = rs_part(g, 1), rs_part(g, 2)
-        rs_wait(g, 0, rdx.at[g, :, one], to_x)
-
-        def add_x(i):
-            here = rs_rows(g, 1)
-            wts[g, x, i, ny, here] = (wts[g, x, i, ny, here].astype(F32) + rdx[g, i, one].astype(F32)).astype(BF)
-
-        loop(4, add_x)
-        rs_send(g, 4, wts.at[g, x, far_z, ny, rs_rows(g, 1)], ryy.at[g, far_z, one], to_y)
-        rs_send(g, 13, wts.at[g, x, near_z, ny, rs_rows(g, 1)], ryy.at[g, near_z, one], to_y)
+        one, here = rs_part(g, 1), rs_rows(g, 1)
+        for planes, i in ((far_z, 0), (near_z, 2)):
+            arrived(rdx.at[g, planes, one], rs_r.at[g, i])
+            wts[g, x, planes, ny, here] = (
+                wts[g, x, planes, ny, here].astype(F32) + rdx[g, planes, one].astype(F32)
+            ).astype(BF)
+            rs_direct_y(g, planes, 1)
         if not near:
-            rs_send(g, 16, wts.at[g, x, near_z, ny, rs_rows(g, 2)], ryy.at[g, near_z, two], to_y)
+            rs_direct_y(g, near_z, 2)
 
     def rs_third_y(g, near):
-        one, two = rs_part(g, 1), rs_part(g, 2)
-        far = pl.ds(0, RS_CUTS[g][2])
-        rs_wait(g, 1, rdy.at[g, :, far], to_y)
-
-        def add_y(i):
-            here = rs_rows(g, 2)
-            wts[g, nx, i, y, here] = (wts[g, nx, i, y, here].astype(F32) + rdy[g, i, far].astype(F32)).astype(BF)
-
-        loop(4, add_y)
-        rs_send(g, 5, wts.at[g, nx, far_z, y, rs_rows(g, 2)], rxx.at[g, far_z, two], to_x)
-        rs_send(g, 14, wts.at[g, nx, near_z, y, rs_rows(g, 2)], rxx.at[g, near_z, two], to_x)
+        here, far = rs_rows(g, 2), pl.ds(0, RS_CUTS[g][2])
+        for planes, i in ((far_z, 1), (near_z, 3)):
+            arrived(rdy.at[g, planes, far], rs_r.at[g, i])
+            wts[g, nx, planes, y, here] = (
+                wts[g, nx, planes, y, here].astype(F32) + rdy[g, planes, far].astype(F32)
+            ).astype(BF)
+            rs_direct_x(g, planes, 2)
         if not near:
-            rs_send(g, 15, wts.at[g, nx, near_z, y, rs_rows(g, 1)], rxx.at[g, near_z, one], to_x)
+            rs_direct_x(g, near_z, 1)
 
     def plane(g, zz):
         rest, here = rs_rows(g, 3), rs_part(g, 3)
         return wts[g, x, zz, y, rest].astype(F32) + rxx[g, zz, here].astype(F32) + ryy[g, zz, here].astype(F32)
 
     def rs_fourth(g):
-        one, two, both, rest = rs_part(g, 1), rs_part(g, 2), rs_part(g, 3), rs_rows(g, 3)
-        rs_wait(g, 2, rxx.at[g, far_z, one], to_x)
-        rs_wait(g, 3, ryy.at[g, far_z, two], to_y)
-        rs_wait(g, 4, ryy.at[g, far_z, one], to_y)
-        rs_wait(g, 5, rxx.at[g, far_z, two], to_x)
+        both, rest = rs_part(g, 3), rs_rows(g, 3)
+        got_rows_of(4 * (PIECE - RS_CUTS[g][0]), rs_r.at[g, 4])
         for k in (3, 2):
             wts[g, x, zk[k], y, rest] = plane(g, zk[k]).astype(BF)
-            rs_send_if(
-                1, g, k - 2, wts.at[g, x, zk[k], y, rest], rzf.at[g, k - 2, both], to_zk[1], rf_r.at[g, k - 2]
-            )
+            send(link_s, g, 2, wts.at[g, x, zk[k], y, rest], rzf.at[g, k - 2, both], rf_r.at[g, k - 2], to_zk[1], 1)
 
     def rs_near(g):
-        one, two, both, rest = rs_part(g, 1), rs_part(g, 2), rs_part(g, 3), rs_rows(g, 3)
-        rs_wait(g, 13, ryy.at[g, near_z, one], to_y)
-        rs_wait(g, 14, rxx.at[g, near_z, two], to_x)
-        rs_wait(g, 15, rxx.at[g, near_z, one], to_x)
-        rs_wait(g, 16, ryy.at[g, near_z, two], to_y)
+        both, rest = rs_part(g, 3), rs_rows(g, 3)
+        got_rows_of(4 * (PIECE - RS_CUTS[g][0]), rs_r.at[g, 5])
         wts[g, x, zk[1], y, rest] = plane(g, zk[1]).astype(BF)
-        rs_send(g, 6, wts.at[g, x, zk[1], y, rest], rz.at[g, 0, both], to_zk[1])
+        send(link_s, g, 2, wts.at[g, x, zk[1], y, rest], rz.at[g, 0, both], rs_r.at[g, 7], to_zk[1])
 
     def rs_fifth(g):
         both, rest = rs_part(g, 3), rs_rows(g, 3)
@@ -1099,22 +1066,25 @@
 
             @pl.when(outer == 0)
             def _(k=k):
-                held = rzf.at[g, k - 2, both]
-                copy(held, held, rf_s.at[g, 0], rf_r.at[g, k - 2], to_zk[1]).wait_recv()
+                arrived(rzf.at[g, k - 2, both], rf_r.at[g, k - 2])
                 wts[g, x, zk[k], y, rest] = (
                     wts[g, x, zk[k], y, rest].astype(F32) + rzf[g, k - 2, both].astype(F32)
                 ).astype(BF)
 
-            rs_send_if(0, g, k, wts.at[g, x, zk[k], y, rest], rz.at[g, 1, both], to_zk[k], rs_r.at[g, 7])
-
-    def strips(g, zz):
-        return wts.at[g, :, zz, :, pl.ds(0, RS_CUTS[g][0])]
-
-    def rs_strip_z(g):
+            send(link_s, g, 2, wts.at[g, x, zk[k], y, rest], rz.at[g, 1, both], rs_r.at[g, 7], to_zk[k], 0)
+
+    def strips(held, g, place, i):
         here = pl.ds(0, RS_CUTS[g][0])
+        return held.at[g, *place, (nx, x)[i] if g == 2 else slice(None), :, here]
+
+    def strips_of(g, zz, i):
+        here = pl.ds(0, RS_CUTS[g][0])
+        return wts.at[g, (nx, x)[i] if g == 2 else slice(None), zz, :, here]
+
+    def rs_strip_z(g, i):
         for k in (3, 2):
-            rs_send_if(1, g, 2 + k, strips(g, zk[k]), rzf2.at[g, k - 2, :, :, here], to_zk[1], rf_r.at[g, k])
-        rs_send(g, 8, strips(g, zk[1]), rz2.at[g, 0, :, :, here], to_zk[1])
+            send(link_s, g, 2, strips_of(g, zk[k], i), strips(rzf2, g, (k - 2,), i), rf_r.at[g, k], to_zk[1], 1)
+        send(link_s, g, 2, strips_of(g, zk[1], i), strips(rz2, g, (0,), i), rs_r.at[g, 6], to_zk[1])
 
     def rs_strip_fwd(g):
         here = pl.ds(0, RS_CUTS[g][0])
@@ -1122,18 +1092,17 @@
 
             @pl.when(outer == 0)
             def _(k=k):
-                held = rzf2.at[g, k - 2, :, :, here]
-                copy(held, held, rf_s.at[g, 0], rf_r.at[g, k], to_zk[1]).wait_recv()
+                got_rows_of(4 * RS_CUTS[g][0], rf_r.at[g, k])
                 wts[g, :, zk[k], :, here] = (
                     wts[g, :, zk[k], :, here].astype(F32) + rzf2[g, k - 2, :, :, here].astype(F32)
                 ).astype(BF)
 
-            rs_send_if(0, g, 4 + k, strips(g, zk[k]), rz2.at[g, 1, :, :, here], to_zk[k], rs_r.at[g, 9])
+            whole = wts.at[g, :, zk[k], :, here]
+            send(link_s, g, 2, whole, rz2.at[g, 1, :, :, here], rs_r.at[g, 6], to_zk[k], 0)
 
     def rs_strip_sum(g):
         here = pl.ds(0, RS_CUTS[g][0])
-        for k in (0, 1):
-            rs_wait(g, 8 + k, rz2.at[g, k, :, :, here], to_zk[1 + k])
+        got_rows_of(8 * RS_CUTS[g][0], rs_r.at[g, 6])
         wts[g, :, z, :, here] = (
             wts[g, :, z, :, here].astype(F32)
             + rz2[g, 0, :, :, here].astype(F32)
@@ -1142,16 +1111,12 @@
 
     def rs_strip_send(g):
         here = pl.ds(0, RS_CUTS[g][0])
-        rs_send(g, 12, wts.at[g, nx, z, ny, here], rst.at[g, 2, here], to_xy)
-        rs_send(g, 10, wts.at[g, nx, z, y, here], rst.at[g, 0, here], to_x)
-        rs_send(g, 11, wts.at[g, x, z, ny, here], rst.at[g, 1, here], to_y)
+        for i, (xx, yy, axis, device) in enumerate(((nx, ny, 0, to_xy), (nx, y, 0, to_x), (x, ny, 1, to_y))):
+            send(link_s, g, axis, wts.at[g, xx, z, yy, here], rst.at[g, i, here], rs_r.at[g, 7], device)
 
     def rs_total(g):
         here, both = pl.ds(0, RS_CUTS[g][0]), rs_part(g, 3)
-        for k in (0, 1):
-            rs_wait(g, 6 + k, rz.at[g, k, both], to_zk[1 + k])
-        for i, device in enumerate((to_x, to_y, to_xy)):
-            rs_wait(g, 10 + i, rst.at[g, i, here], device)
+        got_rows_of(2 * PIECE + RS_CUTS[g][0], rs_r.at[g, 7])
         strip = wts[g, x, z, y, here].astype(F32)
         for i in range(3):
             strip = strip + rst[g, i, here].astype(F32)
@@ -1160,15 +1125,24 @@
             total = total + rz[g, k, both].astype(F32)
         return jnp.concatenate([strip, total], axis=0)
 
+    def ff_grad_planes(g, turned, held, xx, planes, first):
+        rows = pl.ds(mul8(first * 2 * PIECE, 4 * PIECE), 4 * PIECE)
+        got = nn(turned[rows, :], held[:, pl.ds(mul8(xx * WIDE, WIDE), WIDE)])
+        wts[g, xx, planes] = got.reshape(2, 2, PIECE, WIDE).astype(BF)
+
     def ff_grad(g, turned, held, xx):
         got = nn(turned[...], held[:, pl.ds(mul8(xx * WIDE, WIDE), WIDE)])
         wts[g, xx] = got.reshape(4, 2, PIECE, WIDE).astype(BF)
 
-    ff_grad(2, rowt, aq, nx)
-    rs_first(2, True)
+    ff_grad_planes(2, rowt, aq, nx, far_z, 2 - z // 2 * 2)
+    rs_first(2, far_z)
+    ff_grad_planes(2, rowt, aq, nx, near_z, z // 2 * 2)
+    rs_first(2, near_z)
+    rs_direct(2, True)
+    rs_strip_z(2, 0)
     ff_grad(2, rowt, aq, x)
     rs_second(2, True)
-    rs_strip_z(2)
+    rs_strip_z(2, 1)
 
     for xx in range(2):
 
@@ -1186,16 +1160,18 @@
         )
 
     up_part(theirs, exa_s)
-    ex3 = copy(exa_s, exa_r, ex_s.at[4], ex_r.at[4], to_c)
+    ex3 = copy(exa_s, exa_r, ex_s.at[0], ex_r.at[4], to_c)
     ex3.start()
     up_part(mine, r1)
     ff_grad(1, hqt, gu, nx)
     rs_third_x(2, True)
     rs_third_y(2, True)
-    rs_first(1, True)
+    rs_first(1, far_z)
+    rs_first(1, near_z)
+    rs_direct(1, True)
     ff_grad(1, hqt, gu, x)
     rs_second(1, True)
-    rs_strip_z(1)
+    rs_strip_z(1, 0)
     ex3.wait()
 
     def first_back(i):
@@ -1211,7 +1187,7 @@
         tot[0, 0:1, :] += sum_rows(low.astype(F32))
         gf[pl.ds(mul8(mine + i * 64, 64), 64), :] = low
 
-    sent("share")
+    shared(gf)
     loop(4, first_back)
     share_rows(gf, 5)
     turn_rows(gf, rowt, mine)
@@ -1292,17 +1268,19 @@
     small.wait()
     mixed = jnp.where(row_of < 6, tot[0] + tot_c[...], jnp.maximum(tot[0], tot_c[...]))
     tot[1] = jnp.where((row_of >= 6) & (row_of < 9), tot[0], mixed)
-    small = copy(tot.at[1], tot_x, tt_s.at[1], tt_r.at[1], to_x)
+    small = copy(tot.at[1], tot_x, tt_s.at[0], tt_r.at[1], to_x)
     small.start()
-    rs_first(0, False)
+    rs_first(0, far_z)
+    rs_first(0, near_z)
+    rs_direct(0, False)
     rs_second(0, False)
-    rs_strip_z(0)
+    rs_strip_z(0, 0)
 
     def token_part(start, held):
         held[...] = nt(grads[pl.ds(start, OWN), :], wc[...])
 
     token_part(theirs, exb_s)
-    ex4 = copy(exb_s, exb_r, ex_s.at[6], ex_r.at[6], to_c)
+    ex4 = copy(exb_s, exb_r, ex_s.at[0], ex_r.at[6], to_c)
     ex4.start()
     rs_third_x(1, True)
     rs_third_y(1, True)
@@ -1318,17 +1296,17 @@
 
     loop(4, token_grad)
     own = o_tok.at[pl.ds(mul8(mp * OWN, OWN), OWN)]
-    send("tok", own, own, gx_s.at[1], gx_r.at[1], to_c)
+    keep("tok", copy(own, own, gx_s.at[1], gx_r.at[1], to_c))
     leave_rows(mp)
     rs_strip_fwd(1)
     small.wait()
     tot[2] = jnp.where(row_of < 9, tot[1] + tot_x[...], jnp.maximum(tot[1], tot_x[...]))
-    small = copy(tot.at[2], tot_y, tt_s.at[2], tt_r.at[2], to_y)
+    small = copy(tot.at[2], tot_y, tt_s.at[0], tt_r.at[2], to_y)
     small.start()
     rs_third_x(0, False)
     rs_fifth(2)
     rs_third_y(0, False)
-    send("tok", own, own, gx_s.at[0], gx_r.at[0], to_x)
+    keep("tok", copy(own, own, gx_s.at[0], gx_r.at[0], to_x))
     for g in (2, 1):
         rs_strip_sum(g)
         rs_strip_send(g)
@@ -1337,16 +1315,33 @@
     rs_near(1)
     small.wait()
     tot[3] = jnp.where(row_of < 9, tot[2] + tot_y[...], jnp.maximum(tot[2], tot_y[...]))
-    smalls = []
-    for k in (1, 2, 3):
-        made = copy(tot.at[3], tot_z.at[k - 1], tt_s.at[2 + k], tt_r.at[2 + k], to_z[k])
-        made.start()
-        smalls.append(made)
+
+    def both(one, two):
+        return jnp.where(row_of < 9, one + two, jnp.maximum(one, two))
+
+    inward = copy(tot.at[3], tot_z.at[0], tt_s.at[0], tt_r.at[3], to_zk[1])
+    across = copy(tot.at[4], tot_z.at[1], tt_s.at[0], tt_r.at[4], to_zk[2])
+    outward = copy(tot.at[5], tot_z.at[2], tt_s.at[0], tt_r.at[5], to_zk[1])
+    pl.when(outer == 1)(inward.start)
     rs_fourth(0)
     rs_strip_sum(0)
     rs_strip_send(0)
     rs_fifth(1)
+
+    @pl.when(outer == 0)
+    def _():
+        inward.wait_recv()
+        tot[4] = both(tot[3], tot_z[0])
+        across.start()
+
     rs_near(0)
+
+    @pl.when(outer == 0)
+    def _():
+        across.wait()
+        tot[5] = both(tot[4], tot_z[1])
+        outward.start()
+
     rs_fifth(0)
     o_down[...] = rs_total(2) * _slope(w_down[...], w_inv[3])
     leave(o_down, r_down)
@@ -1355,14 +1350,20 @@
 
     far = o_tok.at[pl.ds(mul8((nx * 2 + c) * OWN, OWN), OWN)]
     copy(far, far, gx_s.at[0], gx_r.at[0], to_x).wait_recv()
-    send("tok", far, far, gx_s.at[2], gx_r.at[2], to_c)
+    keep("tok", copy(far, far, gx_s.at[2], gx_r.at[2], to_c))
     leave_rows(nx * 2 + c)
 
-    for made in smalls:
-        made.wait()
-    done = tot[3]
-    for k in range(3):
-        done = jnp.where(row_of < 9, done + tot_z[k], jnp.maximum(done, tot_z[k]))
+    @pl.when(outer == 0)
+    def _():
+        outward.wait_send()
+
+    @pl.when(outer == 1)
+    def _():
+        inward.wait_send()
+        outward.wait_recv()
+        tot[5] = tot_z[2]
+
+    done = tot[5]
     back = pltpu.roll(done, (8 - dp) * 96, 1)
     o_vec[...] = back[0:6, 0:96]
     ups = jnp.where(x == 0, done[6:7, :], done[7:8, :])
@@ -1399,8 +1400,9 @@
     far = pl.ds(mul8((nx * 2 + nc) * OWN, OWN), OWN)
     copy(o_tok.at[far], o_tok.at[far], gx_s.at[2], gx_r.at[2], to_c).wait_recv()
     leave_rows(nx * 2 + nc)
-    for group in list(started):
-        sent(group)
+    sent(link_s)
+    kept("tok")
+    shared(gf)
     for made in leaving:
         made.wait()
 
@@ -1451,7 +1453,8 @@
         buffer(3, 2, 2, 2, 32, WIDE),
         buffer(3, 2, 2, 2, 32, WIDE),
         buffer(3, 3, 32, WIDE),
-        f32(2, 4, 2, 16, 128),
+        buffer(2, 4, 2, 16, 128),
+        buffer(16, 128),
         f32(16, 128),
         f32(16, WIDE),
         f32(8, WIDE),
@@ -1491,41 +1494,29 @@
         buffer(half, 3 * HERE),
         f32(HERE, half),
         f32(WIDE, HERE),
-        f32(4, 16, WIDE),
+        f32(6, 16, WIDE),
         f32(16, WIDE),
         f32(16, WIDE),
         f32(16, WIDE),
         f32(3, 16, WIDE),
-        sems((3, 2)),
-        sems((3, 2)),
-        sems((3, 3)),
-        sems((3, 2)),
-        sems((3, 2)),
         sems((3, 3)),
         sems((3, 3)),
-        sems((3, 3)),
+        sems((2, 3)),
+        sems((2,)),
         sems((3, 4)),
         sems((3, 4)),
-        sems((3, 4)),
-        sems((3, 4)),
-        sems((3, 4)),
-        sems((3, 4)),
-        sems((3, 4)),
-        sems((3, 4)),
-        sems((3, 17)),
-        sems((3, 17)),
+        sems((3,)),
         sems((3, 8)),
         sems((3, 4)),
+        sems((3,)),
+        sems((3,)),
+        sems((2,)),
         sems((7,)),
-        sems((7,)),
-        sems((11,)),
-        sems((11,)),
-        sems((6,)),
+        sems((1,)),
         sems((6,)),
         sems((3,)),
         sems((3,)),
         sems((14,)),
-        sems((13,)),
     ]
     far = pl.BlockSpec(memory_space=pltpu.HBM)
     outs = pl.pallas_call(

time: 134 us -> 129 us (0.963)
  Pallas kernels: 133 us -> 128 us
    pallas_call x1, Pallas kernels: 129 us -> 124 us  [layer_on_chips(): pl.pallas_call(layer_kernel, out_shape=[*kinds, jax.ShapeDtypeStruct((8,...]
where the time goes in v5:
time: 129 us
  Pallas kernels  128 us (99%)
    pallas_call x1, Pallas kernels, layer_on_chips(): pl.pallas_call(layer_kernel, out_shape=[*kinds, jax.ShapeDtypeStruct((8,...  124 us
    pallas_call x1, Pallas kernels, finish(): pl.pallas_call(finish_kernel, out_shape=[shape(v.shape, F32 if i == 1 els...  3.74 us

profile of v5, /device:TPU:0, one launch (start us, length us, event | category | flops | bytes accessed | tf_op | source)
XLA Modules:
  0.0 128.8 jit_solution(6596379442485503979)
XLA Ops:
  0.6 124.2 %encoder_layer.1 = (bf16[256,768]{1,0:T(8,128)(2,1)}, bf16[1024,768]{1,0:T(8,128)(2,1)}, f32[3,96,192]{2,1,0:T(8,128)}, f32[192,96]{1,0:T(8,128)}, f32[96,768]{1...) custom-call(bf16[1024,768]{1,0:T(8,128)(2,1)} %h_tok.1, ...), custom_call_target="tpu_custom_call" | custom-call | tf_op jit(solution)/shard_map/encoder_layer/pallas_call | solution.py:1522
  124.9 3.7 %write_results.1 = (bf16[256,768]{1,0:T(8,128)(2,1)}, f32[1024,768]{1,0:T(8,128)}, f32[3,96,192]{2,1,0:T(8,128)}, f32[192,96]{1,0:T(8,128)}, f32[96,768]{1,0:T(8...) custom-call(bf16[256,768]{1,0:T(8,128)(2,1)} %get-tuple-element.30.refs_0_,, ...), custom_call_target="tpu_custom_call" | custom-call | tf_op jit(solution)/shard_map/write_results/pallas_call | solution.py:1563

commit v6 on v5

--- a/solution.py
+++ b/solution.py
@@ -418,6 +418,8 @@
     exa_r,
     exb_s,
     exb_r,
+    low_s,
+    low_r,
     hq,
     hqt,
     r1,
@@ -575,11 +577,16 @@
 
     def ag_strip_xy(g):
         own = ag_rows(g, x, z, y, 0)
-        for axis, device in ((0, to_x), (1, to_y), (0, to_xy)):
-            send(link_s, g, axis, ag_own(g, 0), own, str_.at[g - 1], device)
+        for axis, device in ((0, to_x), (1, to_y)):
+            send(link_s, g, axis, ag_own(g, 0), own, str_.at[g - 1, int(axis != g - 1)], device)
+
+    def ag_strip_relay(g):
+        held = ag_rows(g, nx, z, y, 0) if g == 1 else ag_rows(g, x, z, ny, 0)
+        arrived(held, str_.at[g - 1, 0])
+        send(link_s, g, 2 - g, held, held, str_.at[g - 1, 1], (to_y, to_x)[g - 1])
 
     def ag_strip_z(g):
-        got_rows_of(3 * AG_CUTS[g][0], str_.at[g - 1])
+        got_rows_of(2 * AG_CUTS[g][0], str_.at[g - 1, 1])
         own = ag_strips(g, z)
         send(link_s, g, 2, own, own, z2r.at[g - 1, 0], to_zk[1])
         send(link_s, g, 2, own, own, z2r.at[g - 1, 1 + outer], to_zk[2])
@@ -624,13 +631,13 @@
     def ag_diag(g, k):
         arrived(ag_rows(g, x, zk[k], ny, 3), yr.at[g, k])
         half = ag_rows(g, x, zk[k], ny, 1)
-        send(link_s, g, 0, half, half, dr.at[g], to_x)
+        send(link_s, g, 0, half, half, dr.at[g + k if g == 2 else g], to_x)
         arrived(ag_rows(g, nx, zk[k], y, 3), xr.at[g, k])
         half = ag_rows(g, nx, zk[k], y, 2)
-        send(link_s, g, 1, half, half, dr.at[g], to_y)
-
-    def ag_last(g):
-        got_rows_of(4 * (PIECE - AG_CUTS[g][0]), dr.at[g])
+        send(link_s, g, 1, half, half, dr.at[g + k if g == 2 else g], to_y)
+
+    def ag_last(g, k=0, pieces=4):
+        got_rows_of(pieces * (PIECE - AG_CUTS[g][0]), dr.at[g + k])
 
     ag_strip_xy(1)
     ag_xy_send(1, 0)
@@ -690,6 +697,7 @@
         xqt[cols, :] = xq[:, cols].T
 
     loop(6, do_turn)
+    ag_strip_relay(1)
     ag_xy_send(0, 1)
     ag_z_fwd(0, 2)
     ag_z_fwd(0, 3)
@@ -705,6 +713,7 @@
     arrived(sm.at[0, 0:3, 0], sm_r.at[1])
     for k in (1, 2, 3):
         copy(sm.at[:, z], sm.at[:, z], sm_s.at[2], sm_r.at[2], to_z[k]).start()
+    ag_strip_relay(2)
     ag_strip_z(1)
     ag_z_send(2)
     ag_diag(0, 0)
@@ -716,7 +725,6 @@
     ag_xy_send(0, 3)
     ag_xy_send(1, 1, 0)
     ag_z_fwd(1, 3)
-    ag_strip_z(2)
     arrived(sm.at[:, 0:3], sm_r.at[2])
     arrived(sm.at[0, 0:3, 0], sm_s.at[1])
     arrived(sm.at[:, 0:3], sm_s.at[2])
@@ -752,6 +760,7 @@
         bqv[j : j + 1, 256:384] = heads[0][0][first + 2 : first + 3] + heads[1][1][first + 2 : first + 3]
 
     ag_diag(0, 2)
+    ag_strip_z(2)
     ag_xy_send(2, 0)
     ag_strip_fwd(1)
     ag_diag(0, 3)
@@ -825,14 +834,13 @@
         cols = pl.ds(mul8(p * 128, 128), 128)
         for e in range(2):
             feats = pl.ds(mul8(p * 128 + e * 64, 64), 64)
-            for n in range(2):
-                q = qs[n * 256 : n * 256 + 256, cols]
-                q = jnp.where(half_of == e, q, jnp.zeros_like(q))
-                s = nt(ks[:, cols], q) + bias[:, n * 256 : n * 256 + 256]
-                s = jnp.exp(s - jnp.max(s, axis=0, keepdims=True))
-                s = (s * (1.0 / jnp.sum(s, axis=0, keepdims=True))).astype(BF)
-                probs[p * 2 + e, :, n * 256 : n * 256 + 256] = s
-                ctxt[feats, n * 256 : n * 256 + 256] = nn(vt[feats, :], s)
+            q = qs[:, cols]
+            q = jnp.where(half_of == e, q, jnp.zeros_like(q))
+            s = nt(ks[:, cols], q) + bias[...]
+            s = jnp.exp(s - jnp.max(s, axis=0, keepdims=True))
+            s = (s * (1.0 / jnp.sum(s, axis=0, keepdims=True))).astype(BF)
+            probs[p * 2 + e] = s
+            ctxt[feats, :] = nn(vt[feats, :], s)
 
     ag_strip_fwd(2)
     attend(0)
@@ -914,7 +922,7 @@
     arrived(hq.at[pl.ds(theirs, OWN)], ex_r.at[1])
     turn_rows(hq, hqt, theirs)
 
-    def expand(xx):
+    def expand(xx, between=None):
         wide = pl.ds(mul8(xx * WIDE, WIDE), WIDE)
 
         def body(i):
@@ -928,14 +936,16 @@
             pdf = 0.3989422804014327 * jnp.exp(-0.5 * u * u)
             fac[rows, wide] = ((1.0 - bent * bent) * (cdf + u * pdf)).astype(fac.dtype)
 
-        loop(2, body)
+        body(0)
+        if between is not None:
+            between()
+        body(1)
 
     expand(x)
     ag_diag(2, 2)
     ag_last(1)
     squash_ff(1, nx)
-    ag_diag(2, 3)
-    expand(nx)
+    expand(nx, functools.partial(ag_diag, 2, 3))
     ag_strip_got(2)
 
     def down_part(start, held, xx, first, cols=slice(0, WIDE)):
@@ -946,20 +956,21 @@
     down_part(theirs, exb_s, x, True)
     down_part(mine, gr2, x, True)
     loop(4, lambda zz: squash_piece(2, nx, zz, y))
-    ag_last(2)
-    loop(4, lambda zz: squash_piece(2, nx, zz, ny))
+    for k in range(4):
+        ag_last(2, k, 1)
+        squash_piece(2, nx, zk[k], ny)
     for i in range(2):
         cols = slice(i * HERE, i * HERE + HERE)
         down_part(theirs, exb_s, nx, False, cols)
-        made = copy(exb_s.at[:, cols], exb_r.at[:, cols], ex_s.at[0], ex_r.at[2], to_c)
-        made.start()
+        low_s[:, cols] = exb_s[:, cols].astype(BF)
+        copy(low_s.at[:, cols], low_r.at[:, cols], ex_s.at[0], ex_r.at[2], to_c).start()
     down_part(mine, gr2, nx, False)
-    arrived(exb_r, ex_r.at[2])
-    arrived(exb_s, ex_s.at[0])
+    arrived(low_r, ex_r.at[2])
+    arrived(low_s, ex_s.at[0])
 
     def second_norm(i):
         rows = pl.ds(mul8(i * 128, 128), 128)
-        v = r1[rows, :] + (gr2[rows, :] + exb_r[rows, :] + vec[1:2, :])
+        v = r1[rows, :] + (gr2[rows, :] + low_r[rows, :].astype(F32) + vec[1:2, :])
         center = v - mean_of(v)
         factor = lax.rsqrt(mean_of(center * center) + 1e-12)
         normed = center * factor
@@ -1210,12 +1221,10 @@
         grad_k = grad_v = None
         for e in range(2):
             feats = pl.ds(mul8(p * 128 + e * 64, 64), 64)
-            for n in range(2):
-                part = slice(n * 256, n * 256 + 256)
-                g = gct[cols, part]
-                g = jnp.where(row_half == e, g, jnp.zeros_like(g))
-                dpr = nn(vs[:, cols], g)
-                ds[:, part] = (probs[p * 2 + e, :, part].astype(F32) * (dpr - dsum[pl.ds(p * 2 + e, 1), part])).astype(BF)
+            g = gct[cols, :]
+            g = jnp.where(row_half == e, g, jnp.zeros_like(g))
+            dpr = nn(vs[:, cols], g)
+            ds[...] = (probs[p * 2 + e].astype(F32) * (dpr - dsum[pl.ds(p * 2 + e, 1), :])).astype(BF)
             g = gc[:, cols]
             g = jnp.where(half_of == e, g, jnp.zeros_like(g))
             more_v = nn(probs[p * 2 + e], g)
@@ -1312,7 +1321,6 @@
         rs_strip_send(g)
     rs_strip_fwd(0)
     rs_fourth(1)
-    rs_near(1)
     small.wait()
     tot[3] = jnp.where(row_of < 9, tot[2] + tot_y[...], jnp.maximum(tot[2], tot_y[...]))
 
@@ -1324,6 +1332,7 @@
     outward = copy(tot.at[5], tot_z.at[2], tt_s.at[0], tt_r.at[5], to_zk[1])
     pl.when(outer == 1)(inward.start)
     rs_fourth(0)
+    rs_near(1)
     rs_strip_sum(0)
     rs_strip_send(0)
     rs_fifth(1)
@@ -1343,15 +1352,15 @@
         outward.start()
 
     rs_fifth(0)
+    far = o_tok.at[pl.ds(mul8((nx * 2 + c) * OWN, OWN), OWN)]
+    copy(far, far, gx_s.at[0], gx_r.at[0], to_x).wait_recv()
+    keep("tok", copy(far, far, gx_s.at[2], gx_r.at[2], to_c))
+    leave_rows(nx * 2 + c)
+
     o_down[...] = rs_total(2) * _slope(w_down[...], w_inv[3])
     leave(o_down, r_down)
     o_up[...] = rs_total(1) * _slope(w_up[...], w_inv[2])
     leave(o_up, r_up)
-
-    far = o_tok.at[pl.ds(mul8((nx * 2 + c) * OWN, OWN), OWN)]
-    copy(far, far, gx_s.at[0], gx_r.at[0], to_x).wait_recv()
-    keep("tok", copy(far, far, gx_s.at[2], gx_r.at[2], to_c))
-    leave_rows(nx * 2 + c)
 
     @pl.when(outer == 0)
     def _():
@@ -1476,6 +1485,8 @@
         f32(OWN, WIDE),
         f32(OWN, WIDE),
         f32(OWN, WIDE),
+        buffer(OWN, WIDE),
+        buffer(OWN, WIDE),
         buffer(half, WIDE),
         buffer(WIDE, half),
         f32(OWN, WIDE),
@@ -1502,10 +1513,10 @@
         sems((3, 3)),
         sems((3, 3)),
         sems((2, 3)),
-        sems((2,)),
+        sems((2, 2)),
         sems((3, 4)),
         sems((3, 4)),
-        sems((3,)),
+        sems((6,)),
         sems((3, 8)),
         sems((3, 4)),
         sems((3,)),

time: 129 us -> 125 us (0.969)
  Pallas kernels: 128 us -> 124 us
    pallas_call x1, Pallas kernels: 124 us -> 121 us  [layer_on_chips(): pl.pallas_call(layer_kernel, out_shape=[*kinds, jax.ShapeDtypeStruct((8,...]
where the time goes in v6:
time: 125 us
  Pallas kernels  124 us (99%)
    pallas_call x1, Pallas kernels, layer_on_chips(): pl.pallas_call(layer_kernel, out_shape=[*kinds, jax.ShapeDtypeStruct((8,...  121 us
    pallas_call x1, Pallas kernels, finish(): pl.pallas_call(finish_kernel, out_shape=[shape(v.shape, F32 if i == 1 els...  3.74 us

profile of v6, /device:TPU:0, one launch (start us, length us, event | category | flops | bytes accessed | tf_op | source)
XLA Modules:
  0.0 125.3 jit_solution(11997378165458340063)
XLA Ops:
  0.6 120.7 %encoder_layer.1 = (bf16[256,768]{1,0:T(8,128)(2,1)}, bf16[1024,768]{1,0:T(8,128)(2,1)}, f32[3,96,192]{2,1,0:T(8,128)}, f32[192,96]{1,0:T(8,128)}, f32[96,768]{1...) custom-call(bf16[1024,768]{1,0:T(8,128)(2,1)} %h_tok.1, ...), custom_call_target="tpu_custom_call" | custom-call | tf_op jit(solution)/shard_map/encoder_layer/pallas_call | solution.py:1533
  121.4 3.7 %write_results.1 = (bf16[256,768]{1,0:T(8,128)(2,1)}, f32[1024,768]{1,0:T(8,128)}, f32[3,96,192]{2,1,0:T(8,128)}, f32[192,96]{1,0:T(8,128)}, f32[96,768]{1,0:T(8...) custom-call(bf16[256,768]{1,0:T(8,128)(2,1)} %get-tuple-element.30.refs_0_,, ...), custom_call_target="tpu_custom_call" | custom-call | tf_op jit(solution)/shard_map/write_results/pallas_call | solution.py:1574

commit v7 on v6

--- a/solution.py
+++ b/solution.py
@@ -993,6 +993,16 @@
     leave(o_layer, r_layer)
     turn_rows(gf, rowt, mine)
     sent(link_s)
+
+    far_rows = pl.ds(mul8((2 - z // 2 * 2) * 2 * PIECE, 4 * PIECE), 4 * PIECE)
+    far_hidden = pl.ds(mul8(nx * WIDE, WIDE), WIDE)
+
+    def far_part(start):
+        return nn(rowt[far_rows, pl.ds(start, OWN)], aq[pl.ds(start, OWN), far_hidden])
+
+    own_part = far_part(mine)
+    exb_s[...] = own_part[0:OWN, :]
+    exb_r[0 : HERE - OWN, :] = own_part[OWN:HERE, :]
     arrived(gf.at[pl.ds(theirs, OWN)], ex_r.at[3])
     turn_rows(gf, rowt, theirs)
 
@@ -1145,7 +1155,9 @@
         got = nn(turned[...], held[:, pl.ds(mul8(xx * WIDE, WIDE), WIDE)])
         wts[g, xx] = got.reshape(4, 2, PIECE, WIDE).astype(BF)
 
-    ff_grad_planes(2, rowt, aq, nx, far_z, 2 - z // 2 * 2)
+    other_part = far_part(theirs)
+    own_part = jnp.concatenate([exb_s[...], exb_r[0 : HERE - OWN, :]], axis=0)
+    wts[2, nx, far_z] = (own_part + other_part).reshape(2, 2, PIECE, WIDE).astype(BF)
     rs_first(2, far_z)
     ff_grad_planes(2, rowt, aq, nx, near_z, z // 2 * 2)
     rs_first(2, near_z)

time: 125 us -> 125 us (level)
  no operation moved by 1% of the time
where the time goes in v7:
time: 125 us
  Pallas kernels  124 us (99%)
    pallas_call x1, Pallas kernels, layer_on_chips(): pl.pallas_call(layer_kernel, out_shape=[*kinds, jax.ShapeDtypeStruct((8,...  121 us
    pallas_call x1, Pallas kernels, finish(): pl.pallas_call(finish_kernel, out_shape=[shape(v.shape, F32 if i == 1 els...  3.74 us

profile of v7, /device:TPU:0, one launch (start us, length us, event | category | flops | bytes accessed | tf_op | source)
XLA Modules:
  0.0 125.1 jit_solution(6842842443769633604)
XLA Ops:
  0.6 120.5 %encoder_layer.1 = (bf16[256,768]{1,0:T(8,128)(2,1)}, bf16[1024,768]{1,0:T(8,128)(2,1)}, f32[3,96,192]{2,1,0:T(8,128)}, f32[192,96]{1,0:T(8,128)}, f32[96,768]{1...) custom-call(bf16[1024,768]{1,0:T(8,128)(2,1)} %h_tok.1, ...), custom_call_target="tpu_custom_call" | custom-call | tf_op jit(solution)/shard_map/encoder_layer/pallas_call | solution.py:1545
  121.2 3.7 %write_results.1 = (bf16[256,768]{1,0:T(8,128)(2,1)}, f32[1024,768]{1,0:T(8,128)}, f32[3,96,192]{2,1,0:T(8,128)}, f32[192,96]{1,0:T(8,128)}, f32[96,768]{1,0:T(8...) custom-call(bf16[256,768]{1,0:T(8,128)(2,1)} %get-tuple-element.30.refs_0_,, ...), custom_call_target="tpu_custom_call" | custom-call | tf_op jit(solution)/shard_map/write_results/pallas_call | solution.py:1586
